TPU v7x, 32 devices: a whole 2x2x4 slice. The times are simulated.
32 devices in a mesh: img: 8 (over z, x), blk: 4 (over y, core).
Axes of the slice: x: 2, y: 2, z: 4, core: 2. Of those that a mesh axis runs over, the one named last changes fastest.
Arguments:
- x_large: bfloat16 [128, 14, 14, 1024], P(('img', 'blk')), may hold values from -18 to 18
- x_small: bfloat16 [256, 6, 6, 1024], P(('img', 'blk')), may hold values from -18 to 18
- large_image: int32 [128], P(('img', 'blk')), may hold values from 0 to 63, as said below
- small_image: int32 [256], P(('img', 'blk')), may hold values from 0 to 63, as said below
- first_reduce: bfloat16 [1024, 512], P('img'), may hold values from -0.1875 to 0.1875
- first_spatial: bfloat16 [3, 3, 512, 512], P(None, None, 'img'), may hold values from -0.09375 to 0.09375
- first_expand: bfloat16 [512, 2048], P('img'), may hold values from -0.25 to 0.25
- first_short: bfloat16 [1024, 2048], P('img'), may hold values from -0.1875 to 0.1875
- second_reduce: bfloat16 [2048, 512], P('img'), may hold values from -0.125 to 0.125
- second_spatial: bfloat16 [3, 3, 512, 512], P(None, None, 'img'), may hold values from -0.09375 to 0.09375
- second_expand: bfloat16 [512, 2048], P('img'), may hold values from -0.25 to 0.25
- head_hidden: bfloat16 [2048, 2048], P('img'), may hold values from -0.125 to 0.125
- head_embed: bfloat16 [2048, 128], P('img'), may hold values from -0.125 to 0.125
- norm_gain: float32 [10240], replicated, may hold values from 0.5 to 1.5
- norm_shift: float32 [10240], replicated, may hold values from -0.5 to 0.5
Outputs:
- loss: float32 [], replicated
- grad_large: bfloat16 [128, 14, 14, 1024], P(('img', 'blk'))
- grad_small: bfloat16 [256, 6, 6, 1024], P(('img', 'blk'))
- first_reduce_grad: float32 [1024, 512], P('img')
- first_spatial_grad: float32 [3, 3, 512, 512], P(None, None, 'img')
- first_expand_grad: float32 [512, 2048], P('img')
- first_short_grad: float32 [1024, 2048], P('img')
- second_reduce_grad: float32 [2048, 512], P('img')
- second_spatial_grad: float32 [3, 3, 512, 512], P(None, None, 'img')
- second_expand_grad: float32 [512, 2048], P('img')
- head_hidden_grad: float32 [2048, 2048], P('img')
- head_embed_grad: float32 [2048, 128], P('img')
- norm_gain_grad: float32 [10240], replicated
- norm_shift_grad: float32 [10240], replicated
Inputs may be any that keep to these rules, and one draw needn't show every extreme that they name: `large_image`: the images fall into groups of 2 in a row; the d-th aligned block of 4 entries holds each image of one group exactly 2 times, in an order drawn from the seed, and which group each block holds is a permutation of the groups drawn from the seed. `small_image`: the d-th aligned block of 8 entries holds each image of the group of the large views' block (d + 16) modulo 64 / 2 exactly 4 times, in an order drawn from the seed.
All inputs are finite; a program needn't handle non-finite values.
Results may differ from a plain program's by a relative error of at most 0.024.
Values may be sent and summed in bfloat16 or wider, within the bound.
No kernel may reach another device: no remote copies, remote signals or barrier semaphores. Data moves between devices by JAX's collectives and lax.ppermute only.
A program may use at most 192 MiB of HBM per device.

v0:
```python
import jax
import jax.numpy as jnp
from jax import lax
from jax.sharding import PartitionSpec as P

POSITIVES = 5


EPSILON = 1e-05
NORM_EPSILON = 1e-06
SOFTMAX_TEMP = 0.1
MASKED = -1e30


def to_frames(matrix, shapes):
    frames = []
    offset = 0
    for number, breadth in shapes:
        length = number * breadth * breadth
        frames.append(
            matrix[offset : offset + length].reshape(number, breadth, breadth, matrix.shape[1])
        )
        offset += length
    return frames


def to_rows(frames):
    return jnp.concatenate([picture.reshape(-1, picture.shape[3]) for picture in frames], 0)


def patch_rows(frames, stride):
    blocks = []
    for picture in frames:
        breadth = picture.shape[1]
        extent = stride * ((breadth - 1) // stride) + 1
        padded = jnp.pad(picture, ((0, 0), (1, 1), (1, 1), (0, 0)))
        shifted = [
            lax.slice(
                padded,
                (0, row_tap, col_tap, 0),
                (picture.shape[0], row_tap + extent, col_tap + extent, picture.shape[3]),
                (1, stride, stride, 1),
            )
            for row_tap in range(3)
            for col_tap in range(3)
        ]
        blocks.append(jnp.concatenate(shifted, 3).reshape(-1, 9 * picture.shape[3]))
    return jnp.concatenate(blocks, 0)


def fold_patches(matrix, shapes, stride, channels):
    frames = []
    offset = 0
    for number, breadth in shapes:
        out_side = (breadth - 1) // stride + 1
        extent = stride * (out_side - 1) + 1
        length = number * out_side * out_side
        patches = matrix[offset : offset + length].reshape(number, out_side, out_side, 9, channels)
        offset += length
        summed = jnp.zeros((number, breadth + 2, breadth + 2, channels), jnp.float32)
        for kernel_tap in range(9):
            row_tap = kernel_tap // 3
            col_tap = kernel_tap % 3
            summed = summed + lax.pad(
                patches[:, :, :, kernel_tap],
                jnp.float32(0.0),
                (
                    (0, 0, 0),
                    (row_tap, breadth + 2 - row_tap - extent, stride - 1),
                    (col_tap, breadth + 2 - col_tap - extent, stride - 1),
                    (0, 0, 0),
                ),
            )
        frames.append(summed[:, 1:-1, 1:-1])
    return to_rows(frames)


def product(left_side, right_side):
    return jnp.dot(left_side, right_side, preferred_element_type=jnp.float32)


def weight_product(left_side, right_side):
    return lax.dot_general(
        left_side, right_side, (((0,), (0,)), ((), ())), preferred_element_type=jnp.float32
    )


def backward_product(left_side, right_side):
    return lax.dot_general(
        left_side, right_side, (((1,), (1,)), ((), ())), preferred_element_type=jnp.float32
    )


def smooth(values):
    return jax.nn.silu(values)


def smooth_slope(values):
    sigmoid_value = jax.nn.sigmoid(values)
    return sigmoid_value * (1.0 + values * (1.0 - sigmoid_value))


def norm_forward(values, gain_vector, shift_vector):
    number = values.shape[0] * lax.axis_size(("img", "blk"))
    center = lax.psum(jnp.sum(values, 0), ("img", "blk")) / number
    centered = values - center
    spread = lax.psum(jnp.sum(centered * centered, 0), ("img", "blk")) / number
    factor = lax.rsqrt(spread + EPSILON)
    normed = centered * factor
    return (normed * gain_vector + shift_vector, (normed, factor * gain_vector))


def norm_backward(upstream, stored):
    normed, factor = stored
    number = upstream.shape[0] * lax.axis_size(("img", "blk"))
    shift_grad, gain_grad = lax.psum(
        (jnp.sum(upstream, 0), jnp.sum(upstream * normed, 0)), ("img", "blk")
    )
    return (
        factor * (upstream - shift_grad / number - normed * (gain_grad / number)),
        gain_grad,
        shift_grad,
    )


def per_device(
    x_large,
    x_small,
    large_image,
    small_image,
    first_reduce,
    first_spatial,
    first_expand,
    first_short,
    second_reduce,
    second_spatial,
    second_expand,
    head_hidden,
    head_embed,
    norm_gain,
    norm_shift,
):
    mid_width = first_reduce.shape[1]
    out_width = first_short.shape[1]
    head_width = head_hidden.shape[1]
    widths = [
        mid_width,
        mid_width,
        out_width,
        out_width,
        mid_width,
        mid_width,
        out_width,
        head_width,
    ]
    starts = [sum(widths[:layer_index]) for layer_index in range(8)]
    gain_parts = [
        norm_gain[starts[layer_index] : starts[layer_index] + widths[layer_index]]
        for layer_index in range(8)
    ]
    shift_parts = [
        norm_shift[starts[layer_index] : starts[layer_index] + widths[layer_index]]
        for layer_index in range(8)
    ]
    gain_grads = [None] * 8
    shift_grads = [None] * 8
    (
        reduce_full,
        spatial_full,
        expand_full,
        short_full,
        reduce2_full,
        spatial2_full,
        expand2_full,
        hidden_full,
        embed_full,
    ) = (
        lax.all_gather(first_reduce, "img", axis=0, tiled=True),
        lax.all_gather(first_spatial, "img", axis=2, tiled=True),
        lax.all_gather(first_expand, "img", axis=0, tiled=True),
        lax.all_gather(first_short, "img", axis=0, tiled=True),
        lax.all_gather(second_reduce, "img", axis=0, tiled=True),
        lax.all_gather(second_spatial, "img", axis=2, tiled=True),
        lax.all_gather(second_expand, "img", axis=0, tiled=True),
        lax.all_gather(head_hidden, "img", axis=0, tiled=True),
        lax.all_gather(head_embed, "img", axis=0, tiled=True),
    )
    large_count = x_large.shape[0]
    small_count = x_small.shape[0]
    input_shapes = [(large_count, x_large.shape[1]), (small_count, x_small.shape[1])]
    output_shapes = [
        (large_count, (x_large.shape[1] - 1) // 2 + 1),
        (small_count, (x_small.shape[1] - 1) // 2 + 1),
    ]
    pixel_rows = to_rows([x_large, x_small])
    reduced = product(pixel_rows, reduce_full)
    reduced_normed, reduced_kept = norm_forward(reduced, gain_parts[0], shift_parts[0])
    reduced_low = smooth(reduced_normed).astype(jnp.bfloat16)
    reduced_patch = patch_rows(to_frames(reduced_low, input_shapes), 2)
    spatial_matrix = spatial_full.reshape(9 * mid_width, mid_width)
    turned = product(reduced_patch, spatial_matrix)
    turned_normed, turned_kept = norm_forward(turned, gain_parts[1], shift_parts[1])
    turned_low = smooth(turned_normed).astype(jnp.bfloat16)
    expanded = product(turned_low, expand_full)
    branch, expanded_kept = norm_forward(expanded, gain_parts[2], shift_parts[2])
    sub_rows = to_rows([x_large[:, ::2, ::2], x_small[:, ::2, ::2]])
    skipped = product(sub_rows, short_full)
    shortcut, skipped_kept = norm_forward(skipped, gain_parts[3], shift_parts[3])
    block_pre = branch + shortcut
    block_out = smooth(block_pre)
    block_low = block_out.astype(jnp.bfloat16)
    mixing = product(block_low, reduce2_full)
    mixing_normed, mixing_kept = norm_forward(mixing, gain_parts[4], shift_parts[4])
    mixing_low = smooth(mixing_normed).astype(jnp.bfloat16)
    mixing_patch = patch_rows(to_frames(mixing_low, output_shapes), 1)
    spatial2_matrix = spatial2_full.reshape(9 * mid_width, mid_width)
    rotated = product(mixing_patch, spatial2_matrix)
    rotated_normed, rotated_kept = norm_forward(rotated, gain_parts[5], shift_parts[5])
    rotated_low = smooth(rotated_normed).astype(jnp.bfloat16)
    widened = product(rotated_low, expand2_full)
    grown_out, widened_kept = norm_forward(widened, gain_parts[6], shift_parts[6])
    final_pre = grown_out + block_out
    final_out = smooth(final_pre)
    pooled = jnp.concatenate(
        [jnp.mean(picture, (1, 2)) for picture in to_frames(final_out, output_shapes)], 0
    )
    pooled_low = pooled.astype(jnp.bfloat16)
    head_linear = product(pooled_low, hidden_full)
    head_normed, head_kept = norm_forward(head_linear, gain_parts[7], shift_parts[7])
    head_low = smooth(head_normed).astype(jnp.bfloat16)
    embedding = product(head_low, embed_full)
    inverse = lax.rsqrt(jnp.sum(embedding * embedding, 1, keepdims=True) + NORM_EPSILON)
    unit_rows = embedding * inverse
    unit_lowered = unit_rows.astype(jnp.bfloat16)
    labels = jnp.concatenate([large_image, small_image], 0)
    view_count = unit_lowered.shape[0]
    total_views = view_count * lax.axis_size(("img", "blk"))
    anchor_index = lax.axis_index(("img", "blk")) * view_count + jnp.arange(
        view_count, dtype=jnp.int32
    )

    def compare(portion_normalized, portion_label):
        similarity_scores = backward_product(unit_lowered, portion_normalized) / SOFTMAX_TEMP
        itself = (
            anchor_index[:, None]
            == jnp.arange(portion_normalized.shape[0], dtype=jnp.int32)[None, :]
        )
        paired = (labels[:, None] == portion_label[None, :]) & jnp.logical_not(itself)
        return (similarity_scores, itself, paired)

    highest = jnp.full((view_count,), MASKED, jnp.float32)
    similarity_scores, itself, paired = compare(
        lax.all_gather(unit_lowered, ("img", "blk"), axis=0, tiled=True),
        lax.all_gather(labels, ("img", "blk"), axis=0, tiled=True),
    )
    masked = jnp.where(itself, MASKED, similarity_scores)
    new_high = jnp.maximum(highest, jnp.max(masked, 1))
    terms = jnp.where(itself, 0.0, jnp.exp(masked - new_high[:, None]))
    summed = jnp.sum(terms, 1)
    positive = jnp.sum(jnp.where(paired, similarity_scores, 0.0), 1)
    highest, summed, positive = (new_high, summed, positive)
    log_total = highest + jnp.log(summed)
    loss_value = lax.psum(jnp.sum(log_total - positive / POSITIVES), ("img", "blk")) / total_views

    def pair_weights(similarity_scores, itself, paired, log_rows):
        chance = jnp.where(itself, 0.0, jnp.exp(similarity_scores - log_rows))
        return ((chance - paired.astype(jnp.float32) / POSITIVES) / total_views).astype(
            jnp.bfloat16
        )

    portion_normalized = lax.all_gather(unit_lowered, ("img", "blk"), axis=0, tiled=True)
    portion_label = lax.all_gather(labels, ("img", "blk"), axis=0, tiled=True)
    portion_log = lax.all_gather(
        log_total.astype(jnp.bfloat16), ("img", "blk"), axis=0, tiled=True
    ).astype(jnp.float32)
    similarity_scores, itself, paired = compare(portion_normalized, portion_label)
    row_weights = pair_weights(similarity_scores, itself, paired, log_total[:, None])
    column_weights = pair_weights(similarity_scores, itself, paired, portion_log[None, :])
    unit_grad = (
        product(row_weights, portion_normalized) + product(column_weights, portion_normalized)
    ) / SOFTMAX_TEMP
    along = jnp.sum(unit_rows * unit_grad, 1, keepdims=True)
    embedding_grad = (inverse * (unit_grad - unit_rows * along)).astype(jnp.bfloat16)
    embed_weight_grad = weight_product(head_low, embedding_grad)
    head_grad = backward_product(embedding_grad, embed_full) * smooth_slope(head_normed)
    head_grad, gain_grads[7], shift_grads[7] = norm_backward(head_grad, head_kept)
    head_back = head_grad.astype(jnp.bfloat16)
    hidden_weight_grad = weight_product(pooled_low, head_back)
    pooled_grad = backward_product(head_back, hidden_full)
    spread_back = []
    first_row = 0
    for number, breadth in output_shapes:
        portion_grad = pooled_grad[first_row : first_row + number] / (breadth * breadth)
        spread_back.append(
            jnp.broadcast_to(portion_grad[:, None, None, :], (number, breadth, breadth, out_width))
        )
        first_row += number
    final_grad = to_rows(spread_back) * smooth_slope(final_pre)
    widened_grad, gain_grads[6], shift_grads[6] = norm_backward(final_grad, widened_kept)
    widened_back = widened_grad.astype(jnp.bfloat16)
    expand2_grad = weight_product(rotated_low, widened_back)
    rotated_grad = backward_product(widened_back, expand2_full) * smooth_slope(rotated_normed)
    rotated_grad, gain_grads[5], shift_grads[5] = norm_backward(rotated_grad, rotated_kept)
    rotated_back = rotated_grad.astype(jnp.bfloat16)
    spatial2_grad = weight_product(mixing_patch, rotated_back).reshape(3, 3, mid_width, mid_width)
    mixing_grad = fold_patches(
        backward_product(rotated_back, spatial2_matrix), output_shapes, 1, mid_width
    ) * smooth_slope(mixing_normed)
    mixing_grad, gain_grads[4], shift_grads[4] = norm_backward(mixing_grad, mixing_kept)
    mixing_back = mixing_grad.astype(jnp.bfloat16)
    reduce2_grad = weight_product(block_low, mixing_back)
    block_grad = (final_grad + backward_product(mixing_back, reduce2_full)) * smooth_slope(
        block_pre
    )
    expanded_grad, gain_grads[2], shift_grads[2] = norm_backward(block_grad, expanded_kept)
    skipped_grad, gain_grads[3], shift_grads[3] = norm_backward(block_grad, skipped_kept)
    expanded_back = expanded_grad.astype(jnp.bfloat16)
    skipped_back = skipped_grad.astype(jnp.bfloat16)
    expand_grad = weight_product(turned_low, expanded_back)
    short_grad = weight_product(sub_rows, skipped_back)
    sub_grad = backward_product(skipped_back, short_full)
    turned_grad = backward_product(expanded_back, expand_full) * smooth_slope(turned_normed)
    turned_grad, gain_grads[1], shift_grads[1] = norm_backward(turned_grad, turned_kept)
    turned_back = turned_grad.astype(jnp.bfloat16)
    spatial_grad = weight_product(reduced_patch, turned_back).reshape(3, 3, mid_width, mid_width)
    reduced_grad = fold_patches(
        backward_product(turned_back, spatial_matrix), input_shapes, 2, mid_width
    ) * smooth_slope(reduced_normed)
    reduced_grad, gain_grads[0], shift_grads[0] = norm_backward(reduced_grad, reduced_kept)
    reduced_back = reduced_grad.astype(jnp.bfloat16)
    reduce_grad = weight_product(pixel_rows, reduced_back)
    input_frames = to_frames(backward_product(reduced_back, reduce_full), input_shapes)
    sub_frames = to_frames(sub_grad, output_shapes)
    input_grads = []
    for whole_frame, sub_frame in zip(input_frames, sub_frames):
        breadth = whole_frame.shape[1]
        out_side = sub_frame.shape[1]
        placed = lax.pad(
            sub_frame,
            jnp.float32(0.0),
            (
                (0, 0, 0),
                (0, breadth - 2 * out_side + 1, 1),
                (0, breadth - 2 * out_side + 1, 1),
                (0, 0, 0),
            ),
        )
        input_grads.append((whole_frame + placed).astype(jnp.bfloat16))
    (
        reduce_grad,
        spatial_grad,
        expand_grad,
        short_grad,
        reduce2_grad,
        spatial2_grad,
        expand2_grad,
        hidden_weight_grad,
        embed_weight_grad,
    ) = (
        lax.psum_scatter(reduce_grad, "img", scatter_dimension=0, tiled=True),
        lax.psum_scatter(spatial_grad, "img", scatter_dimension=2, tiled=True),
        lax.psum_scatter(expand_grad, "img", scatter_dimension=0, tiled=True),
        lax.psum_scatter(short_grad, "img", scatter_dimension=0, tiled=True),
        lax.psum_scatter(reduce2_grad, "img", scatter_dimension=0, tiled=True),
        lax.psum_scatter(spatial2_grad, "img", scatter_dimension=2, tiled=True),
        lax.psum_scatter(expand2_grad, "img", scatter_dimension=0, tiled=True),
        lax.psum_scatter(hidden_weight_grad, "img", scatter_dimension=0, tiled=True),
        lax.psum_scatter(embed_weight_grad, "img", scatter_dimension=0, tiled=True),
    )
    (
        reduce_grad,
        spatial_grad,
        expand_grad,
        short_grad,
        reduce2_grad,
        spatial2_grad,
        expand2_grad,
        hidden_weight_grad,
        embed_weight_grad,
    ) = (
        lax.psum(reduce_grad.astype(jnp.bfloat16), "blk").astype(jnp.float32),
        lax.psum(spatial_grad.astype(jnp.bfloat16), "blk").astype(jnp.float32),
        lax.psum(expand_grad.astype(jnp.bfloat16), "blk").astype(jnp.float32),
        lax.psum(short_grad.astype(jnp.bfloat16), "blk").astype(jnp.float32),
        lax.psum(reduce2_grad.astype(jnp.bfloat16), "blk").astype(jnp.float32),
        lax.psum(spatial2_grad.astype(jnp.bfloat16), "blk").astype(jnp.float32),
        lax.psum(expand2_grad.astype(jnp.bfloat16), "blk").astype(jnp.float32),
        lax.psum(hidden_weight_grad.astype(jnp.bfloat16), "blk").astype(jnp.float32),
        lax.psum(embed_weight_grad.astype(jnp.bfloat16), "blk").astype(jnp.float32),
    )
    return (
        loss_value,
        input_grads[0],
        input_grads[1],
        reduce_grad,
        spatial_grad,
        expand_grad,
        short_grad,
        reduce2_grad,
        spatial2_grad,
        expand2_grad,
        hidden_weight_grad,
        embed_weight_grad,
        jnp.concatenate(gain_grads, 0),
        jnp.concatenate(shift_grads, 0),
    )


def solution(mesh):
    placed = (
        P(("img", "blk"), None, None, None),
        P(("img", "blk"), None, None, None),
        P(("img", "blk")),
        P(("img", "blk")),
        P("img", None),
        P(None, None, "img", None),
        P("img", None),
        P("img", None),
        P("img", None),
        P(None, None, "img", None),
        P("img", None),
        P("img", None),
        P("img", None),
        P(),
        P(),
    )
    return jax.shard_map(
        per_device,
        mesh=mesh,
        in_specs=placed,
        out_specs=(
            P(),
            P(("img", "blk"), None, None, None),
            P(("img", "blk"), None, None, None),
            P("img", None),
            P(None, None, "img", None),
            P("img", None),
            P("img", None),
            P("img", None),
            P(None, None, "img", None),
            P("img", None),
            P("img", None),
            P("img", None),
            P(),
            P(),
        ),
        check_vma=False,
    )
```

profile of v0, /device:TPU:0, one launch (start us, length us, event | category | flops | bytes accessed | tf_op | source)
XLA Modules:
  0.0 2971.8 jit_solution(14791485867016098323)
XLA Ops:
  22.7 35.8 %all_gather.46 = bf16[2048,128]{1,0:T(8,128)(2,1)} all-gather(bf16[256,128]{1,0:T(8,128)(2,1)S(1)} %copy-done.102), channel_id=1, replica_groups=mesh['img'=8,'blk'=4] {'img'}, dimensions={0}, use_global_device_ids=true | all-gather | bytes 589824 | tf_op jit(solution)/shard_map/all_gather | solution.py:186
  59.6 40.8 %all-reduce.42 = s32[384]{0:T(512)} all-reduce(s32[384]{0:T(512)S(1)} %get-tuple-element.219), channel_id=1, replica_groups=mesh['img'=8,'blk'=4] {'img','blk'}, use_global_device_ids=true, to_apply=%add.42 | all-reduce | flops 384 | bytes 3072
  104.5 41.4 %psum.290 = f32[512]{0:T(512)S(1)} all-reduce(f32[512]{0:T(512)S(1)} %get-tuple-element.307), channel_id=1, replica_groups=mesh['img'=8,'blk'=4] {'img','blk'}, use_global_device_ids=true, to_apply=%region_1.0 | all-reduce | flops 512 | bytes 4096 | tf_op jit(solution)/shard_map/psum | solution.py:105
  146.2 41.8 %psum.291 = f32[512]{0:T(512)S(1)} all-reduce(f32[512]{0:T(512)S(1)} %multiply_reduce_fusion.7), channel_id=1, replica_groups=mesh['img'=8,'blk'=4] {'img','blk'}, use_global_device_ids=true, to_apply=%region_3.0 | all-reduce | flops 512 | bytes 4096 | tf_op jit(solution)/shard_map/psum | solution.py:107
  191.3 8.7 slice.329
  208.7 8.7 slice.331
  344.4 43.7 %psum.292 = f32[512]{0:T(512)S(1)} all-reduce(f32[512]{0:T(512)S(1)} %get-tuple-element.309), channel_id=1, replica_groups=mesh['img'=8,'blk'=4] {'img','blk'}, use_global_device_ids=true, to_apply=%region_5.6 | all-reduce | flops 512 | bytes 4096 | tf_op jit(solution)/shard_map/psum | solution.py:105
  388.2 39.3 %psum.293 = f32[512]{0:T(512)S(1)} all-reduce(f32[512]{0:T(512)S(1)} %multiply_reduce_fusion.13), channel_id=1, replica_groups=mesh['img'=8,'blk'=4] {'img','blk'}, use_global_device_ids=true, to_apply=%region_7.8 | all-reduce | flops 512 | bytes 4096 | tf_op jit(solution)/shard_map/psum | solution.py:107
  431.4 41.8 %all-reduce.52 = (f32[2048]{0:T(1024)S(1)}, f32[2048]{0:T(1024)S(1)}) all-reduce(f32[2048]{0:T(1024)S(1)} %get-tuple-element.305, f32[2048]{0:T(1024)S(1)} %get-tuple-element.311), channel_id=1, replica_groups=mesh['img'=8,'blk'=4] {'img','blk'}, use_global_device_ids=true, to_apply=%region_13.14 | all-reduce | flops 4096 | bytes 32768 | tf_op jit(solution)/shard_map/psum | solution.py:105
  475.4 42.8 %all-reduce.51 = (f32[2048]{0:T(1024)S(1)}, f32[2048]{0:T(1024)S(1)}) all-reduce(f32[2048]{0:T(1024)S(1)} %multiply_reduce_fusion.4, f32[2048]{0:T(1024)S(1)} %multiply_reduce_fusion.5), channel_id=1, replica_groups=mesh['img'=8,'blk'=4] {'img','blk'}, use_global_device_ids=true, to_apply=%region_15.16 | all-reduce | flops 4096 | bytes 32768 | tf_op jit(solution)/shard_map/psum | solution.py:107
  524.0 43.1 %psum.298 = f32[512]{0:T(512)S(1)} all-reduce(f32[512]{0:T(512)S(1)} %get-tuple-element.313), channel_id=1, replica_groups=mesh['img'=8,'blk'=4] {'img','blk'}, use_global_device_ids=true, to_apply=%region_17.18 | all-reduce | flops 512 | bytes 4096 | tf_op jit(solution)/shard_map/psum | solution.py:105
  567.2 40.0 %psum.299 = f32[512]{0:T(512)S(1)} all-reduce(f32[512]{0:T(512)S(1)} %multiply_reduce_fusion.12), channel_id=1, replica_groups=mesh['img'=8,'blk'=4] {'img','blk'}, use_global_device_ids=true, to_apply=%region_19.20 | all-reduce | flops 512 | bytes 4096 | tf_op jit(solution)/shard_map/psum | solution.py:107
  664.9 40.0 %psum.300 = f32[512]{0:T(512)S(1)} all-reduce(f32[512]{0:T(512)S(1)} %get-tuple-element.315), channel_id=1, replica_groups=mesh['img'=8,'blk'=4] {'img','blk'}, use_global_device_ids=true, to_apply=%region_21.22 | all-reduce | flops 512 | bytes 4096 | tf_op jit(solution)/shard_map/psum | solution.py:105
  706.0 40.0 %psum.301 = f32[512]{0:T(512)S(1)} all-reduce(f32[512]{0:T(512)S(1)} %multiply_reduce_fusion.11), channel_id=1, replica_groups=mesh['img'=8,'blk'=4] {'img','blk'}, use_global_device_ids=true, to_apply=%region_23.24 | all-reduce | flops 512 | bytes 4096 | tf_op jit(solution)/shard_map/psum | solution.py:107
  752.0 40.1 %psum.302 = f32[2048]{0:T(1024)S(1)} all-reduce(f32[2048]{0:T(1024)S(1)} %get-tuple-element.317), channel_id=1, replica_groups=mesh['img'=8,'blk'=4] {'img','blk'}, use_global_device_ids=true, to_apply=%region_25.26 | all-reduce | flops 2048 | bytes 16384 | tf_op jit(solution)/shard_map/psum | solution.py:105
  794.0 40.2 %psum.303 = f32[2048]{0:T(1024)S(1)} all-reduce(f32[2048]{0:T(1024)S(1)} %multiply_reduce_fusion.3), channel_id=1, replica_groups=mesh['img'=8,'blk'=4] {'img','blk'}, use_global_device_ids=true, to_apply=%region_27.28 | all-reduce | flops 2048 | bytes 16384 | tf_op jit(solution)/shard_map/psum | solution.py:107
  851.5 40.2 %psum.304 = f32[2048]{0:T(1024)S(1)} all-reduce(f32[2048]{0:T(1024)S(1)} %get-tuple-element.319), channel_id=1, replica_groups=mesh['img'=8,'blk'=4] {'img','blk'}, use_global_device_ids=true, to_apply=%region_31.32 | all-reduce | flops 2048 | bytes 16384 | tf_op jit(solution)/shard_map/psum | solution.py:105
  891.7 40.1 %psum.305 = f32[2048]{0:T(1024)S(1)} all-reduce(f32[2048]{0:T(1024)S(1)} %multiply_reduce_fusion.15), channel_id=1, replica_groups=mesh['img'=8,'blk'=4] {'img','blk'}, use_global_device_ids=true, to_apply=%region_33.34 | all-reduce | flops 2048 | bytes 16384 | tf_op jit(solution)/shard_map/psum | solution.py:107
  934.7 42.3 %all-gather = bf16[32,12,128]{2,1,0:T(8,128)(2,1)} all-gather(bf16[1,12,128]{2,1,0:T(8,128)(2,1)S(1)} %fusion.61), channel_id=1, replica_groups=mesh['img'=8,'blk'=4] {'img','blk'}, dimensions={0}, use_global_device_ids=true | all-gather | bytes 101376 | tf_op jit(solution)/shard_map/all_gather | solution.py:253
  985.8 37.1 %all-reduce.43 = bf16[384]{0:T(512)(128)(2,1)} all-reduce(bf16[384]{0:T(512)(128)(2,1)} %dynamic-update-slice.1), channel_id=1, replica_groups=mesh['img'=8,'blk'=4] {'img','blk'}, use_global_device_ids=true, to_apply=%add.43 | all-reduce | flops 384 | bytes 1536
  1027.5 41.5 %all-reduce.50 = (f32[2048]{0:T(1024)S(1)}, f32[2048]{0:T(1024)S(1)}) all-reduce(f32[2048]{0:T(1024)S(1)} %get-tuple-element.182, f32[2048]{0:T(1024)S(1)} %get-tuple-element.181), channel_id=1, replica_groups=mesh['img'=8,'blk'=4] {'img','blk'}, use_global_device_ids=true, to_apply=%region_44.45 | all-reduce | flops 4096 | bytes 32768 | tf_op jit(solution)/shard_map/psum | solution.py:116
  1090.9 39.9 %all-reduce.49 = (f32[2048]{0:T(1024)}, f32[2048]{0:T(1024)}) all-reduce(f32[2048]{0:T(1024)} %get-tuple-element.172, f32[2048]{0:T(1024)} %get-tuple-element.171), channel_id=1, replica_groups=mesh['img'=8,'blk'=4] {'img','blk'}, use_global_device_ids=true, to_apply=%region_48.49 | all-reduce | flops 4096 | bytes 32768 | tf_op jit(solution)/shard_map/psum | solution.py:116
  1137.7 41.7 %all-reduce.48 = (f32[512]{0:T(512)}, f32[512]{0:T(512)}) all-reduce(f32[512]{0:T(512)} %get-tuple-element.180, f32[512]{0:T(512)} %get-tuple-element.179), channel_id=1, replica_groups=mesh['img'=8,'blk'=4] {'img','blk'}, use_global_device_ids=true, to_apply=%region_52.53 | all-reduce | flops 1024 | bytes 8192 | tf_op jit(solution)/shard_map/psum | solution.py:116
  1194.8 13.7 fusion.79
  1228.2 40.1 %all-reduce.47 = (f32[512]{0:T(512)}, f32[512]{0:T(512)}) all-reduce(f32[512]{0:T(512)} %get-tuple-element.178, f32[512]{0:T(512)} %get-tuple-element.177), channel_id=1, replica_groups=mesh['img'=8,'blk'=4] {'img','blk'}, use_global_device_ids=true, to_apply=%region_56.57 | all-reduce | flops 1024 | bytes 8192 | tf_op jit(solution)/shard_map/psum | solution.py:116
  1277.8 40.9 %all-reduce.46 = (f32[2048]{0:T(1024)S(1)}, f32[2048]{0:T(1024)S(1)}) all-reduce(f32[2048]{0:T(1024)S(1)} %get-tuple-element.169, f32[2048]{0:T(1024)S(1)} %get-tuple-element.170), channel_id=1, replica_groups=mesh['img'=8,'blk'=4] {'img','blk'}, use_global_device_ids=true, to_apply=%region_60.61 | all-reduce | flops 4096 | bytes 32768 | tf_op jit(solution)/shard_map/psum | solution.py:116
  1324.2 39.6 %all-reduce.45 = (f32[512]{0:T(512)S(1)}, f32[512]{0:T(512)S(1)}) all-reduce(f32[512]{0:T(512)S(1)} %get-tuple-element.176, f32[512]{0:T(512)S(1)} %get-tuple-element.175), channel_id=1, replica_groups=mesh['img'=8,'blk'=4] {'img','blk'}, use_global_device_ids=true, to_apply=%region_64.65 | all-reduce | flops 1024 | bytes 8192 | tf_op jit(solution)/shard_map/psum | solution.py:116
  1379.7 14.5 fusion.78
  1395.1 23.5 pad.154
  1420.4 23.5 pad.152
  1445.8 23.5 pad.153
  1471.1 23.3 pad.300
  1496.3 23.5 pad.301
  1521.6 23.3 pad.201
  1546.7 23.3 pad.202
  1571.9 23.3 pad.204
  1596.1 23.3 pad.205
  1695.4 41.1 %all-reduce.44 = (f32[]{:T(128)}, f32[512]{0:T(512)S(1)}, f32[512]{0:T(512)S(1)}, f32[2048]{0:T(1024)S(1)}) all-reduce(f32[]{:T(128)} %subtract_reduce_fusion, f32[512]{0:T(512)S(1)} %get-tuple-element.174, f32[512]{0:T(512)S(1)} %get-tuple-element.173, f32[2048]{0:T(1024)S(1)} %get-tuple-element.168), channel_id=1, replica_groups=mesh['img'=8,'blk'=4] {'img','blk'}, use_global_device_ids=true, to_apply=%region_39.40 | all-reduce | flops 3073 | bytes 24584 | tf_op jit(solution)/shard_map/psum | solution.py:263
  1806.2 12.8 pad.171
  1826.9 89.5 %reduce-scatter.22.cloned.1.call-done = f32[64,2048]{1,0:T(8,128)} async-done(((f32[512,2048]{1,0:T(8,128)}), f32[64,2048]{1,0:T(8,128)}) %reduce-scatter.22.cloned.1.call-update) | async-done | bytes 524304 | tf_op jit(solution)/shard_map/reduce_scatter | solution.py:366
  1918.1 89.6 %reduce-scatter.14.cloned.1.call-done = f32[64,2048]{1,0:T(8,128)} async-done(((f32[512,2048]{1,0:T(8,128)}), f32[64,2048]{1,0:T(8,128)}) %reduce-scatter.14.cloned.1.call-update) | async-done | bytes 524304 | tf_op jit(solution)/shard_map/reduce_scatter | solution.py:362
  2009.5 90.0 %reduce-scatter.18.cloned.1.call-done = f32[256,512]{1,0:T(8,128)} async-done(((f32[2048,512]{1,0:T(8,128)}), f32[256,512]{1,0:T(8,128)}) %reduce-scatter.18.cloned.1.call-update) | async-done | bytes 524304 | tf_op jit(solution)/shard_map/reduce_scatter | solution.py:364
  2101.3 150.5 %reduce-scatter.16.cloned.1.call-done = f32[128,2048]{1,0:T(8,128)} async-done(((f32[1024,2048]{1,0:T(8,128)}), f32[128,2048]{1,0:T(8,128)}) %reduce-scatter.16.cloned.1.call-update) | async-done | bytes 1048592 | tf_op jit(solution)/shard_map/reduce_scatter | solution.py:363
  2253.9 164.7 %reduce-scatter.20.cloned.1.call-done = f32[3,3,64,512]{3,2,1,0:T(8,128)} async-done(((f32[3,3,512,512]{3,2,1,0:T(8,128)}), f32[3,3,64,512]{3,2,1,0:T(8,128)}) %reduce-scatter.20.cloned.1.call-update) | async-done | bytes 1179664 | tf_op jit(solution)/shard_map/reduce_scatter | solution.py:365
  2420.7 164.7 %reduce-scatter.12.cloned.1.call-done = f32[3,3,64,512]{3,2,1,0:T(8,128)} async-done(((f32[3,3,512,512]{3,2,1,0:T(8,128)}), f32[3,3,64,512]{3,2,1,0:T(8,128)}) %reduce-scatter.12.cloned.1.call-update) | async-done | bytes 1179664 | tf_op jit(solution)/shard_map/reduce_scatter | solution.py:361
  2587.6 283.3 %reduce-scatter.24.cloned.1.call-done = f32[256,2048]{1,0:T(8,128)} async-done(((f32[2048,2048]{1,0:T(8,128)}), f32[256,2048]{1,0:T(8,128)}) %reduce-scatter.24.cloned.1.call-update) | async-done | bytes 2097168 | tf_op jit(solution)/shard_map/reduce_scatter | solution.py:367
  2879.0 15.8 pad.170
  2907.9 45.4 %all-reduce.56.cloned.1.call-done = (bf16[128,512]{1,0:T(8,128)(2,1)}, bf16[3,3,64,512]{3,2,1,0:T(8,128)(2,1)}, bf16[64,2048]{1,0:T(8,128)(2,1)}, bf16[128,2048]...) async-done(((bf16[128,512]{1,0:T(8,128)(2,1)}, ...) | async-done | bytes 3735568 | tf_op jit(solution)/shard_map/psum | solution.py:381
  (727 shorter events, 575.7 us)
Async XLA Ops:
  7.2 94.0 %all-gather.10.cloned.1.call-start = ((), (), s32[]{:S(2)}) async-start(), calls=%async_computation.9 | async-start | bytes 1179648 | tf_op jit(solution)/shard_map/all_gather | solution.py:178
  7.9 327.5 %all-gather.16.cloned.1.call-start = ((), (), s32[]{:S(2)}) async-start(), calls=%async_computation.12 | async-start | bytes 4718592 | tf_op jit(solution)/shard_map/all_gather | solution.py:181
  8.7 330.3 %all-gather.12.cloned.1.call-start = ((), (), s32[]{:S(2)}) async-start(), calls=%async_computation.10 | async-start | bytes 5308416 | tf_op jit(solution)/shard_map/all_gather | solution.py:179
  9.4 418.2 %all-gather.14.cloned.1.call-start = ((), (), s32[]{:S(2)}) async-start(), calls=%async_computation.11 | async-start | bytes 2359296 | tf_op jit(solution)/shard_map/all_gather | solution.py:180
  10.0 511.7 %all-gather.18.cloned.1.call-start = ((), (), s32[]{:S(2)}) async-start(), calls=%async_computation.13 | async-start | bytes 2359296 | tf_op jit(solution)/shard_map/all_gather | solution.py:182
  10.6 648.9 %all-gather.20.cloned.1.call-start = ((), (), s32[]{:S(2)}) async-start(), calls=%async_computation.14 | async-start | bytes 5308416 | tf_op jit(solution)/shard_map/all_gather | solution.py:183
  11.1 736.3 %all-gather.22.cloned.1.call-start = ((), (), s32[]{:S(2)}) async-start(), calls=%async_computation.15 | async-start | bytes 2359296 | tf_op jit(solution)/shard_map/all_gather | solution.py:184
  11.9 835.0 %all-gather.24.cloned.1.call-start = ((), (), s32[]{:S(2)}) async-start(), calls=%async_computation.16 | async-start | bytes 9437184 | tf_op jit(solution)/shard_map/all_gather | solution.py:185
  12.7 1808.8 %reduce-scatter.26.cloned.1.call-start = ((), (), s32[]{:S(2)}) async-start(), calls=%async_computation.25 | async-start | bytes 1179648 | tf_op jit(solution)/shard_map/reduce_scatter | solution.py:368
  16.6 171.3 %copy-start.146 = (f32[512]{0:T(512)}, f32[512]{0:T(512)S(1)}, u32[]{:S(2)}) copy-start(f32[512]{0:T(512)S(1)} %get-tuple-element.290) | copy-start | bytes 6148
  16.7 411.0 %copy-start.113 = (f32[512]{0:T(512)}, f32[512]{0:T(512)S(1)}, u32[]{:S(2)}) copy-start(f32[512]{0:T(512)S(1)} %get-tuple-element.289) | copy-start | bytes 6148
  17.9 170.1 %copy-start.143 = (f32[512]{0:T(512)}, f32[512]{0:T(512)S(1)}, u32[]{:S(2)}) copy-start(f32[512]{0:T(512)S(1)} %get-tuple-element.293) | copy-start | bytes 6148
  17.9 409.7 %copy-start.110 = (f32[512]{0:T(512)}, f32[512]{0:T(512)S(1)}, u32[]{:S(2)}) copy-start(f32[512]{0:T(512)S(1)} %get-tuple-element.292) | copy-start | bytes 6148
  18.5 499.7 %copy-start.127 = (f32[2048]{0:T(1024)}, f32[2048]{0:T(1024)S(1)}, u32[]{:S(2)}) copy-start(f32[2048]{0:T(1024)S(1)} %get-tuple-element.295) | copy-start | bytes 24580
  18.5 499.7 %copy-start.128 = (f32[2048]{0:T(1024)}, f32[2048]{0:T(1024)S(1)}, u32[]{:S(2)}) copy-start(f32[2048]{0:T(1024)S(1)} %get-tuple-element.296) | copy-start | bytes 24580
  104.5 84.2 %copy-start = (f32[1072,512]{1,0:T(8,128)}, f32[1072,512]{1,0:T(8,128)S(1)}, u32[]{:S(2)}) copy-start(f32[1072,512]{1,0:T(8,128)S(1)} %get-tuple-element.308) | copy-start | bytes 6586372
  261.5 68.9 %copy-start.40 = (bf16[4,7,7,512]{3,2,1,0:T(8,128)(2,1)S(1)}, bf16[4,7,7,512]{3,2,1,0:T(8,128)(2,1)}, u32[]{:S(2)}) copy-start(bf16[4,7,7,512]{3,2,1,0:T(8,128)(2,1)} %slice.332) | copy-start | bytes 602116
  261.5 68.9 %copy-start.39 = (bf16[4,7,7,512]{3,2,1,0:T(8,128)(2,1)S(1)}, bf16[4,7,7,512]{3,2,1,0:T(8,128)(2,1)}, u32[]{:S(2)}) copy-start(bf16[4,7,7,512]{3,2,1,0:T(8,128)(2,1)} %slice.333) | copy-start | bytes 602116
  261.7 68.8 %copy-start.38 = (bf16[4,7,7,512]{3,2,1,0:T(8,128)(2,1)S(1)}, bf16[4,7,7,512]{3,2,1,0:T(8,128)(2,1)}, u32[]{:S(2)}) copy-start(bf16[4,7,7,512]{3,2,1,0:T(8,128)(2,1)} %slice.334) | copy-start | bytes 602116
  269.0 61.4 %copy-start.37 = (bf16[4,7,7,512]{3,2,1,0:T(8,128)(2,1)S(1)}, bf16[4,7,7,512]{3,2,1,0:T(8,128)(2,1)}, u32[]{:S(2)}) copy-start(bf16[4,7,7,512]{3,2,1,0:T(8,128)(2,1)} %slice.335) | copy-start | bytes 602116
  339.0 136.1 %copy-start.1 = (f32[268,2048]{1,0:T(8,128)}, f32[268,2048]{1,0:T(8,128)S(1)}, u32[]{:S(2)}) copy-start(f32[268,2048]{1,0:T(8,128)S(1)} %get-tuple-element.306) | copy-start | bytes 6586372
  521.6 86.1 %copy-start.145 = (f32[512]{0:T(512)S(1)}, f32[512]{0:T(512)}, u32[]{:S(2)}) copy-start(f32[512]{0:T(512)} %get-tuple-element.291) | copy-start | bytes 6148
  521.6 86.1 %copy-start.148 = (f32[512]{0:T(512)S(1)}, f32[512]{0:T(512)}, u32[]{:S(2)}) copy-start(f32[512]{0:T(512)} %get-tuple-element.288) | copy-start | bytes 6148
  659.4 86.6 %copy-start.150 = (f32[512]{0:T(512)S(1)}, f32[512]{0:T(512)}, u32[]{:S(2)}) copy-start(f32[512]{0:T(512)} %copy-done.149) | copy-start | bytes 6148
  659.4 86.6 %copy-start.152 = (f32[512]{0:T(512)S(1)}, f32[512]{0:T(512)}, u32[]{:S(2)}) copy-start(f32[512]{0:T(512)} %copy-done.151) | copy-start | bytes 6148
  659.4 86.6 %copy-start.154 = (f32[512]{0:T(512)S(1)}, f32[512]{0:T(512)}, u32[]{:S(2)}) copy-start(f32[512]{0:T(512)} %copy-done.153) | copy-start | bytes 6148
  659.5 88.5 %copy-start.116 = (f32[512]{0:T(512)S(1)}, f32[512]{0:T(512)}, u32[]{:S(2)}) copy-start(f32[512]{0:T(512)} %get-tuple-element.287) | copy-start | bytes 6148
  704.9 47.1 %copy-start.79 = (f32[512]{0:T(512)}, f32[512]{0:T(512)S(1)}, u32[]{:S(2)}) copy-start(f32[512]{0:T(512)S(1)} %broadcast_multiply_fusion.17) | copy-start | bytes 6148
  752.0 82.3 %copy-start.93 = (f32[2048]{0:T(1024)S(1)}, f32[2048]{0:T(1024)}, u32[]{:S(2)}) copy-start(f32[2048]{0:T(1024)} %get-tuple-element.294) | copy-start | bytes 24580
  752.0 82.3 %copy-start.94 = (f32[2048]{0:T(1024)S(1)}, f32[2048]{0:T(1024)}, u32[]{:S(2)}) copy-start(f32[2048]{0:T(1024)} %get-tuple-element.286) | copy-start | bytes 24580
  851.5 174.0 %copy-start.129 = (f32[2048]{0:T(1024)S(1)}, f32[2048]{0:T(1024)}, u32[]{:S(2)}) copy-start(f32[2048]{0:T(1024)} %get-tuple-element.283) | copy-start | bytes 24580
  891.7 177.4 %copy-start.71 = (f32[2048]{0:T(1024)}, f32[2048]{0:T(1024)S(1)}, u32[]{:S(2)}) copy-start(f32[2048]{0:T(1024)S(1)} %broadcast_multiply_fusion.2) | copy-start | bytes 24580
  933.2 135.9 %copy-start.89 = (f32[2048]{0:T(1024)}, f32[2048]{0:T(1024)S(1)}, u32[]{:S(2)}) copy-start(f32[2048]{0:T(1024)S(1)} %get-tuple-element.297) | copy-start | bytes 24580
  933.2 135.9 %copy-start.124 = (f32[2048]{0:T(1024)}, f32[2048]{0:T(1024)S(1)}, u32[]{:S(2)}) copy-start(f32[2048]{0:T(1024)S(1)} %get-tuple-element.277) | copy-start | bytes 24580
  1222.9 47.9 %copy-start.70 = (f32[2048]{0:T(1024)S(1)}, f32[2048]{0:T(1024)}, u32[]{:S(2)}) copy-start(f32[2048]{0:T(1024)} %copy-done.69) | copy-start | bytes 24580
  1270.8 48.5 %copy-start.86 = (f32[2048]{0:T(1024)S(1)}, f32[2048]{0:T(1024)}, u32[]{:S(2)}) copy-start(f32[2048]{0:T(1024)} %copy-done.85) | copy-start | bytes 24580
  1270.8 48.5 %copy-start.126 = (f32[2048]{0:T(1024)S(1)}, f32[2048]{0:T(1024)}, u32[]{:S(2)}) copy-start(f32[2048]{0:T(1024)} %get-tuple-element.274) | copy-start | bytes 24580
  1690.6 48.5 %copy-start.157 = (f32[512]{0:T(512)S(1)}, f32[512]{0:T(512)}, u32[]{:S(2)}) copy-start(f32[512]{0:T(512)} %get-tuple-element.278) | copy-start | bytes 6148
  1690.6 134.7 %reduce-scatter.10.cloned.1.call-start = ((), (), s32[]{:S(2)}) async-start(), calls=%async_computation.17 | async-start | bytes 2359296 | tf_op jit(solution)/shard_map/reduce_scatter | solution.py:360
  1746.1 170.2 %reduce-scatter.22.cloned.1.call-start = ((), (), s32[]{:S(2)}) async-start(), calls=%async_computation.23 | async-start | bytes 4718592 | tf_op jit(solution)/shard_map/reduce_scatter | solution.py:366
  1750.8 256.9 %reduce-scatter.14.cloned.1.call-start = ((), (), s32[]{:S(2)}) async-start(), calls=%async_computation.19 | async-start | bytes 4718592 | tf_op jit(solution)/shard_map/reduce_scatter | solution.py:362
  1756.1 343.3 %reduce-scatter.18.cloned.1.call-start = ((), (), s32[]{:S(2)}) async-start(), calls=%async_computation.21 | async-start | bytes 4718592 | tf_op jit(solution)/shard_map/reduce_scatter | solution.py:364
  1760.4 491.4 %reduce-scatter.16.cloned.1.call-start = ((), (), s32[]{:S(2)}) async-start(), calls=%async_computation.20 | async-start | bytes 9437184 | tf_op jit(solution)/shard_map/reduce_scatter | solution.py:363
  1771.7 646.8 %reduce-scatter.20.cloned.1.call-start = ((), (), s32[]{:S(2)}) async-start(), calls=%async_computation.22 | async-start | bytes 10616832 | tf_op jit(solution)/shard_map/reduce_scatter | solution.py:365
  1780.1 805.3 %reduce-scatter.12.cloned.1.call-start = ((), (), s32[]{:S(2)}) async-start(), calls=%async_computation.18 | async-start | bytes 10616832 | tf_op jit(solution)/shard_map/reduce_scatter | solution.py:361
  1788.1 1082.8 %reduce-scatter.24.cloned.1.call-start = ((), (), s32[]{:S(2)}) async-start(), calls=%async_computation.24 | async-start | bytes 18874368 | tf_op jit(solution)/shard_map/reduce_scatter | solution.py:367
  1797.0 1156.3 %all-reduce.56.cloned.1.call-start = ((), (), s32[]{:S(2)}) async-start(), calls=%async_computation.26 | async-start | bytes 7471104 | tf_op jit(solution)/shard_map/psum | solution.py:381
  2906.7 50.7 %copy-start.177 = (f32[10240]{0:T(1024)}, f32[10240]{0:T(1024)S(1)}, u32[]{:S(2)}) copy-start(f32[10240]{0:T(1024)S(1)} %constant_dynamic-update-slice_fusion.47) | copy-start | bytes 122884
  (148 other events, 1051.3 us)
Sparse Core Ops, SparseCore 0:
  10.1 46.1 all-gather.9
  58.4 75.1 all-gather.15
  135.8 79.1 all-gather.11
  217.0 47.4 all-gather.13
  266.4 47.7 all-gather.17
  316.3 78.6 all-gather.19
  397.1 48.5 all-gather.21
  447.8 125.5 all-gather.23
  1690.7 63.1 reduce-scatter.25
  1758.3 66.9 reduce-scatter.9
  1829.3 86.9 reduce-scatter.21
  1919.9 87.8 reduce-scatter.13
  2011.8 87.6 reduce-scatter.17
  2103.0 148.7 reduce-scatter.15
  2255.7 162.8 reduce-scatter.19
  2422.4 162.9 reduce-scatter.11
  2589.5 281.2 reduce-scatter.23
  2874.9 78.4 all-reduce.55
where the time goes:
time: 3000 us; the launch traced here: 2970 us
  waiting for transfers between devices  1090 us (36%)
  blocking collectives  1020 us (34%)
  local copies, waits for them, and re-layouts  634 us (21%)
  matrix products  113 us (4%)
  other arithmetic  105 us (4%)
    psum x7, blocking collectives, norm_forward(): center = lax.psum(jnp.sum(values, 0), ('img', 'blk')) / number  290 us
    psum x7, blocking collectives, norm_forward(): spread = lax.psum(jnp.sum(centered * centered, 0), ('img', 'blk')) / number  284 us
    reduce_scatter x1, waiting for transfers between devices, per_device(): lax.psum_scatter(hidden_weight_grad, 'img', scatter_dimension=0, tiled=True)  283 us
    psum x6, blocking collectives, norm_backward(): lax.psum((jnp.sum(upstream, 0), jnp.sum(upstream * normed, 0)), ('img', '...  244 us
    reduce_scatter x1, waiting for transfers between devices, per_device(): lax.psum_scatter(spatial_grad, 'img', scatter_dimension=2, tiled=True)  165 us
    reduce_scatter x1, waiting for transfers between devices, per_device(): lax.psum_scatter(spatial2_grad, 'img', scatter_dimension=2, tiled=True)  165 us
    reduce_scatter x1, waiting for transfers between devices, per_device(): lax.psum_scatter(short_grad, 'img', scatter_dimension=0, tiled=True)  151 us
    slice x20, local copies, waits for them, and re-layouts, patch_rows(): lax.slice(padded, (0, row_tap, col_tap, 0), (picture.shape[0], row_tap +...  141 us
  transfers between devices with their start and end apart: 18, of which 9 were waited for; matrix products, arithmetic and copies ran while one was open for 13% of the time, Pallas kernels for 0%

commit v1 on v0

v1 whole, which is shorter than its diff:
```python
import functools

import jax
import jax.numpy as jnp
import numpy as np
from jax import lax
from jax.experimental import pallas as pl
from jax.experimental.pallas import tpu as pltpu
from jax.sharding import PartitionSpec as P

POSITIVES = 5
EPSILON = 1e-05
NORM_EPSILON = 1e-06
SOFTMAX_TEMP = 0.1
MASKED = -1e30
GUARD = 16
SLOT = 16
VMEM_LIMIT = 56 * 1024 * 1024
AXES = ("img", "blk")
F32 = jnp.float32
BF16 = jnp.bfloat16

NN = (((1,), (0,)), ((), ()))
NT = (((1,), (1,)), ((), ()))
TN = (((0,), (0,)), ((), ()))


def dot(left, right, dims=NN):
    return lax.dot_general(left, right, dims, preferred_element_type=F32)


def call(kernel, grid, inputs, outputs, scratch=(), flops=0):
    moved = sum(a.size * a.dtype.itemsize for a, _, _ in inputs)
    moved += sum(int(np.prod(s)) * jnp.dtype(d).itemsize for s, d, _, _ in outputs)
    return pl.pallas_call(
        kernel,
        grid=grid,
        in_specs=[pl.BlockSpec(b, m) for _, b, m in inputs],
        out_specs=[pl.BlockSpec(b, m) for _, _, b, m in outputs],
        out_shape=[jax.ShapeDtypeStruct(s, d) for s, d, _, _ in outputs],
        scratch_shapes=list(scratch),
        compiler_params=pltpu.CompilerParams(vmem_limit_bytes=VMEM_LIMIT),
        cost_estimate=pl.CostEstimate(flops=flops, bytes_accessed=moved, transcendentals=0),
    )(*[a for a, _, _ in inputs])


def whole(a):
    return (a, a.shape, lambda *_: (0,) * a.ndim)


def cols(a, width):
    return (a, a.shape[:-1] + (width,), lambda i: (0,) * (a.ndim - 1) + (i,))


def rows(a, height):
    return (a, (height,) + a.shape[1:], lambda i: (i,) + (0,) * (a.ndim - 1))


def out_whole(shape, dtype):
    return (shape, dtype, shape, lambda *_: (0,) * len(shape))


def out_cols(shape, dtype, width):
    return (shape, dtype, shape[:-1] + (width,), lambda i: (0,) * (len(shape) - 1) + (i,))


def sigmoid(v):
    return 1.0 / (1.0 + jnp.exp(-v))


def spread(mask, width):
    return jnp.concatenate([mask] * (width // mask.shape[1]), 1)


def column_sum(v):
    return jnp.sum(v, 0, keepdims=True)


class Frames:
    def __init__(self, large, small):
        self.large, self.small = large.shape[0], small.shape[0]
        self.large_in, self.small_in = large.shape[1], small.shape[1]
        self.lo, self.so = self.large_in // 2, self.small_in // 2
        self.lp, self.sp = self.lo + 1, self.so + 1
        self.lrows, self.srows = self.large * self.lp**2, self.small * self.sp**2
        self.rows = self.lrows + self.srows
        self.valid = self.large * self.lo**2 + self.small * self.so**2
        self.views = self.large + self.small

    def mask(self):
        def grid(number, out):
            g = np.zeros((number, out + 1, out + 1), np.float32)
            g[:, :out, :out] = 1
            return g.reshape(-1)

        m = np.concatenate([grid(self.large, self.lo), grid(self.small, self.so)])
        return jnp.asarray(np.repeat(m[:, None], 128, 1))

    def cells(self):
        c = np.zeros((SLOT, 1), np.float32)
        c[: self.large] = 1.0 / self.lo**2
        c[self.large : self.views] = 1.0 / self.so**2
        return c

    def shifted(self, ref, row, col):
        a = GUARD + row * self.lp + col
        b = GUARD + self.lrows + row * self.sp + col
        return jnp.concatenate([ref[a : a + self.lrows, :], ref[b : b + self.srows, :]], 0)

    def per_view(self, v):
        w = v.shape[1]
        large = jnp.sum(v[: self.lrows].reshape(self.large, -1, w), 1)
        small = jnp.sum(v[self.lrows :].reshape(self.small, -1, w), 1)
        return large, small

    def to_rows(self, v):
        w = v.shape[1]
        large = jnp.broadcast_to(
            v[: self.large][:, None, :], (self.large, self.lp**2, w)
        ).reshape(self.lrows, w)
        small = jnp.broadcast_to(
            v[self.large : self.views][:, None, :], (self.small, self.sp**2, w)
        ).reshape(self.srows, w)
        return jnp.concatenate([large, small], 0)


class Norm:
    def __init__(self, stats, affine, count):
        self.center = stats[0:1, :]
        self.factor = lax.rsqrt(stats[1:2, :] / count + EPSILON)
        self.gain = affine[0:1, :]
        self.offset = affine[1:2, :]
        self.count = count

    def hat(self, v):
        return (v - self.center) * self.factor

    def scaled(self, hat):
        return hat * self.gain + self.offset

    def backward(self, d, hat, sums):
        return (self.gain * self.factor) * (
            d - sums[0:1, :] / self.count - hat * (sums[1:2, :] / self.count)
        )


def slope(v):
    s = sigmoid(v)
    return s * (1.0 + v * (1.0 - s))


def store_stats(ref, blocks, mask, count):
    center = sum(column_sum(b[...] * mask) for b in blocks) / count
    square = sum(column_sum(jnp.square((b[...] - center) * mask)) for b in blocks)
    ref[0:1, :] = center
    ref[1:2, :] = square


def lanes(width):
    return [slice(at, at + 128) for at in range(0, width, 128)]


def parity_pieces(f):
    for large, number, out, pitch, base in (
        (True, f.large, f.lo, f.lp, 0),
        (False, f.small, f.so, f.sp, f.lrows),
    ):
        for n in range(number):
            for i in range(out):
                for ph in range(2):
                    for pw in range(2):
                        at = (2 * ph + pw) * f.rows + base + n * pitch**2 + i * pitch
                        yield large, n, 2 * i + ph, pw, at, pitch


def split_kernel(f, large_ref, small_ref, out_ref, lt, st, acc):
    acc[...] = jnp.zeros_like(acc)
    for k, lane in enumerate(lanes(out_ref.shape[1])):
        for t, ref, side in ((lt, large_ref, f.large_in), (st, small_ref, f.small_in)):
            t[k] = jnp.zeros_like(t[k])
            t[k, :, :, 0:side, :] = ref[:, :, :, lane].astype(F32)
        for large, n, row, pw, at, pitch in parity_pieces(f):
            t = lt if large else st
            acc[at : at + pitch, lane] = t[k, n, row, pl.ds(pw, pitch, stride=2), :]
    out_ref[...] = acc[...].astype(BF16)


def parity_scratch(f, width):
    return [
        pltpu.VMEM((width // 128, f.large, f.large_in, 2 * f.lp, 128), F32),
        pltpu.VMEM((width // 128, f.small, f.small_in, 2 * f.sp, 128), F32),
        pltpu.VMEM((4 * f.rows, width), F32),
    ]


def split_cells(f, large, small, width=256):
    c = large.shape[3]
    return call(
        functools.partial(split_kernel, f),
        (c // width,),
        [cols(large, width), cols(small, width)],
        [out_cols((4 * f.rows, c), BF16, width)],
        parity_scratch(f, width),
    )[0]


def linear_kernel(f, count, x_ref, w_ref, mask_ref, out_ref, stats_ref):
    width = out_ref.shape[1]
    mask = spread(mask_ref[...], width)
    blocks = []
    for at in range(0, out_ref.shape[0], f.rows):
        block = out_ref.at[at : at + f.rows, :]
        block[...] = dot(x_ref[at : at + f.rows, :], w_ref[...])
        blocks.append(block)
    store_stats(stats_ref, blocks, mask, count)


def linear(f, x, w, mask, phases, width):
    n = w.shape[1]
    x_in = (x, (phases * f.rows, x.shape[1]), lambda i: (0, 0))
    return call(
        functools.partial(linear_kernel, f, phases * f.valid),
        (n // width,),
        [x_in, cols(w, width), whole(mask)],
        [out_cols((phases * f.rows, n), F32, width), out_cols((2, n), F32, width)],
        flops=2 * phases * f.rows * w.size,
    )


TAPS = [(p, q) for p in range(3) for q in range(3)]


def conv_kernel(
    f, stride, count, pre_ref, stats_ref, affine_ref, w_ref, mask_ref,
    patch_ref, out_ref, new_ref, act,
):
    width = pre_ref.shape[1]

    @pl.when(pl.program_id(0) == 0)
    def _():
        norm = Norm(stats_ref, affine_ref, count)
        mask = spread(mask_ref[...], width)
        for phase in range(act.shape[0]):
            act[phase, 0:GUARD, :] = jnp.zeros((GUARD, width), F32)
            act[phase, GUARD + f.rows :, :] = jnp.zeros((GUARD, width), F32)
            v = norm.scaled(norm.hat(pre_ref[phase * f.rows : (phase + 1) * f.rows, :]))
            act[phase, GUARD : GUARD + f.rows, :] = v * sigmoid(v) * mask
        for tap, (p, q) in enumerate(TAPS):
            if stride == 2:
                phase = 2 * (p != 1) + (q != 1)
                step = (-(p == 0), -(q == 0))
            else:
                phase, step = 0, (p - 1, q - 1)
            patch_ref[:, tap * width : (tap + 1) * width] = f.shifted(
                act.at[phase], *step
            ).astype(BF16)

    out_ref[...] = dot(patch_ref[...], w_ref[...])
    store_stats(new_ref, [out_ref], spread(mask_ref[...], out_ref.shape[1]), f.valid)


def conv(f, stride, count, pre, stats, affine, w, mask, tile=256):
    c, n = pre.shape[1], w.shape[1]
    phases = stride * stride
    return call(
        functools.partial(conv_kernel, f, stride, count),
        (n // tile,),
        [whole(pre), whole(stats), whole(affine), cols(w, tile), whole(mask)],
        [
            out_whole((f.rows, 9 * c), BF16),
            out_cols((f.rows, n), F32, tile),
            out_cols((2, n), F32, tile),
        ],
        [pltpu.VMEM((phases, f.rows + 2 * GUARD, c), F32)],
        flops=2 * f.rows * w.size,
    )


def expand_kernel(f, count, pre_ref, stats_ref, affine_ref, w_ref, mask_ref, low_ref, out_ref, new_ref):
    @pl.when(pl.program_id(0) == 0)
    def _():
        norm = Norm(stats_ref, affine_ref, count)
        v = norm.scaled(norm.hat(pre_ref[...]))
        low_ref[...] = (v * sigmoid(v) * spread(mask_ref[...], v.shape[1])).astype(BF16)

    out_ref[...] = dot(low_ref[...], w_ref[...])
    store_stats(new_ref, [out_ref], spread(mask_ref[...], out_ref.shape[1]), f.valid)


def expand(f, count, pre, stats, affine, w, mask, tile=512):
    c, n = w.shape
    return call(
        functools.partial(expand_kernel, f, count),
        (n // tile,),
        [whole(pre), whole(stats), whole(affine), cols(w, tile), whole(mask)],
        [
            out_whole((f.rows, c), BF16),
            out_cols((f.rows, n), F32, tile),
            out_cols((2, n), F32, tile),
        ],
        flops=2 * f.rows * w.size,
    )


def mix_kernel(
    f, count, exp_ref, skip_ref, stats_a, affine_a, stats_b, affine_b, w_ref, mask_ref,
    low_ref, pre_ref, out_ref, new_ref,
):
    step = pl.program_id(0)
    mask = spread(mask_ref[...], exp_ref.shape[1])
    first = Norm(stats_a, affine_a, count)
    second = Norm(stats_b, affine_b, count)
    v = first.scaled(first.hat(exp_ref[...])) + second.scaled(second.hat(skip_ref[...]))
    pre_ref[...] = v
    low = (v * sigmoid(v) * mask).astype(BF16)
    low_ref[...] = low
    part = dot(low, w_ref[...])

    @pl.when(step == 0)
    def _():
        out_ref[...] = part

    @pl.when(step > 0)
    def _():
        out_ref[...] += part

    @pl.when(step == pl.num_programs(0) - 1)
    def _():
        store_stats(new_ref, [out_ref], spread(mask_ref[...], out_ref.shape[1]), f.valid)


def mix(f, count, expanded, skipped, stats_a, affine_a, stats_b, affine_b, w, mask, tile=512):
    k, n = w.shape
    return call(
        functools.partial(mix_kernel, f, count),
        (k // tile,),
        [cols(a, tile) for a in (expanded, skipped, stats_a, affine_a, stats_b, affine_b)]
        + [rows(w, tile), whole(mask)],
        [
            out_cols((f.rows, k), BF16, tile),
            out_cols((f.rows, k), F32, tile),
            out_whole((f.rows, n), F32),
            out_whole((2, n), F32),
        ],
        flops=2 * f.rows * w.size,
    )


def pool_kernel(
    f, count, wide_ref, pre_ref, stats_ref, affine_ref, mask_ref,
    pooled_ref, slope_ref, view_ref,
):
    mask = spread(mask_ref[...], wide_ref.shape[1])
    norm = Norm(stats_ref, affine_ref, count)
    hat = norm.hat(wide_ref[...])
    before = pre_ref[...]
    v = norm.scaled(hat) + before * sigmoid(before)
    s = sigmoid(v)
    d = s * (1.0 + v * (1.0 - s)) * mask
    slope_ref[...] = d

    def put(ref, at, pair, scale=(1.0, 1.0)):
        ref[at : at + f.large, :] = pair[0] * scale[0]
        ref[at + f.large : at + f.views, :] = pair[1] * scale[1]
        if f.views < SLOT:
            ref[at + f.views : at + SLOT, :] = jnp.zeros((SLOT - f.views, ref.shape[1]), F32)

    put(pooled_ref, 0, f.per_view(v * s * mask), (1.0 / f.lo**2, 1.0 / f.so**2))
    put(view_ref, 0, f.per_view(d))
    put(view_ref, SLOT, f.per_view(d * hat))


def pool(f, count, wide, pre, stats, affine, mask, tile=512):
    n = wide.shape[1]
    return call(
        functools.partial(pool_kernel, f, count),
        (n // tile,),
        [cols(a, tile) for a in (wide, pre, stats, affine)] + [whole(mask)],
        [
            out_cols((SLOT, n), F32, tile),
            out_cols((f.rows, n), F32, tile),
            out_cols((2 * SLOT, n), F32, tile),
        ],
        flops=20 * wide.size,
    )


def head_kernel(
    f, devices, shard, place_ref, p_ref, h_ref, e_ref, affine_ref, label_col, label_row,
    view_ref, cells_ref,
    loss_ref, hidden_ref, embed_ref, gain_ref, back_ref, sums_ref,
    hat, low, emb, grad, own, factors, pooled_grad,
):
    step = pl.program_id(0)
    tiles = pl.num_programs(0) // 2
    v = p_ref.shape[0]
    tile = h_ref.shape[1]
    number = devices * f.views
    row_id = lax.broadcasted_iota(jnp.int32, (v, 128), 0)
    row_ok = (row_id % SLOT < f.views).astype(F32)
    mask = spread(row_ok, tile)
    gain, offset = affine_ref[0:1, :], affine_ref[1:2, :]

    @pl.when(step < tiles)
    def _():
        t = dot(p_ref[...], h_ref[...])
        center = column_sum(t * mask) / number
        t = (t - center) * mask
        factor = lax.rsqrt(column_sum(t * t) / number + EPSILON)
        t = t * factor
        hat[step] = t
        factors[step, 0:1, :] = factor
        t = t * gain + offset
        lowered = (t * sigmoid(t) * mask).astype(BF16)
        low[step] = lowered
        part = dot(lowered, e_ref[...])

        @pl.when(step == 0)
        def _():
            emb[...] = part

        @pl.when(step > 0)
        def _():
            emb[...] += part

    @pl.when(step == tiles - 1)
    def _():
        e = emb[...]
        inverse = lax.rsqrt(jnp.sum(e * e, 1, keepdims=True) + NORM_EPSILON)
        unit = e * inverse
        lowered = unit.astype(BF16)
        scores = dot(lowered, lowered, NT) / SOFTMAX_TEMP
        i = lax.broadcasted_iota(jnp.int32, (v, v), 0)
        j = lax.broadcasted_iota(jnp.int32, (v, v), 1)
        i_ok = i % SLOT < f.views
        j_ok = j % SLOT < f.views
        use = (i != j) & i_ok & j_ok
        paired = use & (label_col[:, 0:1] == label_row[0:1, :])
        weight = paired.astype(F32) / POSITIVES
        masked = jnp.where(use, scores, MASKED)

        def log_total(axis):
            top = jnp.max(masked, axis, keepdims=True)
            terms = jnp.where(use, jnp.exp(masked - top), 0.0)
            total = jnp.sum(terms, axis, keepdims=True)
            return top + jnp.log(jnp.where(total > 0.0, total, 1.0))

        by_row = log_total(1)
        by_col = log_total(0)
        positive = jnp.sum(jnp.where(paired, scores, 0.0), 1, keepdims=True)
        fine = lax.broadcasted_iota(jnp.int32, (v, 1), 0) % SLOT < f.views
        per_row = jnp.where(fine, by_row - positive / POSITIVES, 0.0)
        loss_ref[...] = jnp.broadcast_to(
            jnp.sum(per_row, 0, keepdims=True) / number, loss_ref.shape
        )

        def pair_grad(logs):
            chance = jnp.where(use, jnp.exp(masked - logs), 0.0)
            return ((chance - weight) / number).astype(BF16)

        unit_grad = (dot(pair_grad(by_row), lowered) + dot(pair_grad(by_col), lowered)) / SOFTMAX_TEMP
        along = jnp.sum(unit * unit_grad, 1, keepdims=True)
        g = inverse * (unit_grad - unit * along)
        grad[...] = jnp.where(fine, g, 0.0).astype(BF16)

    @pl.when(step >= tiles)
    def _():
        now = step - tiles
        t = hat[now]
        d = dot(grad[...], e_ref[...], NT) * slope(t * gain + offset)
        shift_grad = column_sum(d)
        gain_grad = column_sum(d * t)
        gain_ref[0:1, :] = gain_grad
        gain_ref[1:2, :] = shift_grad
        d = (factors[now, 0:1, :] * gain) * (d - shift_grad / number - t * (gain_grad / number))
        lowered = (d * mask).astype(BF16)
        own[...] = lowered
        mine = pl.multiple_of(place_ref[0] * shard, 128)
        hidden_ref[...] = dot(p_ref[:, pl.ds(mine, shard)], lowered, TN)
        here = pl.multiple_of(place_ref[1] * SLOT, SLOT)
        part = dot(own[pl.ds(here, SLOT), :], h_ref[...], NT)

        @pl.when(now == 0)
        def _():
            pooled_grad[...] = part

        @pl.when(now > 0)
        def _():
            pooled_grad[...] += part

    @pl.when(step == 2 * tiles - 1)
    def _():
        per = tile // shard if tile > shard else 1
        at = place_ref[0] // per
        inner = pl.multiple_of((place_ref[0] % per) * shard, 128)
        embed_ref[...] = dot(low[at, :, pl.ds(inner, shard)], grad[...], TN)
        b = pooled_grad[...] * cells_ref[...]
        back_ref[...] = b
        sums_ref[0:1, :] = column_sum(b * view_ref[0:SLOT, :])
        sums_ref[1:2, :] = column_sum(b * view_ref[SLOT:, :])


def head(f, devices, shard, place, pooled, hidden, embed, affine, labels, view_sums, tile=512):
    v, c = pooled.shape
    n, w = embed.shape
    tiles = n // tile
    label_col = jnp.broadcast_to(labels[:, None], (v, 128))
    label_row = jnp.broadcast_to(labels[None, :], (8, v))
    cells = jnp.asarray(np.repeat(f.cells(), c, 1))
    late = lambda i: (0, jnp.maximum(i - tiles, 0))
    inputs = [
        whole(pooled),
        (hidden, (c, tile), lambda i: (0, i % tiles)),
        (embed, (tile, w), lambda i: (i % tiles, 0)),
        (affine, (2, tile), lambda i: (0, i % tiles)),
        whole(label_col),
        whole(label_row),
        whole(view_sums),
        whole(cells),
    ]
    outputs = [
        out_whole((8, 128), F32),
        ((shard, n), F32, (shard, tile), late),
        out_whole((shard, w), F32),
        ((2, n), F32, (2, tile), late),
        out_whole((SLOT, c), F32),
        out_whole((2, c), F32),
    ]
    return pl.pallas_call(
        functools.partial(head_kernel, f, devices, shard),
        grid=(2 * tiles,),
        in_specs=[pl.BlockSpec(memory_space=pltpu.SMEM)] + [pl.BlockSpec(b, m) for _, b, m in inputs],
        out_specs=[pl.BlockSpec(b, m) for _, _, b, m in outputs],
        out_shape=[jax.ShapeDtypeStruct(s, d) for s, d, _, _ in outputs],
        scratch_shapes=[
            pltpu.VMEM((tiles, v, tile), F32),
            pltpu.VMEM((tiles, v, tile), BF16),
            pltpu.VMEM((v, w), F32),
            pltpu.VMEM((v, w), BF16),
            pltpu.VMEM((v, tile), BF16),
            pltpu.VMEM((tiles, 8, tile), F32),
            pltpu.VMEM((SLOT, c), F32),
        ],
        compiler_params=pltpu.CompilerParams(vmem_limit_bytes=VMEM_LIMIT),
        cost_estimate=pl.CostEstimate(
            flops=4 * v * c * n, bytes_accessed=20 * 1024 * 1024, transcendentals=0
        ),
    )(place, *[a for a, _, _ in inputs])


def widen_back_kernel(
    f, count, wide_ref, slope_ref, back_ref, stats_ref, affine_ref, sums_ref, w_ref,
    turn_ref, turn_stats, turn_affine, mask_ref,
    low_ref, out_ref, new_ref,
):
    step = pl.program_id(0)
    norm = Norm(stats_ref, affine_ref, count)
    hat = norm.hat(wide_ref[...])
    d = f.to_rows(back_ref[...]) * slope_ref[...]
    low = (norm.backward(d, hat, sums_ref) * spread(mask_ref[...], hat.shape[1])).astype(BF16)
    low_ref[...] = low
    finish_back(step, dot(low, w_ref[...], NT), turn_ref, turn_stats, turn_affine, count, mask_ref, out_ref, new_ref)


def finish_back(step, part, pre_ref, stats, affine, count, mask_ref, out_ref, new_ref):
    @pl.when(step == 0)
    def _():
        out_ref[...] = part

    @pl.when(step > 0)
    def _():
        out_ref[...] += part

    @pl.when(step == pl.num_programs(0) - 1)
    def _():
        norm = Norm(stats, affine, count)
        hat = norm.hat(pre_ref[...])
        d = out_ref[...] * slope(norm.scaled(hat)) * spread(mask_ref[...], hat.shape[1])
        out_ref[...] = d
        new_ref[0:1, :] = column_sum(d)
        new_ref[1:2, :] = column_sum(d * hat)


def widen_back(f, count, wide, slopes, back, stats, affine, sums, w, turn, tstats, taffine, mask, tile=512):
    c, n = w.shape
    return call(
        functools.partial(widen_back_kernel, f, count),
        (n // tile,),
        [cols(a, tile) for a in (wide, slopes, back, stats, affine, sums, w)]
        + [whole(a) for a in (turn, tstats, taffine, mask)],
        [
            out_cols((f.rows, n), BF16, tile),
            out_whole((f.rows, c), F32),
            out_whole((2, c), F32),
        ],
        flops=2 * f.rows * w.size,
    )


def conv_back_kernel(
    f, stride, count, in_count, d_ref, pre_ref, stats_ref, affine_ref, sums_ref, w_ref,
    in_ref, in_stats, in_affine, mask_ref,
    low_ref, out_ref, new_ref, act, moved,
):
    width = d_ref.shape[1]
    steps = [(a, b) for a in (0, 1) for b in (0, 1)] if stride == 2 else [(1 - p, 1 - q) for p, q in TAPS]

    @pl.when(pl.program_id(0) == 0)
    def _():
        norm = Norm(stats_ref, affine_ref, count)
        hat = norm.hat(pre_ref[...])
        low = (norm.backward(d_ref[...], hat, sums_ref) * spread(mask_ref[...], width)).astype(BF16)
        low_ref[...] = low
        act[0:GUARD, :] = jnp.zeros((GUARD, width), F32)
        act[GUARD + f.rows :, :] = jnp.zeros((GUARD, width), F32)
        act[GUARD : GUARD + f.rows, :] = low.astype(F32)
        for k, step in enumerate(steps):
            moved[k] = f.shifted(act, *step).astype(BF16)

    tile = out_ref.shape[1]
    mask = spread(mask_ref[...], tile)
    norm = Norm(in_stats, in_affine, in_count)
    total = jnp.zeros((1, tile), F32)
    total_hat = jnp.zeros((1, tile), F32)
    for phase in range(stride * stride):
        acc = None
        for tap, (p, q) in enumerate(TAPS):
            if stride == 2:
                if phase != 2 * (p != 1) + (q != 1):
                    continue
                step = (int(p == 0), int(q == 0))
            else:
                step = (1 - p, 1 - q)
            part = dot(moved[steps.index(step)], w_ref[tap], NT)
            acc = part if acc is None else acc + part
        at = phase * f.rows
        hat = norm.hat(in_ref[at : at + f.rows, :])
        d = acc * slope(norm.scaled(hat)) * mask
        out_ref[at : at + f.rows, :] = d
        total += column_sum(d)
        total_hat += column_sum(d * hat)
    new_ref[0:1, :] = total
    new_ref[1:2, :] = total_hat


def conv_back(f, stride, count, in_count, d, pre, stats, affine, sums, w, inside, istats, iaffine, mask, tile=256):
    n = d.shape[1]
    c = w.shape[1]
    phases = stride * stride
    return call(
        functools.partial(conv_back_kernel, f, stride, count, in_count),
        (c // tile,),
        [whole(a) for a in (d, pre, stats, affine, sums)]
        + [(w, (9, tile, n), lambda i: (0, i, 0))]
        + [cols(a, tile) for a in (inside, istats, iaffine)]
        + [whole(mask)],
        [
            out_whole((f.rows, n), BF16),
            out_cols((phases * f.rows, c), F32, tile),
            out_cols((2, c), F32, tile),
        ],
        [
            pltpu.VMEM((f.rows + 2 * GUARD, n), F32),
            pltpu.VMEM((4 if stride == 2 else 9, f.rows, n), BF16),
        ],
        flops=2 * f.rows * w.size,
    )


def mix_back_kernel(
    f, count, d_ref, mix_ref, stats_ref, affine_ref, sums_ref, w_ref, back_ref, slope_ref,
    pre_ref, exp_ref, exp_stats, exp_affine, skip_ref, skip_stats, skip_affine, mask_ref,
    low_ref, out_ref, new_ref,
):
    @pl.when(pl.program_id(0) == 0)
    def _():
        norm = Norm(stats_ref, affine_ref, count)
        hat = norm.hat(mix_ref[...])
        d = norm.backward(d_ref[...], hat, sums_ref)
        low_ref[...] = (d * spread(mask_ref[...], hat.shape[1])).astype(BF16)

    g = f.to_rows(back_ref[...]) * slope_ref[...] + dot(low_ref[...], w_ref[...], NT)
    g = g * slope(pre_ref[...]) * spread(mask_ref[...], g.shape[1])
    out_ref[...] = g
    first = Norm(exp_stats, exp_affine, count)
    second = Norm(skip_stats, skip_affine, count)
    new_ref[0:1, :] = column_sum(g)
    new_ref[1:2, :] = column_sum(g * first.hat(exp_ref[...]))
    new_ref[2:3, :] = column_sum(g * second.hat(skip_ref[...]))


def mix_back(
    f, count, d, mixing, stats, affine, sums, w, back, slopes, pre,
    expanded, estats, eaffine, skipped, sstats, saffine, mask, tile=512,
):
    n, c = w.shape
    return call(
        functools.partial(mix_back_kernel, f, count),
        (n // tile,),
        [whole(a) for a in (d, mixing, stats, affine, sums)]
        + [rows(w, tile)]
        + [cols(a, tile) for a in (back, slopes, pre, expanded, estats, eaffine, skipped, sstats, saffine)]
        + [whole(mask)],
        [
            out_whole((f.rows, c), BF16),
            out_cols((f.rows, n), F32, tile),
            out_cols((3, n), F32, tile),
        ],
        flops=2 * f.rows * w.size,
    )


def block_back_kernel(
    f, count, g_ref, exp_ref, exp_stats, exp_affine, skip_ref, skip_stats, skip_affine,
    sums_ref, w_ref, turn_ref, turn_stats, turn_affine, mask_ref,
    exp_low, skip_low, out_ref, new_ref,
):
    g = g_ref[...]
    mask = spread(mask_ref[...], g.shape[1])
    sums = sums_ref[...]
    first = Norm(exp_stats, exp_affine, count)
    low = (first.backward(g, first.hat(exp_ref[...]), sums[0:2]) * mask).astype(BF16)
    exp_low[...] = low
    second = Norm(skip_stats, skip_affine, count)
    other = jnp.concatenate([sums[0:1], sums[2:3]], 0)
    skip_low[...] = (second.backward(g, second.hat(skip_ref[...]), other) * mask).astype(BF16)
    finish_back(
        pl.program_id(0), dot(low, w_ref[...], NT), turn_ref, turn_stats, turn_affine,
        count, mask_ref, out_ref, new_ref,
    )


def block_back(
    f, count, g, expanded, estats, eaffine, skipped, sstats, saffine, sums, w,
    turned, tstats, taffine, mask, tile=512,
):
    c, n = w.shape
    return call(
        functools.partial(block_back_kernel, f, count),
        (n // tile,),
        [cols(a, tile) for a in (g, expanded, estats, eaffine, skipped, sstats, saffine, sums, w)]
        + [whole(a) for a in (turned, tstats, taffine, mask)],
        [
            out_cols((f.rows, n), BF16, tile),
            out_cols((f.rows, n), BF16, tile),
            out_whole((f.rows, c), F32),
            out_whole((2, c), F32),
        ],
        flops=2 * f.rows * w.size,
    )


def input_back_kernel(
    f, count, d_ref, pre_ref, stats_ref, affine_ref, sums_ref, w_ref, sub_ref, mask_ref,
    low_ref, large_ref, small_ref, lt, st, acc,
):
    @pl.when(pl.program_id(0) == 0)
    def _():
        norm = Norm(stats_ref, affine_ref, count)
        mask = spread(mask_ref[...], d_ref.shape[1])
        for phase in range(4):
            at = phase * f.rows
            hat = norm.hat(pre_ref[at : at + f.rows, :])
            d = norm.backward(d_ref[at : at + f.rows, :], hat, sums_ref)
            low_ref[at : at + f.rows, :] = (d * mask).astype(BF16)

    for phase in range(4):
        at = phase * f.rows
        part = dot(low_ref[at : at + f.rows, :], w_ref[...], NT)
        if phase == 0:
            part = part + sub_ref[...]
        acc[at : at + f.rows, :] = part
    for k, lane in enumerate(lanes(acc.shape[1])):
        for large, n, row, pw, at, pitch in parity_pieces(f):
            t = lt if large else st
            t[k, n, row, pl.ds(pw, pitch, stride=2), :] = acc[at : at + pitch, lane]
        large_ref[:, :, :, lane] = lt[k, :, :, 0 : f.large_in, :].astype(BF16)
        small_ref[:, :, :, lane] = st[k, :, :, 0 : f.small_in, :].astype(BF16)


def input_back(f, count, d, pre, stats, affine, sums, w, sub, mask, tile=256):
    n, c = w.shape
    return call(
        functools.partial(input_back_kernel, f, count),
        (n // tile,),
        [whole(a) for a in (d, pre, stats, affine, sums)]
        + [rows(w, tile), cols(sub, tile), whole(mask)],
        [
            out_whole((4 * f.rows, c), BF16),
            out_cols((f.large, f.large_in, f.large_in, n), BF16, tile),
            out_cols((f.small, f.small_in, f.small_in, n), BF16, tile),
        ],
        parity_scratch(f, tile),
        flops=8 * f.rows * w.size,
    )


class Links:
    def __init__(self):
        self.img, self.blk = lax.axis_size("img"), lax.axis_size("blk")
        self.size = self.img * self.blk
        self.me = lax.axis_index("img") * self.blk + lax.axis_index("blk")
        low, high = self.blk.bit_length() - 1, self.img.bit_length() - 1
        self.low, self.high = low, high

    def swap(self, v, bits):
        return lax.ppermute(v, AXES, [(i, i ^ bits) for i in range(self.size)])

    def stages(self):
        found = []

        def cut(start, number):
            if number % 2 and number > 1:
                found.append([1 << start])
                start, number = start + 1, number - 1
            while number > 0:
                take = min(2, number)
                found.append([1 << (start + k) for k in range(take)])
                start, number = start + take, number - take

        cut(0, self.low)
        cut(self.low, self.high)
        return found

    def partners(self, v, stage):
        if len(stage) == 1:
            return [self.swap(v, stage[0])]
        a, b = stage
        return [self.swap(v, a), self.swap(v, b), self.swap(v, a | b)]

    def total(self, v):
        for stage in self.stages():
            got = self.partners(v, stage)
            if len(got) == 1:
                v = v + got[0]
            else:
                v = (v + got[0]) + (got[1] + got[2])
        return v

    def moments(self, v, count):
        for stage in self.stages():
            got = [v] + self.partners(v, stage)
            if len(got) == 2:
                a, b = got
                center = (a[0] + b[0]) * 0.5
                square = (a[1] + b[1]) + count * (
                    jnp.square(a[0] - center) + jnp.square(b[0] - center)
                )
            else:
                a, b, c, d = got
                center = ((a[0] + b[0]) + (c[0] + d[0])) * 0.25
                square = ((a[1] + b[1]) + (c[1] + d[1])) + count * (
                    (jnp.square(a[0] - center) + jnp.square(b[0] - center))
                    + (jnp.square(c[0] - center) + jnp.square(d[0] - center))
                )
            count = count * len(got)
            v = jnp.stack([center, square])
        return v

    def gather(self, v):
        depth = 0
        for bit in reversed(range(self.low + self.high)):
            got = self.swap(v, 1 << bit)
            upper = (self.me >> bit) & 1
            v = jnp.stack(
                [jnp.where(upper == 0, v, got), jnp.where(upper == 0, got, v)], depth
            )
            depth += 1
        return v.reshape((self.size,) + v.shape[depth:])


def head_plain(f, links, pooled, hidden, embed, affine, labels):
    number = links.size * f.views
    line = dot(pooled, hidden)
    center = lax.psum(jnp.sum(line, 0), AXES) / number
    line = line - center
    factor = lax.rsqrt(lax.psum(jnp.sum(line * line, 0), AXES) / number + EPSILON)
    hat = line * factor
    v = hat * affine[0] + affine[1]
    low = (v * sigmoid(v)).astype(BF16)
    e = dot(low, embed)
    inverse = lax.rsqrt(jnp.sum(e * e, 1, keepdims=True) + NORM_EPSILON)
    unit = e * inverse
    lowered = unit.astype(BF16)
    every = lax.all_gather(lowered, AXES, axis=0, tiled=True)
    every_label = lax.all_gather(labels, AXES, axis=0, tiled=True)
    scores = dot(lowered, every, NT) / SOFTMAX_TEMP
    anchor = links.me * f.views + jnp.arange(f.views, dtype=jnp.int32)
    itself = anchor[:, None] == jnp.arange(number, dtype=jnp.int32)[None, :]
    paired = (labels[:, None] == every_label[None, :]) & jnp.logical_not(itself)
    masked = jnp.where(itself, MASKED, scores)
    top = jnp.max(masked, 1)
    log_total = top + jnp.log(jnp.sum(jnp.where(itself, 0.0, jnp.exp(masked - top[:, None])), 1))
    positive = jnp.sum(jnp.where(paired, scores, 0.0), 1)
    loss = lax.psum(jnp.sum(log_total - positive / POSITIVES), AXES) / number
    every_log = lax.all_gather(log_total, AXES, axis=0, tiled=True)

    def pair_grad(logs):
        chance = jnp.where(itself, 0.0, jnp.exp(scores - logs))
        return ((chance - paired.astype(F32) / POSITIVES) / number).astype(BF16)

    unit_grad = (
        dot(pair_grad(log_total[:, None]), every) + dot(pair_grad(every_log[None, :]), every)
    ) / SOFTMAX_TEMP
    along = jnp.sum(unit * unit_grad, 1, keepdims=True)
    grad = (inverse * (unit_grad - unit * along)).astype(BF16)
    d = dot(grad, embed, NT) * slope(v)
    shift_grad = lax.psum(jnp.sum(d, 0), AXES)
    gain_grad = lax.psum(jnp.sum(d * hat, 0), AXES)
    back = (affine[0] * factor * (d - shift_grad / number - hat * (gain_grad / number))).astype(BF16)
    return loss, dot(pooled, back, TN), dot(low, grad, TN), gain_grad, shift_grad, dot(back, hidden, NT)


def per_device(
    x_large, x_small, large_image, small_image,
    first_reduce, first_spatial, first_expand, first_short,
    second_reduce, second_spatial, second_expand, head_hidden, head_embed,
    norm_gain, norm_shift,
):
    f = Frames(x_large, x_small)
    links = Links()
    mid, wide, proj = first_reduce.shape[1], first_short.shape[1], head_hidden.shape[1]
    widths = [mid, mid, wide, wide, mid, mid, wide, proj]
    starts = np.cumsum([0] + widths)
    both = jnp.stack([norm_gain, norm_shift])
    affine = [both[:, starts[k] : starts[k + 1]] for k in range(8)]
    mask = f.mask()

    def gathered(w, axis=0):
        return lax.all_gather(w, "img", axis=axis, tiled=True)

    w_reduce = gathered(first_reduce)
    w_spatial = gathered(first_spatial, 2).reshape(9, mid, mid)
    w_expand = gathered(first_expand)
    w_short = gathered(first_short)
    w_reduce2 = gathered(second_reduce)
    w_spatial2 = gathered(second_spatial, 2).reshape(9, mid, mid)
    w_expand2 = gathered(second_expand)
    w_hidden = gathered(head_hidden)
    w_embed = gathered(head_embed)

    n_in, n_out = 4 * f.valid, f.valid
    all_in, all_out = n_in * links.size, n_out * links.size

    x = split_cells(f, x_large, x_small)
    reduced, st0 = linear(f, x, w_reduce, mask, 4, 256)
    st0 = links.moments(st0, n_in)
    patch1, turned, st1 = conv(f, 2, all_in, reduced, st0, affine[0], w_spatial.reshape(9 * mid, mid), mask)
    st1 = links.moments(st1, n_out)
    skipped, st3 = linear(f, x, w_short, mask, 1, 512)
    turned_low, expanded, st2 = expand(f, all_out, turned, st1, affine[1], w_expand, mask)
    joint = links.moments(jnp.concatenate([st2, st3], 1), n_out)
    st2, st3 = joint[:, :wide], joint[:, wide:]
    block_low, block_pre, mixing, st4 = mix(
        f, all_out, expanded, skipped, st2, affine[2], st3, affine[3], w_reduce2, mask
    )
    st4 = links.moments(st4, n_out)
    patch2, rotated, st5 = conv(f, 1, all_out, mixing, st4, affine[4], w_spatial2.reshape(9 * mid, mid), mask)
    st5 = links.moments(st5, n_out)
    rotated_low, widened, st6 = expand(f, all_out, rotated, st5, affine[5], w_expand2, mask)
    st6 = links.moments(st6, n_out)
    pooled, slopes, view_sums = pool(f, all_out, widened, block_pre, st6, affine[6], mask)
    pooled = pooled.astype(BF16)
    labels = jnp.concatenate([large_image, small_image], 0)

    shard = head_hidden.shape[0]
    joined = links.size * SLOT <= 512 and shard % 128 == 0
    if joined:
        padded = jnp.concatenate([labels, jnp.full((SLOT - f.views,), -1, jnp.int32)])
        every_label = lax.all_gather(padded, AXES, axis=0, tiled=True)
        every = links.gather(pooled).reshape(links.size * SLOT, wide)
        place = jnp.stack([lax.axis_index("img"), links.me]).astype(jnp.int32)
        loss, hidden_grad, embed_grad, gains7, back, sums6 = head(
            f, links.size, shard, place, every, w_hidden, w_embed, affine[7], every_label, view_sums
        )
        loss = loss[0, 0]
        gain7, shift7 = gains7[0], gains7[1]
    else:
        loss, hidden_part, embed_part, gain7, shift7, back = head_plain(
            f, links, pooled[: f.views], w_hidden, w_embed, affine[7], labels
        )
        back = jnp.pad(back, ((0, SLOT - f.views), (0, 0))) * f.cells()
        sums6 = jnp.stack([jnp.sum(back * view_sums[:SLOT], 0), jnp.sum(back * view_sums[SLOT:], 0)])
    sums6 = links.total(sums6)

    widened_back, d5, sums5 = widen_back(
        f, all_out, widened, slopes, back, st6, affine[6], sums6, w_expand2, rotated, st5, affine[5], mask
    )
    expand2_grad = dot(rotated_low, widened_back, TN).astype(BF16)
    sums5 = links.total(sums5)
    rotated_back, d4, sums4 = conv_back(
        f, 1, all_out, all_out, d5, rotated, st5, affine[5], sums5, w_spatial2, mixing, st4, affine[4], mask
    )
    spatial2_grad = dot(patch2, rotated_back, TN).astype(BF16)
    sums4 = links.total(sums4)
    mixing_back, block_grad, sums23 = mix_back(
        f, all_out, d4, mixing, st4, affine[4], sums4, w_reduce2, back, slopes, block_pre,
        expanded, st2, affine[2], skipped, st3, affine[3], mask,
    )
    reduce2_grad = dot(block_low, mixing_back, TN).astype(BF16)
    sums23 = links.total(sums23)
    expanded_back, skipped_back, d1, sums1 = block_back(
        f, all_out, block_grad, expanded, st2, affine[2], skipped, st3, affine[3], sums23, w_expand,
        turned, st1, affine[1], mask,
    )
    expand_grad = dot(turned_low, expanded_back, TN).astype(BF16)
    short_grad = dot(x[: f.rows], skipped_back, TN).astype(BF16)
    sub = dot(skipped_back, w_short, NT)
    sums1 = links.total(sums1)
    turned_back, d0, sums0 = conv_back(
        f, 2, all_out, all_in, d1, turned, st1, affine[1], sums1, w_spatial, reduced, st0, affine[0], mask
    )
    spatial_grad = dot(patch1, turned_back, TN).astype(BF16)
    sums0 = links.total(sums0)
    reduced_back, grad_large, grad_small = input_back(
        f, all_in, d0, reduced, st0, affine[0], sums0, w_reduce, sub, mask
    )
    reduce_grad = dot(x, reduced_back, TN).astype(BF16)

    def scattered(g, axis=0):
        g = lax.psum_scatter(g, "img", scatter_dimension=axis, tiled=True)
        return lax.psum(g, "blk").astype(F32)

    expand2_grad = scattered(expand2_grad)
    spatial2_grad = scattered(spatial2_grad.reshape(3, 3, mid, mid), 2)
    reduce2_grad = scattered(reduce2_grad)
    expand_grad = scattered(expand_grad)
    short_grad = scattered(short_grad)
    spatial_grad = scattered(spatial_grad.reshape(3, 3, mid, mid), 2)
    reduce_grad = scattered(reduce_grad)
    if not joined:
        hidden_grad = scattered(hidden_part.astype(BF16))
        embed_grad = scattered(embed_part.astype(BF16))

    gain_grads = jnp.concatenate(
        [sums0[1], sums1[1], sums23[1], sums23[2], sums4[1], sums5[1], sums6[1], gain7]
    )
    shift_grads = jnp.concatenate(
        [sums0[0], sums1[0], sums23[0], sums23[0], sums4[0], sums5[0], sums6[0], shift7]
    )
    return (
        loss, grad_large, grad_small, reduce_grad, spatial_grad, expand_grad, short_grad,
        reduce2_grad, spatial2_grad, expand2_grad, hidden_grad, embed_grad, gain_grads, shift_grads,
    )


def solution(mesh):
    image = P(("img", "blk"), None, None, None)
    label = P(("img", "blk"))
    matrix = P("img", None)
    kernel = P(None, None, "img", None)
    weights = (matrix, kernel, matrix, matrix, matrix, kernel, matrix, matrix, matrix)
    return jax.shard_map(
        per_device,
        mesh=mesh,
        in_specs=(image, image, label, label) + weights + (P(), P()),
        out_specs=(P(), image, image) + weights + (P(), P()),
        check_vma=False,
    )
```

time: 3000 us -> 1420 us (0.47)
  blocking collectives: 1020 us -> 76.8 us
  local copies, waits for them, and re-layouts: 634 us -> 16.2 us
  Pallas kernels: 0 us -> 127 us
  starting transfers between devices: 0.72 us -> 92.8 us
  matrix products: 113 us -> 36.6 us
  other arithmetic: 105 us -> 28.8 us
  waiting for transfers between devices: 1090 us -> 1020 us
    psum x21 -> x0, blocking collectives: 859 us -> none  [the longest x7 290 us: norm_forward(): center = lax.psum(jnp.sum(values, 0), ('img', 'blk')) / number]
    reduce_scatter x9 -> x7, waiting for transfers between devices: 1030 us -> 523 us  [scattered(): g = lax.psum_scatter(g, 'img', scatter_dimension=axis, tiled=True)]
    slice x94 -> x8, local copies, waits for them, and re-layouts: 336 us -> 1.41 us  [the longest x1 1.34 us: per_device(): loss = loss[0, 0]]
    all_gather x8, waiting for transfers between devices: 0.11 us -> 293 us  [gathered(): return lax.all_gather(w, 'img', axis=axis, tiled=True)]
    ppermute x0 -> x89, waiting for transfers between devices: none -> 138 us  [swap(): return lax.ppermute(v, AXES, [(i, i ^ bits) for i in range(self.size)])]
    pallas_call x0 -> x16, Pallas kernels: none -> 127 us  [the longest x15 105 us: call(): pl.pallas_call(kernel, grid=grid, in_specs=[pl.BlockSpec(b, m) for _, b,...]
    pad x10 -> x0, local copies, waits for them, and re-layouts: 111 us -> none  [the longest x6 82.4 us: fold_patches(): lax.pad(patches[:, :, :, kernel_tap], jnp.float32(0.0), ((0, 0, 0), (row_...]
    ppermute x0 -> x89, starting transfers between devices: none -> 91.5 us  [swap(): return lax.ppermute(v, AXES, [(i, i ^ bits) for i in range(self.size)])]
  transfers between devices with their start and end apart: 18 -> 105, of which waited for: 9 -> 77; matrix products, arithmetic and copies ran while one was open for 13% -> 4% of each run, Pallas kernels for 0% -> 4%
where the time goes in v1:
time: 1420 us
  waiting for transfers between devices  1020 us (72%)
  Pallas kernels  127 us (9%)
  starting transfers between devices  92.8 us (7%)
  blocking collectives  76.8 us (5%)
  matrix products  36.6 us (3%)
  other arithmetic  28.8 us (2%)
  local copies, waits for them, and re-layouts  16.2 us (1%)
  between operations  15.3 us (1%)
    reduce_scatter x7, waiting for transfers between devices, scattered(): g = lax.psum_scatter(g, 'img', scatter_dimension=axis, tiled=True)  523 us
    all_gather x8, waiting for transfers between devices, gathered(): return lax.all_gather(w, 'img', axis=axis, tiled=True)  293 us
    ppermute x89, waiting for transfers between devices, swap(): return lax.ppermute(v, AXES, [(i, i ^ bits) for i in range(self.size)])  138 us
    pallas_call x15, Pallas kernels, call(): pl.pallas_call(kernel, grid=grid, in_specs=[pl.BlockSpec(b, m) for _, b,...  105 us
    ppermute x89, starting transfers between devices, swap(): return lax.ppermute(v, AXES, [(i, i ^ bits) for i in range(self.size)])  91.5 us
    psum x1, waiting for transfers between devices, scattered(): return lax.psum(g, 'blk').astype(F32)  63.3 us
    unnamed x1, blocking collectives  42.4 us
    dot_general x8, matrix products, dot(): return lax.dot_general(left, right, dims, preferred_element_type=F32)  36.6 us
  transfers between devices with their start and end apart: 105, of which 77 were waited for; matrix products, arithmetic and copies ran while one was open for 4% of the time, Pallas kernels for 4%

profile of v1, /device:TPU:0, one launch (start us, length us, event | category | flops | bytes accessed | tf_op | source)
XLA Modules:
  0.0 1415.7 jit_solution(15839732849347179240)
XLA Ops:
  14.9 4.9 shard_map.272.x_ref
  19.8 33.2 %all-gather.9.cloned.1.call-done.w_ref = bf16[1024,512]{1,0:T(8,128)(2,1)} async-done(((bf16[128,512]{1,0:T(8,128)(2,1)}), bf16[1024,512]{1,0:T(8,128)(2,1)}) %all-gather.9.cloned.1.call-update) | async-done | bytes 1048592 | tf_op jit(solution)/shard_map/all_gather | solution.py:930
  53.0 5.7 shard_map.273
  76.9 57.3 %all-gather.11.cloned.1.call-done = bf16[3,3,512,512]{3,2,1,0:T(8,128)(2,1)} async-done(((bf16[3,3,64,512]{3,2,1,0:T(8,128)(2,1)}), bf16[3,3,512,512]{3,2,1,0:T(8,128)(2,1)}) %all-gather.11.cloned.1.call-update) | async-done | bytes 4718608 | tf_op jit(solution)/shard_map/all_gather | solution.py:930
  134.2 7.8 shard_map.274
  155.8 52.4 %all-gather.15.cloned.1.call-done.w_ref = bf16[1024,2048]{1,0:T(8,128)(2,1)} async-done(((bf16[128,2048]{1,0:T(8,128)(2,1)}), bf16[1024,2048]{1,0:T(8,128)(2,1)}) %all-gather.15.cloned.1.call-update) | async-done | bytes 4194320 | tf_op jit(solution)/shard_map/all_gather | solution.py:930
  208.2 6.0 shard_map.276
  214.8 43.0 %all-gather.13.cloned.1.call-done.w_ref = bf16[512,2048]{1,0:T(8,128)(2,1)} async-done(((bf16[64,2048]{1,0:T(8,128)(2,1)}), bf16[512,2048]{1,0:T(8,128)(2,1)}) %all-gather.13.cloned.1.call-update) | async-done | bytes 2097168 | tf_op jit(solution)/shard_map/all_gather | solution.py:930
  257.7 5.3 shard_map.275
  278.2 3.8 collective-permute-done.19
  283.2 26.4 %all-gather.17.cloned.1.call-done.w_ref = bf16[2048,512]{1,0:T(8,128)(2,1)} async-done(((bf16[256,512]{1,0:T(8,128)(2,1)}), bf16[2048,512]{1,0:T(8,128)(2,1)}) %all-gather.17.cloned.1.call-update) | async-done | bytes 2097168 | tf_op jit(solution)/shard_map/all_gather | solution.py:930
  309.6 7.8 shard_map.277
  335.4 54.9 %all-gather.19.cloned.1.call-done = bf16[3,3,512,512]{3,2,1,0:T(8,128)(2,1)} async-done(((bf16[3,3,64,512]{3,2,1,0:T(8,128)(2,1)}), bf16[3,3,512,512]{3,2,1,0:T(8,128)(2,1)}) %all-gather.19.cloned.1.call-update) | async-done | bytes 4718608 | tf_op jit(solution)/shard_map/all_gather | solution.py:930
  390.3 6.1 shard_map.278
  413.9 26.2 %all-gather.21.cloned.1.call-done.w_ref = bf16[512,2048]{1,0:T(8,128)(2,1)} async-done(((bf16[64,2048]{1,0:T(8,128)(2,1)}), bf16[512,2048]{1,0:T(8,128)(2,1)}) %all-gather.21.cloned.1.call-update) | async-done | bytes 2097168 | tf_op jit(solution)/shard_map/all_gather | solution.py:930
  440.1 5.3 shard_map.279
  464.3 6.7 shard_map.280
  473.5 8.0 collective-permute-done.42
  482.6 8.7 collective-permute-done.43
  492.9 7.7 collective-permute-done.44
  502.3 9.6 collective-permute-done.45
  512.4 42.4 %all-reduce = s32[512]{0:T(512)S(1)} all-reduce(s32[512]{0:T(512)S(1)} %add_dynamic-update-slice_fusion), channel_id=1, replica_groups=mesh['img'=8,'blk'=4] {'img','blk'}, use_global_device_ids=true, to_apply=%add | all-reduce | flops 512 | bytes 4096
  555.4 34.4 %all_gather.38.e_ref = bf16[2048,128]{1,0:T(8,128)(2,1)} all-gather(bf16[256,128]{1,0:T(8,128)(2,1)S(1)} %copy-done.16), channel_id=1, replica_groups=mesh['img'=8,'blk'=4] {'img'}, dimensions={0}, use_global_device_ids=true | all-gather | bytes 589824 | tf_op jit(solution)/shard_map/all_gather | solution.py:930
  593.0 22.1 %shard_map.281 = (f32[8,128]{1,0:T(8,128)}, f32[256,2048]{1,0:T(8,128)}, f32[256,128]{1,0:T(8,128)}, f32[2,2048]{1,0:T(2,128)}, f32[16,2048]{1,0:T(8,128)}, /*index=5*/f32[2,2048]{1,0:T(2,128)}) custom-call(s32[2]{0:T(128)} %pad_add_fusion.place_ref, bf16[512,2048]{1,0:T(8,128)(2,1)} %bitcast.68, bf16[2048,2048]{1,0:T(8,128)(2,1)} %all-gather.23.cloned.1.call-done.h_ref, ...), custom_call_target="tpu_custom_call" | custom-call | flops 8589934592 | bytes 20971520 | tf_op jit(solution)/shard_map/pallas_call | solution.py:529
  621.8 3.7 collective-permute-done.50
  632.9 7.4 shard_map.282
  654.0 3.8 collective-permute-done.60
  658.4 6.6 shard_map.283
  681.3 9.9 shard_map.284
  706.4 3.8 collective-permute-done.74
  710.9 8.7 shard_map.285
  735.6 7.8 shard_map.286
  761.8 8.4 shard_map.287
  770.2 4.2 convolution_convert_fusion.6
  774.5 4.0 convolution_convert_fusion.3
  779.5 4.0 convolution_convert_fusion.4
  784.6 4.0 convolution_convert_fusion.5
  788.6 5.8 convolution_convert_fusion.2
  795.4 6.3 convolution_convert_fusion
  803.7 5.3 convolution_convert_fusion.1
  814.3 22.0 %reduce-scatter.8.cloned.1.call-done = bf16[128,512]{1,0:T(8,128)(2,1)} async-done(((bf16[1024,512]{1,0:T(8,128)(2,1)}), bf16[128,512]{1,0:T(8,128)(2,1)}) %reduce-scatter.8.cloned.1.call-update) | async-done | bytes 131088 | tf_op jit(solution)/shard_map/reduce_scatter | solution.py:1021
  836.3 70.7 %reduce-scatter.20.cloned.1.call-done = bf16[64,2048]{1,0:T(8,128)(2,1)} async-done(((bf16[512,2048]{1,0:T(8,128)(2,1)}), bf16[64,2048]{1,0:T(8,128)(2,1)}) %reduce-scatter.20.cloned.1.call-update) | async-done | bytes 262160 | tf_op jit(solution)/shard_map/reduce_scatter | solution.py:1021
  907.0 70.8 %reduce-scatter.16.cloned.1.call-done = bf16[256,512]{1,0:T(8,128)(2,1)} async-done(((bf16[2048,512]{1,0:T(8,128)(2,1)}), bf16[256,512]{1,0:T(8,128)(2,1)}) %reduce-scatter.16.cloned.1.call-update) | async-done | bytes 262160 | tf_op jit(solution)/shard_map/reduce_scatter | solution.py:1021
  977.8 70.6 %reduce-scatter.12.cloned.1.call-done = bf16[64,2048]{1,0:T(8,128)(2,1)} async-done(((bf16[512,2048]{1,0:T(8,128)(2,1)}), bf16[64,2048]{1,0:T(8,128)(2,1)}) %reduce-scatter.12.cloned.1.call-update) | async-done | bytes 262160 | tf_op jit(solution)/shard_map/reduce_scatter | solution.py:1021
  1048.4 91.2 %reduce-scatter.14.cloned.1.call-done = bf16[128,2048]{1,0:T(8,128)(2,1)} async-done(((bf16[1024,2048]{1,0:T(8,128)(2,1)}), bf16[128,2048]{1,0:T(8,128)(2,1)}) %reduce-scatter.14.cloned.1.call-update) | async-done | bytes 524304 | tf_op jit(solution)/shard_map/reduce_scatter | solution.py:1021
  1139.5 98.9 %reduce-scatter.18.cloned.1.call-done = bf16[3,3,64,512]{3,2,1,0:T(8,128)(2,1)} async-done(((bf16[3,3,512,512]{3,2,1,0:T(8,128)(2,1)}), bf16[3,3,64,512]{3,2,1,0:T(8,128)(2,1)}) %reduce-scatter.18.cloned.1.call-update) | async-done | bytes 589840 | tf_op jit(solution)/shard_map/reduce_scatter | solution.py:1021
  1238.5 98.9 %reduce-scatter.10.cloned.1.call-done = bf16[3,3,64,512]{3,2,1,0:T(8,128)(2,1)} async-done(((bf16[3,3,512,512]{3,2,1,0:T(8,128)(2,1)}), bf16[3,3,64,512]{3,2,1,0:T(8,128)(2,1)}) %reduce-scatter.10.cloned.1.call-update) | async-done | bytes 589840 | tf_op jit(solution)/shard_map/reduce_scatter | solution.py:1021
  1337.6 63.3 %all-reduce.4.cloned.1.call-done = (bf16[128,512]{1,0:T(8,128)(2,1)}, bf16[3,3,64,512]{3,2,1,0:T(8,128)(2,1)}, bf16[64,2048]{1,0:T(8,128)(2,1)}, bf16[128,2048]{...) async-done(((bf16[128,512]{1,0:T(8,128)(2,1)}, bf16[3,3,64,512]{3,2,1,0:T(8,128)(2,1)}, ...) | async-done | bytes 2621456 | tf_op jit(solution)/shard_map/psum | solution.py:1022
  (382 shorter events, 234.4 us)
Async XLA Ops:
  7.2 45.8 %all-gather.9.cloned.1.call-start = ((), (), s32[]{:S(2)}) async-start(), calls=%async_computation.7 | async-start | bytes 1179648 | tf_op jit(solution)/shard_map/all_gather | solution.py:930
  7.9 126.2 %all-gather.11.cloned.1.call-start = ((), (), s32[]{:S(2)}) async-start(), calls=%async_computation.8 | async-start | bytes 5308416 | tf_op jit(solution)/shard_map/all_gather | solution.py:930
  8.7 199.5 %all-gather.15.cloned.1.call-start = ((), (), s32[]{:S(2)}) async-start(), calls=%async_computation.10 | async-start | bytes 4718592 | tf_op jit(solution)/shard_map/all_gather | solution.py:930
  9.4 248.3 %all-gather.13.cloned.1.call-start = ((), (), s32[]{:S(2)}) async-start(), calls=%async_computation.9 | async-start | bytes 2359296 | tf_op jit(solution)/shard_map/all_gather | solution.py:930
  10.0 299.6 %all-gather.17.cloned.1.call-start = ((), (), s32[]{:S(2)}) async-start(), calls=%async_computation.11 | async-start | bytes 2359296 | tf_op jit(solution)/shard_map/all_gather | solution.py:930
  10.6 379.7 %all-gather.19.cloned.1.call-start = ((), (), s32[]{:S(2)}) async-start(), calls=%async_computation.12 | async-start | bytes 5308416 | tf_op jit(solution)/shard_map/all_gather | solution.py:930
  11.2 429.0 %all-gather.21.cloned.1.call-start = ((), (), s32[]{:S(2)}) async-start(), calls=%async_computation.13 | async-start | bytes 2359296 | tf_op jit(solution)/shard_map/all_gather | solution.py:930
  11.9 579.7 %all-gather.23.cloned.1.call-start = ((), (), s32[]{:S(2)}) async-start(), calls=%async_computation.14 | async-start | bytes 9437184 | tf_op jit(solution)/shard_map/all_gather | solution.py:930
  68.1 5.1 collective-permute-start.4
  68.7 4.6 collective-permute-start.5
  70.8 5.5 collective-permute-start.6
  148.3 688.0 %reduce-scatter.8.cloned.1.call-start = ((), (), s32[]{:S(2)}) async-start(), calls=%async_computation.15 | async-start | bytes 1179648 | tf_op jit(solution)/shard_map/reduce_scatter | solution.py:1021
  151.3 62.8 %collective-permute-start.11 = (f32[2,512]{1,0:T(2,128)S(1)}, f32[2,512]{1,0:T(2,128)S(1)}, u32[]{:S(2)}, u32[]{:S(2)}) collective-permute-start(f32[2,512]{1,0:T(2,128)S(1)} %pad_maximum_fusion.18), channel_id=1, source_target_pairs={{0,8},{1,9},{2,10},{3,11},{4,12},{5,13},{6,14},{7,15},{8,0},{9,1},... | collective-permute-start | bytes 12296 | tf_op jit(solution)/shard_map/ppermute | solution.py:807
  152.0 62.2 %collective-permute-start.12 = (f32[2,512]{1,0:T(2,128)S(1)}, f32[2,512]{1,0:T(2,128)S(1)}, u32[]{:S(2)}, u32[]{:S(2)}) collective-permute-start(f32[2,512]{1,0:T(2,128)S(1)} %pad_maximum_fusion.18), channel_id=1, source_target_pairs={{0,16},{1,17},{2,18},{3,19},{4,20},{5,21},{6,22},{7,23},{8,24},{9,... | collective-permute-start | bytes 12296 | tf_op jit(solution)/shard_map/ppermute | solution.py:807
  153.4 60.7 %collective-permute-start.13 = (f32[2,512]{1,0:T(2,128)S(1)}, f32[2,512]{1,0:T(2,128)S(1)}, u32[]{:S(2)}, u32[]{:S(2)}) collective-permute-start(f32[2,512]{1,0:T(2,128)S(1)} %pad_maximum_fusion.18), channel_id=1, source_target_pairs={{0,24},{1,25},{2,26},{3,27},{4,28},{5,29},{6,30},{7,31},{8,16},{9,... | collective-permute-start | bytes 12296 | tf_op jit(solution)/shard_map/ppermute | solution.py:807
  273.0 5.2 collective-permute-start.18
  274.6 7.4 collective-permute-start.19
  276.1 6.3 collective-permute-start.20
  328.4 5.1 collective-permute-start.26
  329.3 5.5 collective-permute-start.27
  406.3 4.6 collective-permute-start.33
  407.8 5.4 collective-permute-start.34
  455.4 5.3 collective-permute-start.39
  457.0 5.9 collective-permute-start.40
  457.7 5.9 collective-permute-start.41
  471.9 9.7 collective-permute-start.42
  482.5 8.8 collective-permute-start.43
  491.4 9.3 collective-permute-start.44
  500.8 11.1 collective-permute-start.45
  512.1 77.7 %collective-permute-start.46 = (bf16[2,2,2,2,16,2048]{5,4,0,1,2,3:T(8,128)(2,1)S(1)}, bf16[2,2,2,2,16,2048]{5,4,0,1,2,3:T(8,128)(2,1)S(1)}, u32[]{:S(2)}, u32[]{:S(2)}) collective-permute-start(bf16[2,2,2,2,16,2048]{5,4,0,1,2,3:T(8,128)(2,1)S(1)} %pad_maximum_fusion.1), channel_id=1, source_target_pairs={{0,1},{1,0},{2,3},{3,2},{4,5},{5,4},{6,7},{7,6},{8,9},{9,8},{10,11... | collective-permute-start | bytes 3145736 | tf_op jit(solution)/shard_map/ppermute | solution.py:807
  625.6 4.7 collective-permute-start.52
  626.8 5.5 collective-permute-start.53
  649.0 5.0 collective-permute-start.59
  652.4 5.4 collective-permute-start.60
  675.3 5.4 collective-permute-start.67
  700.8 5.6 collective-permute-start.73
  704.5 5.7 collective-permute-start.74
  729.6 5.4 collective-permute-start.81
  752.0 7.4 collective-permute-start.86
  752.0 7.4 collective-permute-start.87
  755.8 5.4 collective-permute-start.88
  774.5 132.5 %reduce-scatter.20.cloned.1.call-start = ((), (), s32[]{:S(2)}) async-start(), calls=%async_computation.21 | async-start | bytes 2359296 | tf_op jit(solution)/shard_map/reduce_scatter | solution.py:1021
  778.6 199.2 %reduce-scatter.16.cloned.1.call-start = ((), (), s32[]{:S(2)}) async-start(), calls=%async_computation.19 | async-start | bytes 2359296 | tf_op jit(solution)/shard_map/reduce_scatter | solution.py:1021
  783.6 264.8 %reduce-scatter.12.cloned.1.call-start = ((), (), s32[]{:S(2)}) async-start(), calls=%async_computation.17 | async-start | bytes 2359296 | tf_op jit(solution)/shard_map/reduce_scatter | solution.py:1021
  788.6 350.9 %reduce-scatter.14.cloned.1.call-start = ((), (), s32[]{:S(2)}) async-start(), calls=%async_computation.18 | async-start | bytes 4718592 | tf_op jit(solution)/shard_map/reduce_scatter | solution.py:1021
  794.4 444.0 %reduce-scatter.18.cloned.1.call-start = ((), (), s32[]{:S(2)}) async-start(), calls=%async_computation.20 | async-start | bytes 5308416 | tf_op jit(solution)/shard_map/reduce_scatter | solution.py:1021
  801.7 535.7 %reduce-scatter.10.cloned.1.call-start = ((), (), s32[]{:S(2)}) async-start(), calls=%async_computation.16 | async-start | bytes 5308416 | tf_op jit(solution)/shard_map/reduce_scatter | solution.py:1021
  809.1 591.9 %all-reduce.4.cloned.1.call-start = ((), (), s32[]{:S(2)}) async-start(), calls=%async_computation.22 | async-start | bytes 5242880 | tf_op jit(solution)/shard_map/psum | solution.py:1022
  (90 other events, 664.7 us)
Sparse Core Ops, SparseCore 0:
  10.1 42.8 all-gather.8
  55.2 78.9 all-gather.10
  136.3 71.8 all-gather.14
  210.1 47.5 all-gather.12
  259.7 49.8 all-gather.16
  311.6 78.6 all-gather.18
  392.4 47.6 all-gather.20
  442.2 131.3 all-gather.22
  774.6 61.6 reduce-scatter.7
  840.1 66.8 reduce-scatter.19
  910.9 66.8 reduce-scatter.15
  981.6 66.7 reduce-scatter.11
  1052.4 87.0 reduce-scatter.13
  1143.0 95.3 reduce-scatter.17
  1242.0 95.3 reduce-scatter.9
  1340.1 60.7 all-reduce.3

commit v2 on v1

--- a/solution.py
+++ b/solution.py
@@ -29,19 +29,32 @@
     return lax.dot_general(left, right, dims, preferred_element_type=F32)
 
 
-def call(kernel, grid, inputs, outputs, scratch=(), flops=0):
-    moved = sum(a.size * a.dtype.itemsize for a, _, _ in inputs)
-    moved += sum(int(np.prod(s)) * jnp.dtype(d).itemsize for s, d, _, _ in outputs)
+def call(kernel, grid, inputs, outputs, scratch=(), us=6, after=()):
     return pl.pallas_call(
-        kernel,
+        skipping(kernel, len(inputs), len(after)),
+        name=kernel.func.__name__,
         grid=grid,
-        in_specs=[pl.BlockSpec(b, m) for _, b, m in inputs],
+        in_specs=[pl.BlockSpec(b, m) for _, b, m in inputs] + [IN_PLACE] * len(after),
         out_specs=[pl.BlockSpec(b, m) for _, _, b, m in outputs],
         out_shape=[jax.ShapeDtypeStruct(s, d) for s, d, _, _ in outputs],
         scratch_shapes=list(scratch),
         compiler_params=pltpu.CompilerParams(vmem_limit_bytes=VMEM_LIMIT),
-        cost_estimate=pl.CostEstimate(flops=flops, bytes_accessed=moved, transcendentals=0),
-    )(*[a for a, _, _ in inputs])
+        cost_estimate=cost(us),
+    )(*[a for a, _, _ in inputs], *after)
+
+
+def cost(us):
+    return pl.CostEstimate(flops=0, bytes_accessed=int(us * 3.5e6), transcendentals=0)
+
+
+IN_PLACE = pl.BlockSpec(memory_space=pl.ANY)
+IN_SMEM = pl.BlockSpec(memory_space=pltpu.SMEM)
+
+
+def skipping(kernel, used, unused):
+    if not unused:
+        return kernel
+    return lambda *refs: kernel(*refs[:used], *refs[used + unused :])
 
 
 def whole(a):
@@ -193,7 +206,7 @@
     ]
 
 
-def split_cells(f, large, small, width=256):
+def split_cells(f, large, small, width=256, after=()):
     c = large.shape[3]
     return call(
         functools.partial(split_kernel, f),
@@ -201,6 +214,8 @@
         [cols(large, width), cols(small, width)],
         [out_cols((4 * f.rows, c), BF16, width)],
         parity_scratch(f, width),
+        us=5,
+        after=after,
     )[0]
 
 
@@ -215,7 +230,7 @@
     store_stats(stats_ref, blocks, mask, count)
 
 
-def linear(f, x, w, mask, phases, width):
+def linear(f, x, w, mask, phases, width, after=()):
     n = w.shape[1]
     x_in = (x, (phases * f.rows, x.shape[1]), lambda i: (0, 0))
     return call(
@@ -223,7 +238,8 @@
         (n // width,),
         [x_in, cols(w, width), whole(mask)],
         [out_cols((phases * f.rows, n), F32, width), out_cols((2, n), F32, width)],
-        flops=2 * phases * f.rows * w.size,
+        us=6,
+        after=after,
     )
 
 
@@ -259,7 +275,7 @@
     store_stats(new_ref, [out_ref], spread(mask_ref[...], out_ref.shape[1]), f.valid)
 
 
-def conv(f, stride, count, pre, stats, affine, w, mask, tile=256):
+def conv(f, stride, count, pre, stats, affine, w, mask, tile=256, after=()):
     c, n = pre.shape[1], w.shape[1]
     phases = stride * stride
     return call(
@@ -272,7 +288,8 @@
             out_cols((2, n), F32, tile),
         ],
         [pltpu.VMEM((phases, f.rows + 2 * GUARD, c), F32)],
-        flops=2 * f.rows * w.size,
+        us=8,
+        after=after,
     )
 
 
@@ -287,7 +304,7 @@
     store_stats(new_ref, [out_ref], spread(mask_ref[...], out_ref.shape[1]), f.valid)
 
 
-def expand(f, count, pre, stats, affine, w, mask, tile=512):
+def expand(f, count, pre, stats, affine, w, mask, tile=512, after=()):
     c, n = w.shape
     return call(
         functools.partial(expand_kernel, f, count),
@@ -298,7 +315,8 @@
             out_cols((f.rows, n), F32, tile),
             out_cols((2, n), F32, tile),
         ],
-        flops=2 * f.rows * w.size,
+        us=5.3,
+        after=after,
     )
 
 
@@ -329,7 +347,7 @@
         store_stats(new_ref, [out_ref], spread(mask_ref[...], out_ref.shape[1]), f.valid)
 
 
-def mix(f, count, expanded, skipped, stats_a, affine_a, stats_b, affine_b, w, mask, tile=512):
+def mix(f, count, expanded, skipped, stats_a, affine_a, stats_b, affine_b, w, mask, tile=512, after=()):
     k, n = w.shape
     return call(
         functools.partial(mix_kernel, f, count),
@@ -342,7 +360,8 @@
             out_whole((f.rows, n), F32),
             out_whole((2, n), F32),
         ],
-        flops=2 * f.rows * w.size,
+        us=8,
+        after=after,
     )
 
 
@@ -370,7 +389,7 @@
     put(view_ref, SLOT, f.per_view(d * hat))
 
 
-def pool(f, count, wide, pre, stats, affine, mask, tile=512):
+def pool(f, count, wide, pre, stats, affine, mask, tile=512, after=()):
     n = wide.shape[1]
     return call(
         functools.partial(pool_kernel, f, count),
@@ -381,13 +400,13 @@
             out_cols((f.rows, n), F32, tile),
             out_cols((2 * SLOT, n), F32, tile),
         ],
-        flops=20 * wide.size,
+        us=6.7,
+        after=after,
     )
 
 
 def head_kernel(
-    f, devices, shard, place_ref, p_ref, h_ref, e_ref, affine_ref, label_col, label_row,
-    view_ref, cells_ref,
+    f, devices, shard, place_ref, p_ref, digit_ref, h_ref, e_ref, affine_ref, view_ref, cells_ref,
     loss_ref, hidden_ref, embed_ref, gain_ref, back_ref, sums_ref,
     hat, low, emb, grad, own, factors, pooled_grad,
 ):
@@ -435,7 +454,9 @@
         i_ok = i % SLOT < f.views
         j_ok = j % SLOT < f.views
         use = (i != j) & i_ok & j_ok
-        paired = use & (label_col[:, 0:1] == label_row[0:1, :])
+        digits = digit_ref[...].astype(F32)
+        across = digits.T
+        paired = use & (digits[:, 0:1] * 256.0 + digits[:, 1:2] == across[0:1, :] * 256.0 + across[1:2, :])
         weight = paired.astype(F32) / POSITIVES
         masked = jnp.where(use, scores, MASKED)
 
@@ -477,7 +498,7 @@
         own[...] = lowered
         mine = pl.multiple_of(place_ref[0] * shard, 128)
         hidden_ref[...] = dot(p_ref[:, pl.ds(mine, shard)], lowered, TN)
-        here = pl.multiple_of(place_ref[1] * SLOT, SLOT)
+        here = pl.multiple_of(place_ref[2] * SLOT, SLOT)
         part = dot(own[pl.ds(here, SLOT), :], h_ref[...], NT)
 
         @pl.when(now == 0)
@@ -500,21 +521,18 @@
         sums_ref[1:2, :] = column_sum(b * view_ref[SLOT:, :])
 
 
-def head(f, devices, shard, place, pooled, hidden, embed, affine, labels, view_sums, tile=512):
-    v, c = pooled.shape
-    n, w = embed.shape
+def head(f, devices, shard, place, pooled, weight, affine, view_sums, tile=512):
+    v, c = pooled.shape[0], weight.shape[0]
+    n, w = affine.shape[1], weight.shape[1] - affine.shape[1]
     tiles = n // tile
-    label_col = jnp.broadcast_to(labels[:, None], (v, 128))
-    label_row = jnp.broadcast_to(labels[None, :], (8, v))
     cells = jnp.asarray(np.repeat(f.cells(), c, 1))
     late = lambda i: (0, jnp.maximum(i - tiles, 0))
     inputs = [
-        whole(pooled),
-        (hidden, (c, tile), lambda i: (0, i % tiles)),
-        (embed, (tile, w), lambda i: (i % tiles, 0)),
+        (pooled, (v, c), lambda i: (0, 0)),
+        (pooled, (v, 128), lambda i: (0, c // 128)),
+        (weight, (c, tile), lambda i: (0, i % tiles)),
+        (weight, (tile, w), lambda i: (i % tiles, n // w)),
         (affine, (2, tile), lambda i: (0, i % tiles)),
-        whole(label_col),
-        whole(label_row),
         whole(view_sums),
         whole(cells),
     ]
@@ -528,6 +546,7 @@
     ]
     return pl.pallas_call(
         functools.partial(head_kernel, f, devices, shard),
+        name="head",
         grid=(2 * tiles,),
         in_specs=[pl.BlockSpec(memory_space=pltpu.SMEM)] + [pl.BlockSpec(b, m) for _, b, m in inputs],
         out_specs=[pl.BlockSpec(b, m) for _, _, b, m in outputs],
@@ -542,9 +561,7 @@
             pltpu.VMEM((SLOT, c), F32),
         ],
         compiler_params=pltpu.CompilerParams(vmem_limit_bytes=VMEM_LIMIT),
-        cost_estimate=pl.CostEstimate(
-            flops=4 * v * c * n, bytes_accessed=20 * 1024 * 1024, transcendentals=0
-        ),
+        cost_estimate=cost(22),
     )(place, *[a for a, _, _ in inputs])
 
 
@@ -581,7 +598,7 @@
         new_ref[1:2, :] = column_sum(d * hat)
 
 
-def widen_back(f, count, wide, slopes, back, stats, affine, sums, w, turn, tstats, taffine, mask, tile=512):
+def widen_back(f, count, wide, slopes, back, stats, affine, sums, w, turn, tstats, taffine, mask, tile=512, after=()):
     c, n = w.shape
     return call(
         functools.partial(widen_back_kernel, f, count),
@@ -593,7 +610,8 @@
             out_whole((f.rows, c), F32),
             out_whole((2, c), F32),
         ],
-        flops=2 * f.rows * w.size,
+        us=7.4,
+        after=after,
     )
 
 
@@ -643,7 +661,7 @@
     new_ref[1:2, :] = total_hat
 
 
-def conv_back(f, stride, count, in_count, d, pre, stats, affine, sums, w, inside, istats, iaffine, mask, tile=256):
+def conv_back(f, stride, count, in_count, d, pre, stats, affine, sums, w, inside, istats, iaffine, mask, tile=256, after=()):
     n = d.shape[1]
     c = w.shape[1]
     phases = stride * stride
@@ -663,7 +681,8 @@
             pltpu.VMEM((f.rows + 2 * GUARD, n), F32),
             pltpu.VMEM((4 if stride == 2 else 9, f.rows, n), BF16),
         ],
-        flops=2 * f.rows * w.size,
+        us=7.2,
+        after=after,
     )
 
 
@@ -691,8 +710,7 @@
 
 def mix_back(
     f, count, d, mixing, stats, affine, sums, w, back, slopes, pre,
-    expanded, estats, eaffine, skipped, sstats, saffine, mask, tile=512,
-):
+    expanded, estats, eaffine, skipped, sstats, saffine, mask, tile=512, after=()):
     n, c = w.shape
     return call(
         functools.partial(mix_back_kernel, f, count),
@@ -706,7 +724,8 @@
             out_cols((f.rows, n), F32, tile),
             out_cols((3, n), F32, tile),
         ],
-        flops=2 * f.rows * w.size,
+        us=9.8,
+        after=after,
     )
 
 
@@ -732,8 +751,7 @@
 
 def block_back(
     f, count, g, expanded, estats, eaffine, skipped, sstats, saffine, sums, w,
-    turned, tstats, taffine, mask, tile=512,
-):
+    turned, tstats, taffine, mask, tile=512, after=()):
     c, n = w.shape
     return call(
         functools.partial(block_back_kernel, f, count),
@@ -746,7 +764,8 @@
             out_whole((f.rows, c), F32),
             out_whole((2, c), F32),
         ],
-        flops=2 * f.rows * w.size,
+        us=8.8,
+        after=after,
     )
 
 
@@ -778,7 +797,7 @@
         small_ref[:, :, :, lane] = st[k, :, :, 0 : f.small_in, :].astype(BF16)
 
 
-def input_back(f, count, d, pre, stats, affine, sums, w, sub, mask, tile=256):
+def input_back(f, count, d, pre, stats, affine, sums, w, sub, mask, tile=256, after=()):
     n, c = w.shape
     return call(
         functools.partial(input_back_kernel, f, count),
@@ -791,8 +810,230 @@
             out_cols((f.small, f.small_in, f.small_in, n), BF16, tile),
         ],
         parity_scratch(f, tile),
-        flops=8 * f.rows * w.size,
-    )
+        us=8.4,
+        after=after,
+    )
+
+
+def assemble_kernel(axis, rows, place_ref, own_ref, other_ref, out_ref, sems):
+    copies = []
+    for m in range(32):
+        c, j, k = m & 1, (m >> 1) & 3, m >> 3
+        src = (other_ref if c else own_ref).at[j, k]
+        at = pl.ds(pl.multiple_of((place_ref[2] ^ m) * rows, 16), rows)
+        dst = out_ref.at[at, :] if axis == 0 else out_ref.at[:, at, :]
+        copies.append(pltpu.make_async_copy(src, dst, sems.at[m]))
+    for copy in copies:
+        copy.start()
+    for copy in copies:
+        copy.wait()
+
+
+def assemble(place, own, other, after=()):
+    block = own.shape[2:]
+    axis = len(block) - 2
+    shape = block[:axis] + (32 * block[axis],) + block[axis + 1 :]
+    return pl.pallas_call(
+        skipping(functools.partial(assemble_kernel, axis, block[axis]), 3, len(after)),
+        name="assemble",
+        in_specs=[IN_SMEM] + [IN_PLACE] * (2 + len(after)),
+        out_specs=IN_PLACE,
+        out_shape=jax.ShapeDtypeStruct(shape, own.dtype),
+        scratch_shapes=[pltpu.SemaphoreType.DMA((32,))],
+        compiler_params=pltpu.CompilerParams(vmem_limit_bytes=4 * 1024 * 1024),
+        cost_estimate=cost(3.5),
+    )(place, own, other, *after)
+
+
+def join_kernel(at, half, split, folds, place_ref, own_ref, other_ref, out_ref, sems):
+    copies = []
+    pieces = split * folds
+    rows = half // pieces
+    for m in range(16 * pieces):
+        piece, c, k = m % pieces, m // pieces % 2, m // (2 * pieces)
+        src = (other_ref if c else own_ref).at[k]
+        row = (2 * k + ((place_ref[1] % 2) ^ c)) * half + piece * rows
+        there = pl.ds(pl.multiple_of(row, 16), rows)
+        fold, part = piece // split, piece % split
+        here = pl.ds(at + part * rows, rows)
+        if folds > 1:
+            width = out_ref.shape[-1]
+            src, dst = src.at[here, pl.ds(fold * width, width)], out_ref.at[there, :]
+        elif len(src.shape) == 2:
+            src, dst = src.at[here, :], out_ref.at[there, :]
+        else:
+            src, dst = src.at[:, here, :], out_ref.at[:, there, :]
+        copies.append(pltpu.make_async_copy(src, dst, sems.at[m]))
+    for copy in copies:
+        copy.start()
+    for copy in copies:
+        copy.wait()
+
+
+def join_halves(place, own, other, at, half, folds):
+    block = own.shape[1:]
+    split = 1 if folds > 1 else 2
+    shape = block[:-2] + (16 * half, block[-1] // folds)
+    return pl.pallas_call(
+        functools.partial(join_kernel, at, half, split, folds),
+        name="join_halves",
+        in_specs=[IN_SMEM, IN_PLACE, IN_PLACE],
+        out_specs=IN_PLACE,
+        out_shape=jax.ShapeDtypeStruct(shape, own.dtype),
+        scratch_shapes=[pltpu.SemaphoreType.DMA((16 * split * folds,))],
+        compiler_params=pltpu.CompilerParams(vmem_limit_bytes=4 * 1024 * 1024),
+        cost_estimate=cost(4),
+    )(place, own, other)
+
+
+def half_kernel(place_ref, *refs):
+    shards, out_ref = refs[:-1], refs[-1]
+    base = 0
+    for shard in shards:
+        half = shard.shape[-2] // 2
+        at = pl.multiple_of(place_ref[1] % 2 * half, 16)
+        if len(shard.shape) == 3:
+            out_ref[...] = shard[:, pl.ds(at, half), :]
+            continue
+        width = shard.shape[1]
+        folds = out_ref.shape[1] // width
+        rows = half // folds
+        for fold in range(folds):
+            value = shard[pl.ds(pl.multiple_of(at + fold * rows, 16), rows), :]
+            out_ref[base : base + rows, fold * width : (fold + 1) * width] = value
+        base += rows
+
+
+def half_of(place, shards, after=()):
+    shape = shards[0].shape
+    if len(shape) == 2:
+        width = max(s.shape[1] for s in shards)
+        shape = (sum(s.size for s in shards) // (2 * width), width)
+    else:
+        shape = (shape[0], shape[1] // 2, shape[2])
+    in_vmem = pl.BlockSpec(memory_space=pltpu.VMEM)
+    return pl.pallas_call(
+        skipping(half_kernel, 1 + len(shards), len(after)),
+        name="half",
+        in_specs=[IN_SMEM] + [in_vmem] * len(shards) + [IN_PLACE] * len(after),
+        out_specs=in_vmem,
+        out_shape=jax.ShapeDtypeStruct(shape, BF16),
+        compiler_params=pltpu.CompilerParams(vmem_limit_bytes=VMEM_LIMIT),
+        cost_estimate=cost(1.5),
+    )(place, *shards, *after)
+
+
+def cut_kernel(number, place_ref, *refs):
+    ins, outs, sems = refs[:number], refs[number : 2 * number], refs[2 * number]
+    copies = []
+    for k in range(number):
+        rows = outs[k].shape[-2]
+        at = pl.ds(pl.multiple_of(place_ref[1] * rows, 16), rows)
+        src = ins[k].at[at, :] if len(ins[k].shape) == 2 else ins[k].at[:, at, :]
+        copies.append(pltpu.make_async_copy(src, outs[k], sems.at[k]))
+    for copy in copies:
+        copy.start()
+    for copy in copies:
+        copy.wait()
+
+
+def cut(place, shards, after=()):
+    shapes = [s.shape[:-2] + (s.shape[-2] // 4, s.shape[-1]) for s in shards]
+    number = len(shards)
+    return pl.pallas_call(
+        skipping(functools.partial(cut_kernel, number), 1 + number, len(after)),
+        name="cut",
+        in_specs=[IN_SMEM] + [IN_PLACE] * (number + len(after)),
+        out_specs=[IN_PLACE] * number,
+        out_shape=[jax.ShapeDtypeStruct(s, BF16) for s in shapes],
+        scratch_shapes=[pltpu.SemaphoreType.DMA((number,))],
+        compiler_params=pltpu.CompilerParams(vmem_limit_bytes=4 * 1024 * 1024),
+        cost_estimate=cost(0.7),
+    )(place, *shards, *after)
+
+
+def local_kernel(function, number, *refs):
+    ins, outs = refs[:number], refs[number:]
+    for out, value in zip(outs, function(*[r[...] for r in ins])):
+        out[...] = value
+
+
+def local(function, arrays, after=(), name="local", us=2):
+    shapes = jax.eval_shape(function, *arrays)
+    in_vmem = pl.BlockSpec(memory_space=pltpu.VMEM)
+    kernel = functools.partial(local_kernel, function, len(arrays))
+    return pl.pallas_call(
+        skipping(kernel, len(arrays), len(after)),
+        name=name,
+        in_specs=[in_vmem] * len(arrays) + [IN_PLACE] * len(after),
+        out_specs=[in_vmem] * len(shapes),
+        out_shape=list(shapes),
+        compiler_params=pltpu.CompilerParams(vmem_limit_bytes=VMEM_LIMIT),
+        cost_estimate=cost(us),
+    )(*arrays, *after)
+
+
+def nothing(*refs):
+    del refs
+
+
+def pin(v, after):
+    if not after:
+        return v
+    return pl.pallas_call(
+        nothing,
+        name="pin",
+        in_specs=[IN_PLACE] * (1 + len(after)),
+        out_specs=IN_PLACE,
+        out_shape=jax.ShapeDtypeStruct(v.shape, v.dtype),
+        input_output_aliases={0: 0},
+        compiler_params=pltpu.CompilerParams(vmem_limit_bytes=4 * 1024 * 1024),
+        cost_estimate=cost(0.5),
+    )(v, *after)
+
+
+def weight_kernel(by_tap, rows, parts, place_ref, left_ref, right_ref, keep_ref, send_ref, acc):
+    acc[...] = dot(left_ref[...], right_ref[...], TN)
+    for m in range(parts):
+        if parts == 32:
+            at, c, place = place_ref[2] ^ m, m & 1, ((m >> 1) & 3, m >> 3)
+            place = place + (0,) if by_tap else place
+        else:
+            at, c, place = (m & ~1) + ((place_ref[1] % 2) ^ (m & 1)), m & 1, (m >> 1,)
+        block = acc[pl.ds(pl.multiple_of(at * rows, 16), rows), :].astype(BF16)
+        (send_ref if c else keep_ref)[place] = block
+
+
+def weight_grad(place, left, right, taps=1, halves=False, tile=512):
+    k, n = left.shape[1] // taps, right.shape[1]
+    parts = 16 if halves else 32
+    rows = k // parts
+    if taps == 1:
+        steps = n // tile
+        left_in = (right.shape[0], k), lambda i: (0, 0)
+        right_in = (right.shape[0], tile), lambda i: (0, i)
+        shape, block = (4, 4, rows, n), (4, 4, rows, tile)
+        out_map = lambda i: (0, 0, 0, i)
+    else:
+        steps, tile = taps, n
+        left_in = (right.shape[0], k), lambda i: (0, i)
+        right_in = right.shape, lambda i: (0, 0)
+        shape, block = (4, 4, taps, rows, n), (4, 4, 1, rows, n)
+        out_map = lambda i: (0, 0, i, 0, 0)
+    if halves:
+        shape, block = (8, steps * rows, tile), (8, rows, tile)
+        out_map = lambda i: (0, i, 0)
+    return pl.pallas_call(
+        functools.partial(weight_kernel, taps > 1, rows, parts),
+        name="weight_grad",
+        grid=(steps,),
+        in_specs=[IN_SMEM, pl.BlockSpec(*left_in), pl.BlockSpec(*right_in)],
+        out_specs=[pl.BlockSpec(block, out_map)] * 2,
+        out_shape=[jax.ShapeDtypeStruct(shape, BF16)] * 2,
+        scratch_shapes=[pltpu.VMEM((k, tile), F32)],
+        compiler_params=pltpu.CompilerParams(vmem_limit_bytes=VMEM_LIMIT),
+        cost_estimate=cost(10 if taps > 1 else 5),
+    )(place, left, right)
 
 
 class Links:
@@ -857,6 +1098,29 @@
             v = jnp.stack([center, square])
         return v
 
+    def from_each(self, v, bits):
+        return [v] + [self.swap(v, b) for b in bits]
+
+    def across(self, own):
+        return self.swap(own, 1)
+
+    def joined(self, parts):
+        a, b, c, d = parts
+        core, y = self.me & 1, (self.me >> 1) & 1
+        pick = lambda bit, p, q: (jnp.where(bit == 0, p, q), jnp.where(bit == 0, q, p))
+        a, b = pick(core, a, b)
+        c, d = pick(core, c, d)
+        a, c = pick(y, a, c)
+        b, d = pick(y, b, d)
+        return jnp.concatenate([a, b, c, d], a.ndim - 2).astype(F32)
+
+    def scatter_plain(self, left, right, taps=1):
+        g = dot(left[: right.shape[0]], right, TN).astype(BF16)
+        if taps > 1:
+            g = g.reshape(taps, left.shape[1] // taps, -1)
+        g = lax.psum_scatter(g, "img", scatter_dimension=int(taps > 1), tiled=True)
+        return lax.psum(g, "blk").astype(F32)
+
     def gather(self, v):
         depth = 0
         for bit in reversed(range(self.low + self.high)):
@@ -867,6 +1131,139 @@
             )
             depth += 1
         return v.reshape((self.size,) + v.shape[depth:])
+
+
+class Weights:
+    def __init__(self, links, place, staged, shards):
+        self.links, self.place, self.staged, self.shards = links, place, staged, shards
+        self.now, self.halves = {}, {}
+
+    def cut(self, names, after=()):
+        if self.staged:
+            self.now.update(zip(names, cut(self.place, [self.shards[n] for n in names], after)))
+
+    def along_z(self, name):
+        if self.staged:
+            self.now[name] = self.links.from_each(self.now[name], (8, 16, 24))
+
+    def in_plane(self, name, after=()):
+        if self.staged:
+            (z,) = local(lambda *v: [jnp.stack(v)], self.now[name], after, "stack")
+            self.now[name] = self.links.from_each(z, (2, 4, 6))
+
+    def swap(self, name, after=()):
+        if self.staged:
+            (own,) = local(lambda *v: [jnp.stack(v)], self.now[name], after, "stack")
+            self.now[name] = own, self.links.across(own)
+
+    def fetch(self, *names, after=()):
+        if not self.staged:
+            return ()
+        at, widest = 0, max(self.shards[n].shape[-1] for n in names)
+        for n in names:
+            half, folds = self.shards[n].shape[-2] // 2, widest // self.shards[n].shape[-1]
+            self.halves[n] = names, at, half, folds
+            at += half // folds
+        own = half_of(self.place, [self.shards[n] for n in names], after)
+        self.now[names] = lax.all_gather(own, "img")
+        return (own,)
+
+    def hand_on(self, *names, after=()):
+        if self.staged:
+            own = pin(self.now[names], after)
+            self.now[names] = own, self.links.across(own)
+
+    def get(self, name):
+        if not self.staged:
+            shard = self.shards[name]
+            return lax.all_gather(shard, "img", axis=shard.ndim - 2, tiled=True)
+        if name in self.halves:
+            names, *where = self.halves[name]
+            return join_halves(self.place, *self.now[names], *where)
+        return assemble(self.place, *self.now[name])
+
+    def state(self, *names):
+        return tuple(jax.tree.leaves([self.now[n] for n in names])) if self.staged else ()
+
+
+class Sums:
+    def __init__(self, links, place, staged):
+        self.links, self.place, self.staged = links, place, staged
+        self.now = {}
+
+    def start(self, name, left, right, taps=1, halves=False):
+        if self.staged:
+            self.now[name] = weight_grad(self.place, left, right, taps, halves)
+        else:
+            self.now[name] = self.links.scatter_plain(left, right, taps)
+
+    def swap(self, name):
+        if self.staged:
+            keep, send = self.now[name]
+            self.now[name] = keep, self.links.across(send)
+
+    def in_plane(self, name, after=()):
+        if self.staged:
+            fold = lambda keep, got: [add2(keep[j], got[j]) for j in range(4)]
+            part = local(fold, self.now[name], after, "fold")
+            self.now[name] = [part[0]] + [self.links.swap(part[j], 2 * j) for j in (1, 2, 3)]
+
+    def along_z(self, name, after=()):
+        if self.staged:
+            fold = lambda *got: [sum4([g[k] for g in got]) for k in range(4)]
+            part = local(fold, self.now[name], after, "fold")
+            self.now[name] = [part[0]] + [self.links.swap(part[k], 8 * k) for k in (1, 2, 3)]
+
+    def join(self, name, after=()):
+        if self.staged:
+            (part,) = local(lambda *got: [sum4(got)], self.now[name], after, "fold")
+            self.now[name] = self.links.from_each(part, (1, 2, 3))
+
+    def scatter(self, *names, after=()):
+        if self.staged:
+            parts = [p for n in names for p in self.now[n]]
+            join = lambda *v: [jnp.concatenate([add2(a, b) for a, b in zip(v[::2], v[1::2])], 1)]
+            (part,) = local(join, parts, after, "fold", 4)
+            self.now[names] = lax.psum_scatter(part, "img", scatter_dimension=0, tiled=False)
+
+    def across_y(self, *names):
+        if self.staged:
+            own = self.now[names]
+            (own,) = local(lambda a, b: [add2(a, b)], [own, self.links.swap(own, 2)], (), "fold")
+            self.now[names] = own, self.links.across(own)
+
+    def split(self, names, rows):
+        if not self.staged:
+            return [self.now[n] for n in names]
+        own, other = self.now[names]
+        core = self.links.me & 1
+        both = jnp.where(core == 0, own, other), jnp.where(core == 0, other, own)
+        found, at = [], 0
+        for steps, half, by_tap in rows:
+            pieces = [b[at : at + steps * half].reshape(steps, half, -1) for b in both]
+            piece = jnp.concatenate(pieces, 1).astype(F32)
+            if not by_tap:
+                piece = jnp.concatenate([piece[k] for k in range(steps)], 1)
+            found.append(piece)
+            at += steps * half
+        return found
+
+    def state(self, *names):
+        return tuple(jax.tree.leaves([self.now[n] for n in names])) if self.staged else ()
+
+    def get(self, name):
+        if not self.staged:
+            return self.now[name]
+        return self.links.joined(self.now[name])
+
+
+def add2(a, b):
+    return (a.astype(F32) + b.astype(F32)).astype(BF16)
+
+
+def sum4(v):
+    a, b, c, d = [x.astype(F32) for x in v]
+    return ((a + b) + (c + d)).astype(BF16)
 
 
 def head_plain(f, links, pooled, hidden, embed, affine, labels):
@@ -908,7 +1305,7 @@
     shift_grad = lax.psum(jnp.sum(d, 0), AXES)
     gain_grad = lax.psum(jnp.sum(d * hat, 0), AXES)
     back = (affine[0] * factor * (d - shift_grad / number - hat * (gain_grad / number))).astype(BF16)
-    return loss, dot(pooled, back, TN), dot(low, grad, TN), gain_grad, shift_grad, dot(back, hidden, NT)
+    return loss, back, low, grad, gain_grad, shift_grad, dot(back, hidden, NT)
 
 
 def per_device(
@@ -926,111 +1323,156 @@
     affine = [both[:, starts[k] : starts[k + 1]] for k in range(8)]
     mask = f.mask()
 
-    def gathered(w, axis=0):
-        return lax.all_gather(w, "img", axis=axis, tiled=True)
-
-    w_reduce = gathered(first_reduce)
-    w_spatial = gathered(first_spatial, 2).reshape(9, mid, mid)
-    w_expand = gathered(first_expand)
-    w_short = gathered(first_short)
-    w_reduce2 = gathered(second_reduce)
-    w_spatial2 = gathered(second_spatial, 2).reshape(9, mid, mid)
-    w_expand2 = gathered(second_expand)
-    w_hidden = gathered(head_hidden)
-    w_embed = gathered(head_embed)
-
+    place = jnp.stack([lax.axis_index("img"), lax.axis_index("blk"), links.me]).astype(jnp.int32)
+    kernel_shape = (9,) + first_spatial.shape[2:]
+    shards = {
+        "reduce": first_reduce,
+        "spatial": first_spatial.reshape(kernel_shape),
+        "expand": first_expand,
+        "short": first_short,
+        "reduce2": second_reduce,
+        "spatial2": second_spatial.reshape(kernel_shape),
+        "expand2": second_expand,
+        "head": jnp.concatenate([head_hidden, head_embed], 1),
+    }
+    staged = links.img == 8 and links.blk == 4
+    staged = staged and all(w.shape[-2] % 64 == 0 for w in shards.values())
+    weights = Weights(links, place, staged, shards)
+    sums = Sums(links, place, staged)
     n_in, n_out = 4 * f.valid, f.valid
     all_in, all_out = n_in * links.size, n_out * links.size
 
-    x = split_cells(f, x_large, x_small)
-    reduced, st0 = linear(f, x, w_reduce, mask, 4, 256)
-    st0 = links.moments(st0, n_in)
-    patch1, turned, st1 = conv(f, 2, all_in, reduced, st0, affine[0], w_spatial.reshape(9 * mid, mid), mask)
-    st1 = links.moments(st1, n_out)
-    skipped, st3 = linear(f, x, w_short, mask, 1, 512)
-    turned_low, expanded, st2 = expand(f, all_out, turned, st1, affine[1], w_expand, mask)
-    joint = links.moments(jnp.concatenate([st2, st3], 1), n_out)
+    weights.cut(["reduce"])
+    reduce_cut = weights.state("reduce")
+    weights.along_z("reduce")
+    weights.fetch("spatial")
+    x = split_cells(f, x_large, x_small, after=reduce_cut)
+    weights.in_plane("reduce", after=(x,))
+    first = ("expand", "short", "reduce2", "expand2")
+    first_half = weights.fetch(*first, after=(x,))
+    weights.swap("reduce")
+    w_reduce = weights.get("reduce")
+    reduced, part0 = linear(f, x, w_reduce, mask, 4, 256, after=first_half)
+    st0 = links.moments(part0, n_in)
+    weights.hand_on("spatial", after=(st0,))
+    spatial2_half = weights.fetch("spatial2", after=(st0,))
+    w_spatial = weights.get("spatial")
+    patch1, turned, part1 = conv(
+        f, 2, all_in, reduced, st0, affine[0], w_spatial.reshape(9 * mid, mid), mask, after=spatial2_half
+    )
+    st1 = links.moments(part1, n_out)
+    weights.hand_on(*first, after=(st1,))
+    w_expand, w_short, w_reduce2, w_expand2 = [weights.get(n) for n in first]
+    head_half = weights.fetch("head", after=(st1,))
+    turned_low, expanded, part2 = expand(f, all_out, turned, st1, affine[1], w_expand, mask)
+    skipped, part3 = linear(f, x, w_short, mask, 1, 512, after=(part2,) + head_half)
+    joint = links.moments(jnp.concatenate([part2, part3], 1), n_out)
     st2, st3 = joint[:, :wide], joint[:, wide:]
-    block_low, block_pre, mixing, st4 = mix(
+    block_low, block_pre, mixing, part4 = mix(
         f, all_out, expanded, skipped, st2, affine[2], st3, affine[3], w_reduce2, mask
     )
-    st4 = links.moments(st4, n_out)
-    patch2, rotated, st5 = conv(f, 1, all_out, mixing, st4, affine[4], w_spatial2.reshape(9 * mid, mid), mask)
-    st5 = links.moments(st5, n_out)
-    rotated_low, widened, st6 = expand(f, all_out, rotated, st5, affine[5], w_expand2, mask)
-    st6 = links.moments(st6, n_out)
+    weights.hand_on("spatial2", after=(part4,))
+    st4 = links.moments(part4, n_out)
+    w_spatial2 = weights.get("spatial2")
+    patch2, rotated, part5 = conv(
+        f, 1, all_out, mixing, st4, affine[4], w_spatial2.reshape(9 * mid, mid), mask, after=(w_expand2,)
+    )
+    st5 = links.moments(part5, n_out)
+    rotated_low, widened, part6 = expand(f, all_out, rotated, st5, affine[5], w_expand2, mask)
+    st6 = links.moments(part6, n_out)
+    weights.hand_on("head", after=(st6,))
     pooled, slopes, view_sums = pool(f, all_out, widened, block_pre, st6, affine[6], mask)
     pooled = pooled.astype(BF16)
     labels = jnp.concatenate([large_image, small_image], 0)
+    w_head = weights.get("head")
 
     shard = head_hidden.shape[0]
-    joined = links.size * SLOT <= 512 and shard % 128 == 0
-    if joined:
-        padded = jnp.concatenate([labels, jnp.full((SLOT - f.views,), -1, jnp.int32)])
-        every_label = lax.all_gather(padded, AXES, axis=0, tiled=True)
-        every = links.gather(pooled).reshape(links.size * SLOT, wide)
-        place = jnp.stack([lax.axis_index("img"), links.me]).astype(jnp.int32)
+    if staged:
+        digits = jnp.concatenate([labels, jnp.full((SLOT - f.views,), -1, jnp.int32)])
+        digits = jnp.stack([digits // 256, digits % 256], 1).astype(BF16)
+        pooled = jnp.concatenate([pooled, jnp.pad(digits, ((0, 0), (0, 126)))], 1)
+        every = jnp.stack(links.from_each(pooled, (8, 16, 24)))
+        every = jnp.stack(links.from_each(every, (2, 4, 6)))
+        every = assemble(place, every, links.across(every))
         loss, hidden_grad, embed_grad, gains7, back, sums6 = head(
-            f, links.size, shard, place, every, w_hidden, w_embed, affine[7], every_label, view_sums
+            f, links.size, shard, place, every, w_head, affine[7], view_sums
         )
         loss = loss[0, 0]
         gain7, shift7 = gains7[0], gains7[1]
     else:
-        loss, hidden_part, embed_part, gain7, shift7, back = head_plain(
-            f, links, pooled[: f.views], w_hidden, w_embed, affine[7], labels
+        pooled = pooled[: f.views]
+        loss, hidden_back, head_low, embed_back, gain7, shift7, back = head_plain(
+            f, links, pooled, w_head[:, :proj], w_head[:, proj:], affine[7], labels
         )
         back = jnp.pad(back, ((0, SLOT - f.views), (0, 0))) * f.cells()
         sums6 = jnp.stack([jnp.sum(back * view_sums[:SLOT], 0), jnp.sum(back * view_sums[SLOT:], 0)])
+        hidden_grad = links.scatter_plain(pooled, hidden_back)
+        embed_grad = links.scatter_plain(head_low, embed_back)
     sums6 = links.total(sums6)
 
-    widened_back, d5, sums5 = widen_back(
+    widened_back, d5, part5 = widen_back(
         f, all_out, widened, slopes, back, st6, affine[6], sums6, w_expand2, rotated, st5, affine[5], mask
     )
-    expand2_grad = dot(rotated_low, widened_back, TN).astype(BF16)
-    sums5 = links.total(sums5)
-    rotated_back, d4, sums4 = conv_back(
-        f, 1, all_out, all_out, d5, rotated, st5, affine[5], sums5, w_spatial2, mixing, st4, affine[4], mask
-    )
-    spatial2_grad = dot(patch2, rotated_back, TN).astype(BF16)
-    sums4 = links.total(sums4)
-    mixing_back, block_grad, sums23 = mix_back(
+    sums.start("expand2", rotated_low, widened_back, halves=True)
+    sums.swap("expand2")
+    sums5 = links.total(part5)
+    rotated_back, d4, part4 = conv_back(
+        f, 1, all_out, all_out, d5, rotated, st5, affine[5], sums5, w_spatial2, mixing, st4, affine[4],
+        mask, after=sums.state("expand2"),
+    )
+    sums.start("spatial2", patch2, rotated_back, 9, halves=True)
+    sums.swap("spatial2")
+    sums4 = links.total(part4)
+    first = ("expand2", "spatial2")
+    sums.scatter(*first, after=(sums4,))
+    mixing_back, block_grad, part23 = mix_back(
         f, all_out, d4, mixing, st4, affine[4], sums4, w_reduce2, back, slopes, block_pre,
-        expanded, st2, affine[2], skipped, st3, affine[3], mask,
-    )
-    reduce2_grad = dot(block_low, mixing_back, TN).astype(BF16)
-    sums23 = links.total(sums23)
-    expanded_back, skipped_back, d1, sums1 = block_back(
+        expanded, st2, affine[2], skipped, st3, affine[3], mask, after=sums.state("spatial2"),
+    )
+    sums.start("reduce2", block_low, mixing_back, halves=True)
+    sums.swap("reduce2")
+    sums23 = links.total(part23)
+    expanded_back, skipped_back, d1, part1 = block_back(
         f, all_out, block_grad, expanded, st2, affine[2], skipped, st3, affine[3], sums23, w_expand,
-        turned, st1, affine[1], mask,
-    )
-    expand_grad = dot(turned_low, expanded_back, TN).astype(BF16)
-    short_grad = dot(x[: f.rows], skipped_back, TN).astype(BF16)
+        turned, st1, affine[1], mask, after=sums.state("reduce2"),
+    )
+    sums.start("expand", turned_low, expanded_back, halves=True)
+    sums.swap("expand")
+    sums.start("short", x, skipped_back, halves=True)
+    sums.swap("short")
     sub = dot(skipped_back, w_short, NT)
-    sums1 = links.total(sums1)
-    turned_back, d0, sums0 = conv_back(
-        f, 2, all_out, all_in, d1, turned, st1, affine[1], sums1, w_spatial, reduced, st0, affine[0], mask
-    )
-    spatial_grad = dot(patch1, turned_back, TN).astype(BF16)
-    sums0 = links.total(sums0)
+    sums1 = links.total(part1)
+    second = ("reduce2", "expand", "short")
+    sums.scatter(*second, after=(sums1,))
+    turned_back, d0, part0 = conv_back(
+        f, 2, all_out, all_in, d1, turned, st1, affine[1], sums1, w_spatial, reduced, st0, affine[0], mask,
+        after=sums.state("expand", "short"),
+    )
+    sums.start("spatial", patch1, turned_back, 9)
+    sums.swap("spatial")
+    sums0 = links.total(pin(part0, sums.state(first)))
+    sums.across_y(*first)
+    sums.in_plane("spatial", after=(sums0,))
     reduced_back, grad_large, grad_small = input_back(
-        f, all_in, d0, reduced, st0, affine[0], sums0, w_reduce, sub, mask
-    )
-    reduce_grad = dot(x, reduced_back, TN).astype(BF16)
-
-    def scattered(g, axis=0):
-        g = lax.psum_scatter(g, "img", scatter_dimension=axis, tiled=True)
-        return lax.psum(g, "blk").astype(F32)
-
-    expand2_grad = scattered(expand2_grad)
-    spatial2_grad = scattered(spatial2_grad.reshape(3, 3, mid, mid), 2)
-    reduce2_grad = scattered(reduce2_grad)
-    expand_grad = scattered(expand_grad)
-    short_grad = scattered(short_grad)
-    spatial_grad = scattered(spatial_grad.reshape(3, 3, mid, mid), 2)
-    reduce_grad = scattered(reduce_grad)
-    if not joined:
-        hidden_grad = scattered(hidden_part.astype(BF16))
-        embed_grad = scattered(embed_part.astype(BF16))
+        f, all_in, d0, reduced, st0, affine[0], sums0, w_reduce, sub, mask, after=sums.state("spatial")[:1]
+    )
+    sums.start("reduce", x, reduced_back)
+    sums.swap("reduce")
+    sums.in_plane("reduce", after=sums.state("spatial"))
+    sums.along_z("spatial")
+    sums.along_z("reduce")
+    sums.join("spatial")
+    sums.join("reduce")
+    sums.across_y(*second)
+    eighth = lambda n: n // (2 * links.img)
+    expand2_grad, spatial2_grad = sums.split(
+        first, [(wide // 512, eighth(mid), False), (9, eighth(mid), True)]
+    )
+    reduce2_grad, expand_grad, short_grad = sums.split(
+        second,
+        [(1, eighth(wide), False), (wide // 512, eighth(mid), False), (wide // 512, eighth(2 * mid), False)],
+    )
+    spatial_grad, reduce_grad = sums.get("spatial"), sums.get("reduce")
 
     gain_grads = jnp.concatenate(
         [sums0[1], sums1[1], sums23[1], sums23[2], sums4[1], sums5[1], sums6[1], gain7]
@@ -1039,8 +1481,8 @@
         [sums0[0], sums1[0], sums23[0], sums23[0], sums4[0], sums5[0], sums6[0], shift7]
     )
     return (
-        loss, grad_large, grad_small, reduce_grad, spatial_grad, expand_grad, short_grad,
-        reduce2_grad, spatial2_grad, expand2_grad, hidden_grad, embed_grad, gain_grads, shift_grads,
+        loss, grad_large, grad_small, reduce_grad, spatial_grad.reshape(first_spatial.shape), expand_grad, short_grad,
+        reduce2_grad, spatial2_grad.reshape(first_spatial.shape), expand2_grad, hidden_grad, embed_grad, gain_grads, shift_grads,
     )
 
 

time: 1420 us -> 705 us (0.50)
  waiting for transfers between devices: 1020 us -> 234 us
  Pallas kernels: 127 us -> 240 us
  blocking collectives: 76.8 us -> 0 us
  starting transfers between devices: 92.8 us -> 133 us
  matrix products: 36.6 us -> 5.81 us
  local copies, waits for them, and re-layouts: 16.2 us -> 43.9 us
    reduce_scatter x7 -> x2, waiting for transfers between devices: 523 us -> 0.02 us  [scatter(): lax.psum_scatter(part, 'img', scatter_dimension=0, tiled=False)]
    all_gather x8 -> x4, waiting for transfers between devices: 293 us -> 47.1 us  [fetch(): self.now[names] = lax.all_gather(own, 'img')]
    pallas_call x16 -> x54, Pallas kernels: 127 us -> 240 us  [the longest x15 104 us: call(): pl.pallas_call(skipping(kernel, len(inputs), len(after)), name=kernel.fun...]
    psum x1 -> x0, waiting for transfers between devices: 63.3 us -> none  [scattered(): return lax.psum(g, 'blk').astype(F32)]
    ppermute x89 -> x131, waiting for transfers between devices: 138 us -> 186 us  [swap(): return lax.ppermute(v, AXES, [(i, i ^ bits) for i in range(self.size)])]
    unnamed x1 -> x0, blocking collectives: 42.4 us -> none
    ppermute x89 -> x131, starting transfers between devices: 91.5 us -> 132 us  [swap(): return lax.ppermute(v, AXES, [(i, i ^ bits) for i in range(self.size)])]
    all_gather x1 -> x0, blocking collectives: 34.4 us -> none  [gathered(): return lax.all_gather(w, 'img', axis=axis, tiled=True)]
  transfers between devices with their start and end apart: 105 -> 137, of which waited for: 77 -> 79; matrix products, arithmetic and copies ran while one was open for 4% -> 5% of each run, Pallas kernels for 4% -> 26%
where the time goes in v2:
time: 705 us; the launch traced here: 694 us
  Pallas kernels  240 us (34%)
  waiting for transfers between devices  234 us (33%)
  starting transfers between devices  133 us (19%)
  local copies, waits for them, and re-layouts  43.9 us (6%)
  other arithmetic  22.4 us (3%)
  between operations  16 us (2%)
    ppermute x131, waiting for transfers between devices, swap(): return lax.ppermute(v, AXES, [(i, i ^ bits) for i in range(self.size)])  186 us
    ppermute x131, starting transfers between devices, swap(): return lax.ppermute(v, AXES, [(i, i ^ bits) for i in range(self.size)])  132 us
    pallas_call x15, Pallas kernels, call(): pl.pallas_call(skipping(kernel, len(inputs), len(after)), name=kernel.fun...  104 us
    all_gather x4, waiting for transfers between devices, fetch(): self.now[names] = lax.all_gather(own, 'img')  47.1 us
    pallas_call x7, Pallas kernels, weight_grad(): pl.pallas_call(functools.partial(weight_kernel, taps > 1, rows, parts), n...  44.8 us
    unnamed x173, local copies, waits for them, and re-layouts  41.5 us
    pallas_call x12, Pallas kernels, local(): pl.pallas_call(skipping(kernel, len(arrays), len(after)), name=name, in_s...  33.3 us
    pallas_call x1, Pallas kernels, head(): pl.pallas_call(functools.partial(head_kernel, f, devices, shard), name='h...  22.1 us
  transfers between devices with their start and end apart: 137, of which 79 were waited for; matrix products, arithmetic and copies ran while one was open for 5% of the time, Pallas kernels for 26%

profile of v2, /device:TPU:0, one launch (start us, length us, event | category | flops | bytes accessed | tf_op | source)
XLA Modules:
  0.0 694.1 jit_solution(14859494067161922016)
XLA Ops:
  16.9 4.9 split_kernel.1.refs_4_.refs_5_.refs_0_.left_ref
  29.7 5.0 collective-permute-done.1.refs_2_
  44.9 4.0 collective-permute-done.5.refs_3_
  58.0 5.7 linear_kernel.2
  68.5 3.4 collective-permute-start.10
  73.5 3.6 collective-permute-start.11
  92.6 7.9 %conv_kernel.2 = (bf16[384,4608]{1,0:T(8,128)(2,1)}, f32[384,512]{1,0:T(8,128)}, f32[2,512]{1,0:T(2,128)}) custom-call(f32[1536,512]{1,0:T(8,128)} %get-tuple-element.92.refs_0_.refs_6_.refs_1_, f32[2,512]{1,0:T(2,128)} %copy-done.19, f32[2,512]{1,0:T(2,128)} %get-tuple-element.273.refs_2_.refs_8_.refs_3_, bf16[4608,512]{1,0:T(8,128)(2,1)} %bitcast.85, ...), custom_call_target="tpu_custom_call" | custom-call | bytes 28000000 | tf_op jit(solution)/shard_map/conv_kernel/pallas_call | solution.py:33
  117.9 39.6 %all-gather.11.cloned.1.call-done = bf16[1280,2048]{1,0:T(8,128)(2,1)} async-done(((bf16[160,2048]{1,0:T(8,128)(2,1)}), bf16[1280,2048]{1,0:T(8,128)(2,1)}) %all-gather.11.cloned.1.call-update) | async-done | bytes 5242896 | tf_op jit(solution)/shard_map/all_gather | solution.py:1168
  161.9 4.7 collective-permute-done.22.other_ref
  170.3 5.4 expand_kernel.2
  180.7 6.0 linear_kernel.3
  193.9 3.6 collective-permute-done.26
  207.5 7.8 %mix_kernel.1 = (bf16[384,2048]{1,0:T(8,128)(2,1)}, f32[384,2048]{1,0:T(8,128)}, f32[384,512]{1,0:T(8,128)}, f32[2,512]{1,0:T(2,128)}) custom-call(f32[384,2048]{1,0:T(8,128)} %get-tuple-element.96.exp_ref.refs_9_.refs_1_, f32[384,2048]{1,0:T(8,128)} %get-tuple-element.98.skip_ref.refs_12_.refs_4_, f32[2,2048]{1,0:T(2,128)} %get-tuple-element.280.stats_a.refs_10_.refs_2_, ...), custom_call_target="tpu_custom_call" | custom-call | bytes 28000000 | tf_op jit(solution)/shard_map/mix_kernel/pallas_call | solution.py:33
  238.2 6.1 conv_kernel.3
  261.6 5.3 expand_kernel.3
  284.9 7.4 %all-gather.15.cloned.1.call-done = bf16[1024,2176]{1,0:T(8,128)(2,1)} async-done(((bf16[128,2176]{1,0:T(8,128)(2,1)}), bf16[1024,2176]{1,0:T(8,128)(2,1)}) %all-gather.15.cloned.1.call-update) | async-done | bytes 4456464 | tf_op jit(solution)/shard_map/all_gather | solution.py:1168
  293.2 6.7 pool_kernel.1
  305.9 3.7 collective-permute-done.53
  313.2 5.8 collective-permute-done.55
  326.1 3.9 assemble.3.p_ref.digit_ref
  331.4 4.4 join_halves.13.h_ref.e_ref
  335.8 3.5 copy-done
  339.3 22.1 %head.1 = (f32[8,128]{1,0:T(8,128)}, f32[256,2048]{1,0:T(8,128)}, f32[256,128]{1,0:T(8,128)}, f32[2,2048]{1,0:T(2,128)}, f32[16,2048]{1,0:T(8,128)}, /*index=5*/f32[2,2048]{1,0:T(2,128)}) custom-call(s32[3]{0:T(128)} %pad_add_fusion.place_ref.refs_0_, bf16[512,2176]{1,0:T(8,128)(2,1)} %copy-done.4, bf16[512,2176]{1,0:T(8,128)(2,1)} %copy-done.4, ...), custom_call_target="tpu_custom_call" | custom-call | bytes 77000000 | tf_op jit(solution)/shard_map/head/pallas_call | solution.py:547
  380.5 7.4 %widen_back_kernel.1 = (bf16[384,2048]{1,0:T(8,128)(2,1)}, f32[384,512]{1,0:T(8,128)}, f32[2,512]{1,0:T(2,128)}) custom-call(f32[384,2048]{1,0:T(8,128)} %get-tuple-element.104.wide_ref, f32[384,2048]{1,0:T(8,128)} %get-tuple-element.110.slope_ref.refs_7_, f32[16,2048]{1,0:T(8,128)} %get-tuple-element.111.back_ref.refs_6_, f32[2,2048]{1,0:T(2,128)} %copy-done.18, ...), custom_call_target="tpu_custom_call" | custom-call | bytes 25900000 | tf_op jit(solution)/shard_map/widen_back_kernel/pallas_call | solution.py:33
  387.9 4.8 weight_grad.7
  410.6 6.7 conv_back_kernel.2
  417.3 9.6 %weight_grad.8 = (bf16[8,288,512]{2,1,0:T(8,128)(2,1)}, bf16[8,288,512]{2,1,0:T(8,128)(2,1)}) custom-call(s32[3]{0:T(128)} %pad_add_fusion.place_ref.refs_0_, bf16[384,4608]{1,0:T(8,128)(2,1)} %get-tuple-element.121.left_ref, bf16[384,512]{1,0:T(8,128)(2,1)} %get-tuple-element.122.right_ref), custom_call_target="tpu_custom_call" | custom-call | bytes 35000000 | tf_op jit(solution)/shard_map/weight_grad/pallas_call | solution.py:1026
  440.2 3.6 collective-permute-done.81
  445.8 5.6 fold.10
  451.5 9.8 %mix_back_kernel.1 = (bf16[384,512]{1,0:T(8,128)(2,1)}, f32[384,2048]{1,0:T(8,128)}, f32[3,2048]{1,0:T(4,128)}) custom-call(f32[384,512]{1,0:T(8,128)} %get-tuple-element.119.refs_0_, f32[384,512]{1,0:T(8,128)} %get-tuple-element.100.refs_0_.refs_6_.refs_1_, f32[2,512]{1,0:T(2,128)} %pad_maximum_fusion.23.refs_1_.refs_7_.refs_2_, ...), custom_call_target="tpu_custom_call" | custom-call | bytes 34300000 | tf_op jit(solution)/shard_map/mix_back_kernel/pallas_call | solution.py:33
  461.3 4.3 weight_grad.9
  472.1 4.0 collective-permute-done.86
  486.6 8.7 %block_back_kernel.1 = (bf16[384,2048]{1,0:T(8,128)(2,1)}, bf16[384,2048]{1,0:T(8,128)(2,1)}, f32[384,512]{1,0:T(8,128)}, f32[2,512]{1,0:T(2,128)}) custom-call(f32[384,2048]{1,0:T(8,128)} %get-tuple-element.125.refs_0_, f32[384,2048]{1,0:T(8,128)} %get-tuple-element.96.exp_ref.refs_9_.refs_1_, f32[2,2048]{1,0:T(2,128)} %get-tuple-element.280.stats_a.refs_10_.refs_2_, ...), custom_call_target="tpu_custom_call" | custom-call | bytes 30800000 | tf_op jit(solution)/shard_map/block_back_kernel/pallas_call | solution.py:33
  495.4 6.3 weight_grad.11
  501.7 4.8 weight_grad.10
  511.7 3.4 collective-permute-done.94
  525.9 6.5 fold.17
  533.6 7.6 %conv_back_kernel.3 = (bf16[384,512]{1,0:T(8,128)(2,1)}, f32[1536,512]{1,0:T(8,128)}, f32[2,512]{1,0:T(2,128)}) custom-call(f32[384,512]{1,0:T(8,128)} %get-tuple-element.131.refs_0_, f32[384,512]{1,0:T(8,128)} %get-tuple-element.94.pre_ref.refs_9_.refs_1_, f32[2,512]{1,0:T(2,128)} %copy-done.20, f32[2,512]{1,0:T(2,128)} %get-tuple-element.272.affine_ref.refs_11_.refs_3_, ...), custom_call_target="tpu_custom_call" | custom-call | bytes 25200000 | tf_op jit(solution)/shard_map/conv_back_kernel/pallas_call | solution.py:33
  541.3 9.7 %weight_grad.12 = (bf16[4,4,9,16,512]{4,3,2,1,0:T(8,128)(2,1)}, bf16[4,4,9,16,512]{4,3,2,1,0:T(8,128)(2,1)}) custom-call(s32[3]{0:T(128)} %pad_add_fusion.place_ref.refs_0_, bf16[384,4608]{1,0:T(8,128)(2,1)} %get-tuple-element.142.left_ref, bf16[384,512]{1,0:T(8,128)(2,1)} %get-tuple-element.143.right_ref), custom_call_target="tpu_custom_call" | custom-call | bytes 35000000 | tf_op jit(solution)/shard_map/weight_grad/pallas_call | solution.py:1026
  556.9 5.8 fusion.51.refs_6_
  573.4 4.0 fold.11
  580.8 8.3 %input_back_kernel.1 = (bf16[1536,512]{1,0:T(8,128)(2,1)}, bf16[4,14,14,1024]{3,2,1,0:T(8,128)(2,1)}, bf16[8,6,6,1024]{3,2,1,0:T(8,128)(2,1)}) custom-call(f32[1536,512]{1,0:T(8,128)} %get-tuple-element.140.refs_0_, f32[1536,512]{1,0:T(8,128)} %get-tuple-element.92.refs_0_.refs_6_.refs_1_, f32[2,512]{1,0:T(2,128)} %copy-done.19, ...), custom_call_target="tpu_custom_call" | custom-call | bytes 29400000 | tf_op jit(solution)/shard_map/input_back_kernel/pallas_call | solution.py:33
  589.1 5.3 weight_grad.13
  596.6 4.7 collective-permute-done.110.refs_4_.refs_2_
  601.3 12.4 %collective-permute-done.111.refs_5_.refs_3_ = bf16[4,9,16,512]{3,2,1,0:T(8,128)(2,1)S(1)} collective-permute-done((bf16[4,9,16,512]{3,2,1,0:T(8,128)(2,1)}, bf16[4,9,16,512]{3,2,1,0:T(8,128)(2,1)S(1)}, u32[]{:S(2)}, u32[]{:S(2)}) %collective-permute-start.111) | collective-permute-done | bytes 589856 | tf_op jit(solution)/shard_map/ppermute | solution.py:1048
  632.4 5.2 collective-permute-done.115.refs_1_
  637.6 5.0 collective-permute-start.117
  661.5 16.5 %collective-permute-done.127.refs_1_ = bf16[512,512]{1,0:T(8,128)(2,1)S(1)} collective-permute-done((bf16[512,512]{1,0:T(8,128)(2,1)}, bf16[512,512]{1,0:T(8,128)(2,1)S(1)}, u32[]{:S(2)}, u32[]{:S(2)}) %collective-permute-start.127) | collective-permute-done | bytes 524320 | tf_op jit(solution)/shard_map/ppermute | solution.py:1048
  (562 shorter events, 337.9 us)
Async XLA Ops:
  7.2 75.3 %all-gather.9.cloned.1.call-start = ((), (), s32[]{:S(2)}) async-start(), calls=%async_computation.4 | async-start | bytes 2654208 | tf_op jit(solution)/shard_map/all_gather | solution.py:1168
  9.7 147.8 %all-gather.11.cloned.1.call-start = ((), (), s32[]{:S(2)}) async-start(), calls=%async_computation.5 | async-start | bytes 5898240 | tf_op jit(solution)/shard_map/all_gather | solution.py:1168
  24.0 191.4 %all-gather.13.cloned.1.call-start = ((), (), s32[]{:S(2)}) async-start(), calls=%async_computation.6 | async-start | bytes 2654208 | tf_op jit(solution)/shard_map/all_gather | solution.py:1168
  27.2 7.6 %collective-permute-start.1 = (bf16[32,512]{1,0:T(8,128)(2,1)S(1)}, bf16[32,512]{1,0:T(8,128)(2,1)S(1)}, u32[]{:S(2)}, u32[]{:S(2)}) collective-permute-start(bf16[32,512]{1,0:T(8,128)(2,1)S(1)} %copy-done.13), channel_id=1, source_target_pairs={{0,16},{1,17},{2,18},{3,19},{4,20},{5,21},{6,22},{7,23},{8,24},{9,... | collective-permute-start | bytes 98312 | tf_op jit(solution)/shard_map/ppermute | solution.py:1048
  41.2 7.7 %collective-permute-start.5 = (bf16[4,32,512]{2,1,0:T(8,128)(2,1)}, bf16[4,32,512]{2,1,0:T(8,128)(2,1)S(1)}, u32[]{:S(2)}, u32[]{:S(2)}) collective-permute-start(bf16[4,32,512]{2,1,0:T(8,128)(2,1)} %stack.185.refs_0_), channel_id=1, source_target_pairs={{0,6},{1,7},{2,4},{3,5},{4,2},{5,3},{6,0},{7,1},{8,14},{9,15},{10,... | collective-permute-start | bytes 393224 | tf_op jit(solution)/shard_map/ppermute | solution.py:1048
  157.5 9.1 %collective-permute-start.22 = (bf16[8,160,2048]{2,1,0:T(8,128)(2,1)}, bf16[8,160,2048]{2,1,0:T(8,128)(2,1)}, u32[]{:S(2)}, u32[]{:S(2)}) collective-permute-start(bf16[8,160,2048]{2,1,0:T(8,128)(2,1)} %pin.6.own_ref), channel_id=1, source_target_pairs={{0,1},{1,0},{2,3},{3,2},{4,5},{5,4},{6,7},{7,6},{8,9},{9,8},{10,11... | collective-permute-start | bytes 15728648 | tf_op jit(solution)/shard_map/ppermute | solution.py:1048
  157.6 134.7 %all-gather.15.cloned.1.call-start = ((), (), s32[]{:S(2)}) async-start(), calls=%async_computation.7 | async-start | bytes 5013504 | tf_op jit(solution)/shard_map/all_gather | solution.py:1168
  193.3 357.8 %reduce-scatter.3.cloned.1.call-start = ((), (), s32[]{:S(2)}) async-start(), calls=%async_computation.2 | async-start | bytes 3833856 | tf_op jit(solution)/shard_map/reduce_scatter | solution.py:1227
  197.6 9.1 %collective-permute-start.27 = (f32[2,4096]{1,0:T(2,128)S(1)}, f32[2,4096]{1,0:T(2,128)S(1)}, u32[]{:S(2)}, u32[]{:S(2)}) collective-permute-start(f32[2,4096]{1,0:T(2,128)S(1)} %pad_maximum_fusion.7), channel_id=1, source_target_pairs={{0,8},{1,9},{2,10},{3,11},{4,12},{5,13},{6,14},{7,15},{8,0},{9,1},... | collective-permute-start | bytes 98312 | tf_op jit(solution)/shard_map/ppermute | solution.py:1048
  198.1 8.6 %collective-permute-start.28 = (f32[2,4096]{1,0:T(2,128)S(1)}, f32[2,4096]{1,0:T(2,128)S(1)}, u32[]{:S(2)}, u32[]{:S(2)}) collective-permute-start(f32[2,4096]{1,0:T(2,128)S(1)} %pad_maximum_fusion.7), channel_id=1, source_target_pairs={{0,16},{1,17},{2,18},{3,19},{4,20},{5,21},{6,22},{7,23},{8,24},{9,... | collective-permute-start | bytes 98312 | tf_op jit(solution)/shard_map/ppermute | solution.py:1048
  199.7 7.0 %collective-permute-start.29 = (f32[2,4096]{1,0:T(2,128)S(1)}, f32[2,4096]{1,0:T(2,128)S(1)}, u32[]{:S(2)}, u32[]{:S(2)}) collective-permute-start(f32[2,4096]{1,0:T(2,128)S(1)} %pad_maximum_fusion.7), channel_id=1, source_target_pairs={{0,24},{1,25},{2,26},{3,27},{4,28},{5,29},{6,30},{7,31},{8,16},{9,... | collective-permute-start | bytes 98312 | tf_op jit(solution)/shard_map/ppermute | solution.py:1048
  216.1 17.3 %collective-permute-start.37 = (bf16[8,9,32,512]{3,2,1,0:T(8,128)(2,1)}, bf16[8,9,32,512]{3,2,1,0:T(8,128)(2,1)S(1)}, u32[]{:S(2)}, u32[]{:S(2)}) collective-permute-start(bf16[8,9,32,512]{3,2,1,0:T(8,128)(2,1)} %pin.7.own_ref), channel_id=1, source_target_pairs={{0,1},{1,0},{2,3},{3,2},{4,5},{5,4},{6,7},{7,6},{8,9},{9,8},{10,11... | collective-permute-start | bytes 7077896 | tf_op jit(solution)/shard_map/ppermute | solution.py:1048
  224.2 7.0 %collective-permute-start.34 = (f32[2,512]{1,0:T(2,128)S(1)}, f32[2,512]{1,0:T(2,128)S(1)}, u32[]{:S(2)}, u32[]{:S(2)}) collective-permute-start(f32[2,512]{1,0:T(2,128)S(1)} %pad_maximum_fusion.22), channel_id=1, source_target_pairs={{0,8},{1,9},{2,10},{3,11},{4,12},{5,13},{6,14},{7,15},{8,0},{9,1},... | collective-permute-start | bytes 12296 | tf_op jit(solution)/shard_map/ppermute | solution.py:1048
  292.4 39.1 %collective-permute-start.59 = (bf16[8,128,2176]{2,1,0:T(8,128)(2,1)}, bf16[8,128,2176]{2,1,0:T(8,128)(2,1)}, u32[]{:S(2)}, u32[]{:S(2)}) collective-permute-start(bf16[8,128,2176]{2,1,0:T(8,128)(2,1)} %pin.8.own_ref), channel_id=1, source_target_pairs={{0,1},{1,0},{2,3},{3,2},{4,5},{5,4},{6,7},{7,6},{8,9},{9,8},{10,11... | collective-permute-start | bytes 13369352 | tf_op jit(solution)/shard_map/ppermute | solution.py:1048
  301.0 8.6 %collective-permute-start.53 = (bf16[16,2176]{1,0:T(8,128)(2,1)S(1)}, bf16[16,2176]{1,0:T(8,128)(2,1)S(1)}, u32[]{:S(2)}, u32[]{:S(2)}) collective-permute-start(bf16[16,2176]{1,0:T(8,128)(2,1)S(1)} %get-tuple-element.275), channel_id=1, source_target_pairs={{0,16},{1,17},{2,18},{3,19},{4,20},{5,21},{6,22},{7,23},{8,24},{9,... | collective-permute-start | bytes 208904 | tf_op jit(solution)/shard_map/ppermute | solution.py:1048
  302.6 7.0 %collective-permute-start.54 = (bf16[16,2176]{1,0:T(8,128)(2,1)S(1)}, bf16[16,2176]{1,0:T(8,128)(2,1)S(1)}, u32[]{:S(2)}, u32[]{:S(2)}) collective-permute-start(bf16[16,2176]{1,0:T(8,128)(2,1)S(1)} %get-tuple-element.275), channel_id=1, source_target_pairs={{0,24},{1,25},{2,26},{3,27},{4,28},{5,29},{6,30},{7,31},{8,16},{9,... | collective-permute-start | bytes 208904 | tf_op jit(solution)/shard_map/ppermute | solution.py:1048
  309.7 9.3 %collective-permute-start.55 = (bf16[4,16,2176]{2,1,0:T(8,128)(2,1)S(1)}, bf16[4,16,2176]{2,1,0:T(8,128)(2,1)S(1)}, u32[]{:S(2)}, u32[]{:S(2)}) collective-permute-start(bf16[4,16,2176]{2,1,0:T(8,128)(2,1)S(1)} %get-tuple-element.261), channel_id=1, source_target_pairs={{0,2},{1,3},{2,0},{3,1},{4,6},{5,7},{6,4},{7,5},{8,10},{9,11},{10,... | collective-permute-start | bytes 835592 | tf_op jit(solution)/shard_map/ppermute | solution.py:1048
  311.3 9.0 %collective-permute-start.56 = (bf16[4,16,2176]{2,1,0:T(8,128)(2,1)S(1)}, bf16[4,16,2176]{2,1,0:T(8,128)(2,1)S(1)}, u32[]{:S(2)}, u32[]{:S(2)}) collective-permute-start(bf16[4,16,2176]{2,1,0:T(8,128)(2,1)S(1)} %get-tuple-element.261), channel_id=1, source_target_pairs={{0,4},{1,5},{2,6},{3,7},{4,0},{5,1},{6,2},{7,3},{8,12},{9,13},{10,... | collective-permute-start | bytes 835592 | tf_op jit(solution)/shard_map/ppermute | solution.py:1048
  311.8 11.3 %collective-permute-start.57 = (bf16[4,16,2176]{2,1,0:T(8,128)(2,1)S(1)}, bf16[4,16,2176]{2,1,0:T(8,128)(2,1)S(1)}, u32[]{:S(2)}, u32[]{:S(2)}) collective-permute-start(bf16[4,16,2176]{2,1,0:T(8,128)(2,1)S(1)} %get-tuple-element.261), channel_id=1, source_target_pairs={{0,6},{1,7},{2,4},{3,5},{4,2},{5,3},{6,0},{7,1},{8,14},{9,15},{10,... | collective-permute-start | bytes 835592 | tf_op jit(solution)/shard_map/ppermute | solution.py:1048
  392.7 16.9 %collective-permute-start.74 = (bf16[8,128,512]{2,1,0:T(8,128)(2,1)}, bf16[8,128,512]{2,1,0:T(8,128)(2,1)S(1)}, u32[]{:S(2)}, u32[]{:S(2)}) collective-permute-start(bf16[8,128,512]{2,1,0:T(8,128)(2,1)} %get-tuple-element.118), channel_id=1, source_target_pairs={{0,1},{1,0},{2,3},{3,2},{4,5},{5,4},{6,7},{7,6},{8,9},{9,8},{10,11... | collective-permute-start | bytes 3145736 | tf_op jit(solution)/shard_map/ppermute | solution.py:1048
  426.9 17.5 %collective-permute-start.82 = (bf16[8,288,512]{2,1,0:T(8,128)(2,1)}, bf16[8,288,512]{2,1,0:T(8,128)(2,1)S(1)}, u32[]{:S(2)}, u32[]{:S(2)}) collective-permute-start(bf16[8,288,512]{2,1,0:T(8,128)(2,1)} %get-tuple-element.124), channel_id=1, source_target_pairs={{0,1},{1,0},{2,3},{3,2},{4,5},{5,4},{6,7},{7,6},{8,9},{9,8},{10,11... | collective-permute-start | bytes 7077896 | tf_op jit(solution)/shard_map/ppermute | solution.py:1048
  451.4 208.4 %reduce-scatter.5.cloned.1.call-start = ((), (), s32[]{:S(2)}) async-start(), calls=%async_computation.3 | async-start | bytes 4718592 | tf_op jit(solution)/shard_map/reduce_scatter | solution.py:1227
  465.7 20.0 %collective-permute-start.90 = (bf16[8,128,512]{2,1,0:T(8,128)(2,1)}, bf16[8,128,512]{2,1,0:T(8,128)(2,1)S(1)}, u32[]{:S(2)}, u32[]{:S(2)}) collective-permute-start(bf16[8,128,512]{2,1,0:T(8,128)(2,1)} %get-tuple-element.130), channel_id=1, source_target_pairs={{0,1},{1,0},{2,3},{3,2},{4,5},{5,4},{6,7},{7,6},{8,9},{9,8},{10,11... | collective-permute-start | bytes 3145736 | tf_op jit(solution)/shard_map/ppermute | solution.py:1048
  476.2 8.8 %collective-permute-start.88 = (f32[3,2048]{1,0:T(4,128)S(1)}, f32[3,2048]{1,0:T(4,128)S(1)}, u32[]{:S(2)}, u32[]{:S(2)}) collective-permute-start(f32[3,2048]{1,0:T(4,128)S(1)} %add.1130), channel_id=1, source_target_pairs={{0,16},{1,17},{2,18},{3,19},{4,20},{5,21},{6,22},{7,23},{8,24},{9,... | collective-permute-start | bytes 73736 | tf_op jit(solution)/shard_map/ppermute | solution.py:1048
  501.7 22.5 %collective-permute-start.99 = (bf16[8,256,512]{2,1,0:T(8,128)(2,1)}, bf16[8,256,512]{2,1,0:T(8,128)(2,1)S(1)}, u32[]{:S(2)}, u32[]{:S(2)}) collective-permute-start(bf16[8,256,512]{2,1,0:T(8,128)(2,1)} %get-tuple-element.139), channel_id=1, source_target_pairs={{0,1},{1,0},{2,3},{3,2},{4,5},{5,4},{6,7},{7,6},{8,9},{9,8},{10,11... | collective-permute-start | bytes 6291464 | tf_op jit(solution)/shard_map/ppermute | solution.py:1048
  506.5 17.7 %collective-permute-start.98 = (bf16[8,128,512]{2,1,0:T(8,128)(2,1)}, bf16[8,128,512]{2,1,0:T(8,128)(2,1)S(1)}, u32[]{:S(2)}, u32[]{:S(2)}) collective-permute-start(bf16[8,128,512]{2,1,0:T(8,128)(2,1)} %get-tuple-element.136), channel_id=1, source_target_pairs={{0,1},{1,0},{2,3},{3,2},{4,5},{5,4},{6,7},{7,6},{8,9},{9,8},{10,11... | collective-permute-start | bytes 3145736 | tf_op jit(solution)/shard_map/ppermute | solution.py:1048
  550.9 20.9 %collective-permute-start.107 = (bf16[4,4,9,16,512]{4,3,2,1,0:T(8,128)(2,1)}, bf16[4,4,9,16,512]{4,3,2,1,0:T(8,128)(2,1)S(1)}, u32[]{:S(2)}, u32[]{:S(2)}) collective-permute-start(bf16[4,4,9,16,512]{4,3,2,1,0:T(8,128)(2,1)} %get-tuple-element.145), channel_id=1, source_target_pairs={{0,1},{1,0},{2,3},{3,2},{4,5},{5,4},{6,7},{7,6},{8,9},{9,8},{10,11... | collective-permute-start | bytes 7077896 | tf_op jit(solution)/shard_map/ppermute | solution.py:1048
  567.2 65.0 %collective-permute-start.129 = (bf16[416,512]{1,0:T(8,128)(2,1)S(1)}, bf16[416,512]{1,0:T(8,128)(2,1)S(1)}, u32[]{:S(2)}, u32[]{:S(2)}) collective-permute-start(bf16[416,512]{1,0:T(8,128)(2,1)S(1)} %bitcast.88), channel_id=1, source_target_pairs={{0,2},{1,3},{2,0},{3,1},{4,6},{5,7},{6,4},{7,5},{8,10},{9,11},{10,... | collective-permute-start | bytes 1277960 | tf_op jit(solution)/shard_map/ppermute | solution.py:1048
  577.4 19.2 %collective-permute-start.109 = (bf16[4,9,16,512]{3,2,1,0:T(8,128)(2,1)}, bf16[4,9,16,512]{3,2,1,0:T(8,128)(2,1)S(1)}, u32[]{:S(2)}, u32[]{:S(2)}) collective-permute-start(bf16[4,9,16,512]{3,2,1,0:T(8,128)(2,1)} %get-tuple-element.152), channel_id=1, source_target_pairs={{0,2},{1,3},{2,0},{3,1},{4,6},{5,7},{6,4},{7,5},{8,10},{9,11},{10,... | collective-permute-start | bytes 1769480 | tf_op jit(solution)/shard_map/ppermute | solution.py:1048
  578.2 23.1 %collective-permute-start.110 = (bf16[4,9,16,512]{3,2,1,0:T(8,128)(2,1)}, bf16[4,9,16,512]{3,2,1,0:T(8,128)(2,1)S(1)}, u32[]{:S(2)}, u32[]{:S(2)}) collective-permute-start(bf16[4,9,16,512]{3,2,1,0:T(8,128)(2,1)} %get-tuple-element.153), channel_id=1, source_target_pairs={{0,4},{1,5},{2,6},{3,7},{4,0},{5,1},{6,2},{7,3},{8,12},{9,13},{10,... | collective-permute-start | bytes 1769480 | tf_op jit(solution)/shard_map/ppermute | solution.py:1048
  579.7 34.0 %collective-permute-start.111 = (bf16[4,9,16,512]{3,2,1,0:T(8,128)(2,1)}, bf16[4,9,16,512]{3,2,1,0:T(8,128)(2,1)S(1)}, u32[]{:S(2)}, u32[]{:S(2)}) collective-permute-start(bf16[4,9,16,512]{3,2,1,0:T(8,128)(2,1)} %get-tuple-element.154), channel_id=1, source_target_pairs={{0,6},{1,7},{2,4},{3,5},{4,2},{5,3},{6,0},{7,1},{8,14},{9,15},{10,... | collective-permute-start | bytes 1769480 | tf_op jit(solution)/shard_map/ppermute | solution.py:1048
  616.5 7.1 %collective-permute-start.112 = (bf16[4,32,512]{2,1,0:T(8,128)(2,1)}, bf16[4,32,512]{2,1,0:T(8,128)(2,1)S(1)}, u32[]{:S(2)}, u32[]{:S(2)}) collective-permute-start(bf16[4,32,512]{2,1,0:T(8,128)(2,1)} %get-tuple-element.156), channel_id=1, source_target_pairs={{0,2},{1,3},{2,0},{3,1},{4,6},{5,7},{6,4},{7,5},{8,10},{9,11},{10,... | collective-permute-start | bytes 393224 | tf_op jit(solution)/shard_map/ppermute | solution.py:1048
  617.0 8.3 %collective-permute-start.113 = (bf16[4,32,512]{2,1,0:T(8,128)(2,1)}, bf16[4,32,512]{2,1,0:T(8,128)(2,1)S(1)}, u32[]{:S(2)}, u32[]{:S(2)}) collective-permute-start(bf16[4,32,512]{2,1,0:T(8,128)(2,1)} %get-tuple-element.157), channel_id=1, source_target_pairs={{0,4},{1,5},{2,6},{3,7},{4,0},{5,1},{6,2},{7,3},{8,12},{9,13},{10,... | collective-permute-start | bytes 393224 | tf_op jit(solution)/shard_map/ppermute | solution.py:1048
  617.6 8.3 %collective-permute-start.114 = (bf16[4,32,512]{2,1,0:T(8,128)(2,1)}, bf16[4,32,512]{2,1,0:T(8,128)(2,1)S(1)}, u32[]{:S(2)}, u32[]{:S(2)}) collective-permute-start(bf16[4,32,512]{2,1,0:T(8,128)(2,1)} %get-tuple-element.158), channel_id=1, source_target_pairs={{0,6},{1,7},{2,4},{3,5},{4,2},{5,3},{6,0},{7,1},{8,14},{9,15},{10,... | collective-permute-start | bytes 393224 | tf_op jit(solution)/shard_map/ppermute | solution.py:1048
  622.7 26.6 %collective-permute-start.121 = (bf16[9,16,512]{2,1,0:T(8,128)(2,1)}, bf16[9,16,512]{2,1,0:T(8,128)(2,1)S(1)}, u32[]{:S(2)}, u32[]{:S(2)}) collective-permute-start(bf16[9,16,512]{2,1,0:T(8,128)(2,1)} %get-tuple-element.164), channel_id=1, source_target_pairs={{0,8},{1,9},{2,10},{3,11},{4,12},{5,13},{6,14},{7,15},{8,0},{9,1},... | collective-permute-start | bytes 442376 | tf_op jit(solution)/shard_map/ppermute | solution.py:1048
  623.6 27.2 %collective-permute-start.122 = (bf16[9,16,512]{2,1,0:T(8,128)(2,1)}, bf16[9,16,512]{2,1,0:T(8,128)(2,1)S(1)}, u32[]{:S(2)}, u32[]{:S(2)}) collective-permute-start(bf16[9,16,512]{2,1,0:T(8,128)(2,1)} %get-tuple-element.165), channel_id=1, source_target_pairs={{0,16},{1,17},{2,18},{3,19},{4,20},{5,21},{6,22},{7,23},{8,24},{9,... | collective-permute-start | bytes 442376 | tf_op jit(solution)/shard_map/ppermute | solution.py:1048
  628.4 9.2 %collective-permute-start.115 = (bf16[32,512]{1,0:T(8,128)(2,1)}, bf16[32,512]{1,0:T(8,128)(2,1)S(1)}, u32[]{:S(2)}, u32[]{:S(2)}) collective-permute-start(bf16[32,512]{1,0:T(8,128)(2,1)} %get-tuple-element.160), channel_id=1, source_target_pairs={{0,8},{1,9},{2,10},{3,11},{4,12},{5,13},{6,14},{7,15},{8,0},{9,1},... | collective-permute-start | bytes 98312 | tf_op jit(solution)/shard_map/ppermute | solution.py:1048
  629.9 24.6 %collective-permute-start.123 = (bf16[9,16,512]{2,1,0:T(8,128)(2,1)}, bf16[9,16,512]{2,1,0:T(8,128)(2,1)S(1)}, u32[]{:S(2)}, u32[]{:S(2)}) collective-permute-start(bf16[9,16,512]{2,1,0:T(8,128)(2,1)} %get-tuple-element.166), channel_id=1, source_target_pairs={{0,24},{1,25},{2,26},{3,27},{4,28},{5,29},{6,30},{7,31},{8,16},{9,... | collective-permute-start | bytes 442376 | tf_op jit(solution)/shard_map/ppermute | solution.py:1048
  632.3 14.4 %collective-permute-start.116 = (bf16[32,512]{1,0:T(8,128)(2,1)}, bf16[32,512]{1,0:T(8,128)(2,1)S(1)}, u32[]{:S(2)}, u32[]{:S(2)}) collective-permute-start(bf16[32,512]{1,0:T(8,128)(2,1)} %get-tuple-element.161), channel_id=1, source_target_pairs={{0,16},{1,17},{2,18},{3,19},{4,20},{5,21},{6,22},{7,23},{8,24},{9,... | collective-permute-start | bytes 98312 | tf_op jit(solution)/shard_map/ppermute | solution.py:1048
  637.6 9.1 %collective-permute-start.117 = (bf16[32,512]{1,0:T(8,128)(2,1)}, bf16[32,512]{1,0:T(8,128)(2,1)S(1)}, u32[]{:S(2)}, u32[]{:S(2)}) collective-permute-start(bf16[32,512]{1,0:T(8,128)(2,1)} %get-tuple-element.162), channel_id=1, source_target_pairs={{0,24},{1,25},{2,26},{3,27},{4,28},{5,29},{6,30},{7,31},{8,16},{9,... | collective-permute-start | bytes 98312 | tf_op jit(solution)/shard_map/ppermute | solution.py:1048
  646.7 14.6 %collective-permute-start.130 = (bf16[416,512]{1,0:T(8,128)(2,1)}, bf16[416,512]{1,0:T(8,128)(2,1)S(1)}, u32[]{:S(2)}, u32[]{:S(2)}) collective-permute-start(bf16[416,512]{1,0:T(8,128)(2,1)} %fold.19), channel_id=1, source_target_pairs={{0,1},{1,0},{2,3},{3,2},{4,5},{5,4},{6,7},{7,6},{8,9},{9,8},{10,11... | collective-permute-start | bytes 1277960 | tf_op jit(solution)/shard_map/ppermute | solution.py:1048
  648.7 8.8 %collective-permute-start.118 = (bf16[32,512]{1,0:T(8,128)(2,1)}, bf16[32,512]{1,0:T(8,128)(2,1)S(1)}, u32[]{:S(2)}, u32[]{:S(2)}) collective-permute-start(bf16[32,512]{1,0:T(8,128)(2,1)} %fold.14), channel_id=1, source_target_pairs={{0,1},{1,0},{2,3},{3,2},{4,5},{5,4},{6,7},{7,6},{8,9},{9,8},{10,11... | collective-permute-start | bytes 98312 | tf_op jit(solution)/shard_map/ppermute | solution.py:1048
  649.3 9.8 %collective-permute-start.119 = (bf16[32,512]{1,0:T(8,128)(2,1)}, bf16[32,512]{1,0:T(8,128)(2,1)S(1)}, u32[]{:S(2)}, u32[]{:S(2)}) collective-permute-start(bf16[32,512]{1,0:T(8,128)(2,1)} %fold.14), channel_id=1, source_target_pairs={{0,2},{1,3},{2,0},{3,1},{4,6},{5,7},{6,4},{7,5},{8,10},{9,11},{10,... | collective-permute-start | bytes 98312 | tf_op jit(solution)/shard_map/ppermute | solution.py:1048
  650.7 8.3 %collective-permute-start.120 = (bf16[32,512]{1,0:T(8,128)(2,1)}, bf16[32,512]{1,0:T(8,128)(2,1)S(1)}, u32[]{:S(2)}, u32[]{:S(2)}) collective-permute-start(bf16[32,512]{1,0:T(8,128)(2,1)} %fold.14), channel_id=1, source_target_pairs={{0,3},{1,2},{2,1},{3,0},{4,7},{5,6},{6,5},{7,4},{8,11},{9,10},{10,... | collective-permute-start | bytes 98312 | tf_op jit(solution)/shard_map/ppermute | solution.py:1048
  657.0 24.9 %collective-permute-start.124 = (bf16[9,16,512]{2,1,0:T(8,128)(2,1)}, bf16[9,16,512]{2,1,0:T(8,128)(2,1)S(1)}, u32[]{:S(2)}, u32[]{:S(2)}) collective-permute-start(bf16[9,16,512]{2,1,0:T(8,128)(2,1)} %fold.16), channel_id=1, source_target_pairs={{0,1},{1,0},{2,3},{3,2},{4,5},{5,4},{6,7},{7,6},{8,9},{9,8},{10,11... | collective-permute-start | bytes 442376 | tf_op jit(solution)/shard_map/ppermute | solution.py:1048
  657.6 24.2 %collective-permute-start.125 = (bf16[9,16,512]{2,1,0:T(8,128)(2,1)}, bf16[9,16,512]{2,1,0:T(8,128)(2,1)S(1)}, u32[]{:S(2)}, u32[]{:S(2)}) collective-permute-start(bf16[9,16,512]{2,1,0:T(8,128)(2,1)} %fold.16), channel_id=1, source_target_pairs={{0,2},{1,3},{2,0},{3,1},{4,6},{5,7},{6,4},{7,5},{8,10},{9,11},{10,... | collective-permute-start | bytes 442376 | tf_op jit(solution)/shard_map/ppermute | solution.py:1048
  659.1 22.8 %collective-permute-start.126 = (bf16[9,16,512]{2,1,0:T(8,128)(2,1)}, bf16[9,16,512]{2,1,0:T(8,128)(2,1)S(1)}, u32[]{:S(2)}, u32[]{:S(2)}) collective-permute-start(bf16[9,16,512]{2,1,0:T(8,128)(2,1)} %fold.16), channel_id=1, source_target_pairs={{0,3},{1,2},{2,1},{3,0},{4,7},{5,6},{6,5},{7,4},{8,11},{9,10},{10,... | collective-permute-start | bytes 442376 | tf_op jit(solution)/shard_map/ppermute | solution.py:1048
  659.8 18.2 %collective-permute-start.127 = (bf16[512,512]{1,0:T(8,128)(2,1)}, bf16[512,512]{1,0:T(8,128)(2,1)S(1)}, u32[]{:S(2)}, u32[]{:S(2)}) collective-permute-start(bf16[512,512]{1,0:T(8,128)(2,1)} %bitcast.99), channel_id=1, source_target_pairs={{0,2},{1,3},{2,0},{3,1},{4,6},{5,7},{6,4},{7,5},{8,10},{9,11},{10,... | collective-permute-start | bytes 1572872 | tf_op jit(solution)/shard_map/ppermute | solution.py:1048
  (166 other events, 807.4 us)
Sparse Core Ops, SparseCore 0:
  10.8 59.2 all-gather.8
  72.8 84.6 all-gather.10
  160.2 52.3 all-gather.12
  215.3 77.0 all-gather.14
  451.6 78.4 reduce-scatter.2
  534.0 103.6 reduce-scatter.4

commit v3 on v2

--- a/solution.py
+++ b/solution.py
@@ -77,6 +77,40 @@
     return (shape, dtype, shape[:-1] + (width,), lambda i: (0,) * (len(shape) - 1) + (i,))
 
 
+class Packed:
+    PARTS = 32
+
+    def __init__(self, buffer, base, rows, steps):
+        self.buffer, self.base, self.rows, self.steps = buffer, base, rows, steps
+
+    def column_tile(self):
+        rows, first = self.rows, self.base // self.rows
+        return self.buffer, (self.PARTS, rows, 512), lambda i: (0, first + i, 0)
+
+    def row_tile(self):
+        rows, first = self.rows, self.base // self.rows
+        return self.buffer, (512 // rows, rows, 512), lambda i: (i, first, 0)
+
+    def taps_by_column(self, tile):
+        rows = self.rows * self.steps
+        first = self.base // rows
+        return self.buffer, (self.PARTS, rows, tile), lambda i: (0, first, i)
+
+    def taps_by_row(self, tile):
+        rows = self.rows * self.steps
+        first = self.base // rows
+        return self.buffer, (tile // self.rows, rows, 512), lambda i: (i, first, 0)
+
+
+def flat(ref):
+    return ref[...].reshape(-1, ref.shape[-1])
+
+
+def tap_of(ref, tap):
+    rows = ref.shape[1] // 9
+    return ref[:, tap * rows : (tap + 1) * rows, :].reshape(-1, ref.shape[2])
+
+
 def sigmoid(v):
     return 1.0 / (1.0 + jnp.exp(-v))
 
@@ -225,18 +259,17 @@
     blocks = []
     for at in range(0, out_ref.shape[0], f.rows):
         block = out_ref.at[at : at + f.rows, :]
-        block[...] = dot(x_ref[at : at + f.rows, :], w_ref[...])
+        block[...] = dot(x_ref[at : at + f.rows, :], flat(w_ref))
         blocks.append(block)
     store_stats(stats_ref, blocks, mask, count)
 
 
-def linear(f, x, w, mask, phases, width, after=()):
-    n = w.shape[1]
+def linear(f, x, w_in, n, mask, phases, width, after=()):
     x_in = (x, (phases * f.rows, x.shape[1]), lambda i: (0, 0))
     return call(
         functools.partial(linear_kernel, f, phases * f.valid),
         (n // width,),
-        [x_in, cols(w, width), whole(mask)],
+        [x_in, w_in, whole(mask)],
         [out_cols((phases * f.rows, n), F32, width), out_cols((2, n), F32, width)],
         us=6,
         after=after,
@@ -271,17 +304,21 @@
                 act.at[phase], *step
             ).astype(BF16)
 
-    out_ref[...] = dot(patch_ref[...], w_ref[...])
+    total = None
+    for tap in range(9):
+        part = dot(patch_ref[:, tap * width : (tap + 1) * width], tap_of(w_ref, tap))
+        total = part if total is None else total + part
+    out_ref[...] = total
     store_stats(new_ref, [out_ref], spread(mask_ref[...], out_ref.shape[1]), f.valid)
 
 
 def conv(f, stride, count, pre, stats, affine, w, mask, tile=256, after=()):
-    c, n = pre.shape[1], w.shape[1]
+    c = n = pre.shape[1]
     phases = stride * stride
     return call(
         functools.partial(conv_kernel, f, stride, count),
         (n // tile,),
-        [whole(pre), whole(stats), whole(affine), cols(w, tile), whole(mask)],
+        [whole(pre), whole(stats), whole(affine), w.taps_by_column(tile), whole(mask)],
         [
             out_whole((f.rows, 9 * c), BF16),
             out_cols((f.rows, n), F32, tile),
@@ -300,16 +337,16 @@
         v = norm.scaled(norm.hat(pre_ref[...]))
         low_ref[...] = (v * sigmoid(v) * spread(mask_ref[...], v.shape[1])).astype(BF16)
 
-    out_ref[...] = dot(low_ref[...], w_ref[...])
+    out_ref[...] = dot(low_ref[...], flat(w_ref))
     store_stats(new_ref, [out_ref], spread(mask_ref[...], out_ref.shape[1]), f.valid)
 
 
 def expand(f, count, pre, stats, affine, w, mask, tile=512, after=()):
-    c, n = w.shape
+    c, n = pre.shape[1], w.steps * tile
     return call(
         functools.partial(expand_kernel, f, count),
         (n // tile,),
-        [whole(pre), whole(stats), whole(affine), cols(w, tile), whole(mask)],
+        [whole(pre), whole(stats), whole(affine), w.column_tile(), whole(mask)],
         [
             out_whole((f.rows, c), BF16),
             out_cols((f.rows, n), F32, tile),
@@ -332,7 +369,7 @@
     pre_ref[...] = v
     low = (v * sigmoid(v) * mask).astype(BF16)
     low_ref[...] = low
-    part = dot(low, w_ref[...])
+    part = dot(low, flat(w_ref))
 
     @pl.when(step == 0)
     def _():
@@ -348,12 +385,12 @@
 
 
 def mix(f, count, expanded, skipped, stats_a, affine_a, stats_b, affine_b, w, mask, tile=512, after=()):
-    k, n = w.shape
+    k, n = expanded.shape[1], 512
     return call(
         functools.partial(mix_kernel, f, count),
         (k // tile,),
         [cols(a, tile) for a in (expanded, skipped, stats_a, affine_a, stats_b, affine_b)]
-        + [rows(w, tile), whole(mask)],
+        + [w.row_tile(), whole(mask)],
         [
             out_cols((f.rows, k), BF16, tile),
             out_cols((f.rows, k), F32, tile),
@@ -576,7 +613,7 @@
     d = f.to_rows(back_ref[...]) * slope_ref[...]
     low = (norm.backward(d, hat, sums_ref) * spread(mask_ref[...], hat.shape[1])).astype(BF16)
     low_ref[...] = low
-    finish_back(step, dot(low, w_ref[...], NT), turn_ref, turn_stats, turn_affine, count, mask_ref, out_ref, new_ref)
+    finish_back(step, dot(low, flat(w_ref), NT), turn_ref, turn_stats, turn_affine, count, mask_ref, out_ref, new_ref)
 
 
 def finish_back(step, part, pre_ref, stats, affine, count, mask_ref, out_ref, new_ref):
@@ -599,11 +636,12 @@
 
 
 def widen_back(f, count, wide, slopes, back, stats, affine, sums, w, turn, tstats, taffine, mask, tile=512, after=()):
-    c, n = w.shape
+    c, n = turn.shape[1], w.steps * tile
     return call(
         functools.partial(widen_back_kernel, f, count),
         (n // tile,),
-        [cols(a, tile) for a in (wide, slopes, back, stats, affine, sums, w)]
+        [cols(a, tile) for a in (wide, slopes, back, stats, affine, sums)]
+        + [w.column_tile()]
         + [whole(a) for a in (turn, tstats, taffine, mask)],
         [
             out_cols((f.rows, n), BF16, tile),
@@ -649,7 +687,7 @@
                 step = (int(p == 0), int(q == 0))
             else:
                 step = (1 - p, 1 - q)
-            part = dot(moved[steps.index(step)], w_ref[tap], NT)
+            part = dot(moved[steps.index(step)], tap_of(w_ref, tap), NT)
             acc = part if acc is None else acc + part
         at = phase * f.rows
         hat = norm.hat(in_ref[at : at + f.rows, :])
@@ -662,14 +700,13 @@
 
 
 def conv_back(f, stride, count, in_count, d, pre, stats, affine, sums, w, inside, istats, iaffine, mask, tile=256, after=()):
-    n = d.shape[1]
-    c = w.shape[1]
+    c = n = d.shape[1]
     phases = stride * stride
     return call(
         functools.partial(conv_back_kernel, f, stride, count, in_count),
         (c // tile,),
         [whole(a) for a in (d, pre, stats, affine, sums)]
-        + [(w, (9, tile, n), lambda i: (0, i, 0))]
+        + [w.taps_by_row(tile)]
         + [cols(a, tile) for a in (inside, istats, iaffine)]
         + [whole(mask)],
         [
@@ -698,7 +735,7 @@
         d = norm.backward(d_ref[...], hat, sums_ref)
         low_ref[...] = (d * spread(mask_ref[...], hat.shape[1])).astype(BF16)
 
-    g = f.to_rows(back_ref[...]) * slope_ref[...] + dot(low_ref[...], w_ref[...], NT)
+    g = f.to_rows(back_ref[...]) * slope_ref[...] + dot(low_ref[...], flat(w_ref), NT)
     g = g * slope(pre_ref[...]) * spread(mask_ref[...], g.shape[1])
     out_ref[...] = g
     first = Norm(exp_stats, exp_affine, count)
@@ -711,12 +748,12 @@
 def mix_back(
     f, count, d, mixing, stats, affine, sums, w, back, slopes, pre,
     expanded, estats, eaffine, skipped, sstats, saffine, mask, tile=512, after=()):
-    n, c = w.shape
+    n, c = expanded.shape[1], d.shape[1]
     return call(
         functools.partial(mix_back_kernel, f, count),
         (n // tile,),
         [whole(a) for a in (d, mixing, stats, affine, sums)]
-        + [rows(w, tile)]
+        + [w.row_tile()]
         + [cols(a, tile) for a in (back, slopes, pre, expanded, estats, eaffine, skipped, sstats, saffine)]
         + [whole(mask)],
         [
@@ -744,7 +781,7 @@
     other = jnp.concatenate([sums[0:1], sums[2:3]], 0)
     skip_low[...] = (second.backward(g, second.hat(skip_ref[...]), other) * mask).astype(BF16)
     finish_back(
-        pl.program_id(0), dot(low, w_ref[...], NT), turn_ref, turn_stats, turn_affine,
+        pl.program_id(0), dot(low, flat(w_ref), NT), turn_ref, turn_stats, turn_affine,
         count, mask_ref, out_ref, new_ref,
     )
 
@@ -752,11 +789,12 @@
 def block_back(
     f, count, g, expanded, estats, eaffine, skipped, sstats, saffine, sums, w,
     turned, tstats, taffine, mask, tile=512, after=()):
-    c, n = w.shape
+    c, n = turned.shape[1], w.steps * tile
     return call(
         functools.partial(block_back_kernel, f, count),
         (n // tile,),
-        [cols(a, tile) for a in (g, expanded, estats, eaffine, skipped, sstats, saffine, sums, w)]
+        [cols(a, tile) for a in (g, expanded, estats, eaffine, skipped, sstats, saffine, sums)]
+        + [w.column_tile()]
         + [whole(a) for a in (turned, tstats, taffine, mask)],
         [
             out_cols((f.rows, n), BF16, tile),
@@ -769,20 +807,51 @@
     )
 
 
-def input_back_kernel(
-    f, count, d_ref, pre_ref, stats_ref, affine_ref, sums_ref, w_ref, sub_ref, mask_ref,
-    low_ref, large_ref, small_ref, lt, st, acc,
-):
+def sub_kernel(low_ref, w_ref, out_ref):
+    part = dot(low_ref[...], flat(w_ref), NT)
+
     @pl.when(pl.program_id(0) == 0)
     def _():
-        norm = Norm(stats_ref, affine_ref, count)
-        mask = spread(mask_ref[...], d_ref.shape[1])
-        for phase in range(4):
-            at = phase * f.rows
-            hat = norm.hat(pre_ref[at : at + f.rows, :])
-            d = norm.backward(d_ref[at : at + f.rows, :], hat, sums_ref)
-            low_ref[at : at + f.rows, :] = (d * mask).astype(BF16)
-
+        out_ref[...] = part
+
+    @pl.when(pl.program_id(0) > 0)
+    def _():
+        out_ref[...] += part
+
+
+def sub_back(low, w, c, tile=512, after=()):
+    return call(
+        functools.partial(sub_kernel),
+        (w.steps,),
+        [cols(low, tile), w.column_tile()],
+        [out_whole((low.shape[0], c), F32)],
+        us=0.1,
+        after=after,
+    )[0]
+
+
+def input_low_kernel(f, count, d_ref, pre_ref, stats_ref, affine_ref, sums_ref, mask_ref, low_ref):
+    norm = Norm(stats_ref, affine_ref, count)
+    mask = spread(mask_ref[...], d_ref.shape[1])
+    for phase in range(4):
+        at = phase * f.rows
+        hat = norm.hat(pre_ref[at : at + f.rows, :])
+        d = norm.backward(d_ref[at : at + f.rows, :], hat, sums_ref)
+        low_ref[at : at + f.rows, :] = (d * mask).astype(BF16)
+
+
+def input_low(f, count, d, pre, stats, affine, sums, mask, tile=256, after=()):
+    return call(
+        functools.partial(input_low_kernel, f, count),
+        (d.shape[1] // tile,),
+        [cols(a, tile) for a in (d, pre, stats, affine, sums)] + [whole(mask)],
+        [out_cols(d.shape, BF16, tile)],
+        us=0.1,
+        after=after,
+    )[0]
+
+
+def input_back_kernel(f, low_ref, w_ref, sub_ref, large_ref, small_ref, lt, st, acc):
     for phase in range(4):
         at = phase * f.rows
         part = dot(low_ref[at : at + f.rows, :], w_ref[...], NT)
@@ -797,20 +866,18 @@
         small_ref[:, :, :, lane] = st[k, :, :, 0 : f.small_in, :].astype(BF16)
 
 
-def input_back(f, count, d, pre, stats, affine, sums, w, sub, mask, tile=256, after=()):
+def input_back(f, low, w, sub, tile=256, after=()):
     n, c = w.shape
     return call(
-        functools.partial(input_back_kernel, f, count),
+        functools.partial(input_back_kernel, f),
         (n // tile,),
-        [whole(a) for a in (d, pre, stats, affine, sums)]
-        + [rows(w, tile), cols(sub, tile), whole(mask)],
+        [whole(low), rows(w, tile), cols(sub, tile)],
         [
-            out_whole((4 * f.rows, c), BF16),
             out_cols((f.large, f.large_in, f.large_in, n), BF16, tile),
             out_cols((f.small, f.small_in, f.small_in, n), BF16, tile),
         ],
         parity_scratch(f, tile),
-        us=8.4,
+        us=0.1,
         after=after,
     )
 
@@ -845,81 +912,29 @@
     )(place, own, other, *after)
 
 
-def join_kernel(at, half, split, folds, place_ref, own_ref, other_ref, out_ref, sems):
-    copies = []
-    pieces = split * folds
-    rows = half // pieces
-    for m in range(16 * pieces):
-        piece, c, k = m % pieces, m // pieces % 2, m // (2 * pieces)
-        src = (other_ref if c else own_ref).at[k]
-        row = (2 * k + ((place_ref[1] % 2) ^ c)) * half + piece * rows
-        there = pl.ds(pl.multiple_of(row, 16), rows)
-        fold, part = piece // split, piece % split
-        here = pl.ds(at + part * rows, rows)
-        if folds > 1:
-            width = out_ref.shape[-1]
-            src, dst = src.at[here, pl.ds(fold * width, width)], out_ref.at[there, :]
-        elif len(src.shape) == 2:
-            src, dst = src.at[here, :], out_ref.at[there, :]
-        else:
-            src, dst = src.at[:, here, :], out_ref.at[:, there, :]
-        copies.append(pltpu.make_async_copy(src, dst, sems.at[m]))
-    for copy in copies:
-        copy.start()
-    for copy in copies:
-        copy.wait()
-
-
-def join_halves(place, own, other, at, half, folds):
-    block = own.shape[1:]
-    split = 1 if folds > 1 else 2
-    shape = block[:-2] + (16 * half, block[-1] // folds)
-    return pl.pallas_call(
-        functools.partial(join_kernel, at, half, split, folds),
-        name="join_halves",
-        in_specs=[IN_SMEM, IN_PLACE, IN_PLACE],
-        out_specs=IN_PLACE,
-        out_shape=jax.ShapeDtypeStruct(shape, own.dtype),
-        scratch_shapes=[pltpu.SemaphoreType.DMA((16 * split * folds,))],
-        compiler_params=pltpu.CompilerParams(vmem_limit_bytes=4 * 1024 * 1024),
-        cost_estimate=cost(4),
-    )(place, own, other)
-
-
-def half_kernel(place_ref, *refs):
+def pack_kernel(bases, place_ref, *refs):
     shards, out_ref = refs[:-1], refs[-1]
-    base = 0
-    for shard in shards:
-        half = shard.shape[-2] // 2
-        at = pl.multiple_of(place_ref[1] % 2 * half, 16)
-        if len(shard.shape) == 3:
-            out_ref[...] = shard[:, pl.ds(at, half), :]
-            continue
-        width = shard.shape[1]
-        folds = out_ref.shape[1] // width
-        rows = half // folds
-        for fold in range(folds):
-            value = shard[pl.ds(pl.multiple_of(at + fold * rows, 16), rows), :]
-            out_ref[base : base + rows, fold * width : (fold + 1) * width] = value
-        base += rows
-
-
-def half_of(place, shards, after=()):
-    shape = shards[0].shape
-    if len(shape) == 2:
-        width = max(s.shape[1] for s in shards)
-        shape = (sum(s.size for s in shards) // (2 * width), width)
-    else:
-        shape = (shape[0], shape[1] // 2, shape[2])
+    out_ref[...] = jnp.zeros_like(out_ref)
+    for base, shard in zip(bases, shards):
+        rows = shard.shape[-2] // 4
+        at = pl.ds(pl.multiple_of(place_ref[1] * rows, 16), rows)
+        by_tap = len(shard.shape) == 3
+        for k in range(shard.shape[0] if by_tap else shard.shape[1] // out_ref.shape[1]):
+            width = out_ref.shape[1]
+            value = shard[k, at, :] if by_tap else shard[at, k * width : (k + 1) * width]
+            out_ref[base + k * rows : base + (k + 1) * rows, :] = value
+
+
+def pack(place, shards, bases, shape, after=()):
     in_vmem = pl.BlockSpec(memory_space=pltpu.VMEM)
     return pl.pallas_call(
-        skipping(half_kernel, 1 + len(shards), len(after)),
-        name="half",
+        skipping(functools.partial(pack_kernel, bases), 1 + len(shards), len(after)),
+        name="pack",
         in_specs=[IN_SMEM] + [in_vmem] * len(shards) + [IN_PLACE] * len(after),
         out_specs=in_vmem,
         out_shape=jax.ShapeDtypeStruct(shape, BF16),
         compiler_params=pltpu.CompilerParams(vmem_limit_bytes=VMEM_LIMIT),
-        cost_estimate=cost(1.5),
+        cost_estimate=cost(2),
     )(place, *shards, *after)
 
 
@@ -952,6 +967,35 @@
     )(place, *shards, *after)
 
 
+def unpack_kernel(kinds, place_ref, own_ref, other_ref, *outs):
+    core = place_ref[1] % 2
+    for ref, c in ((own_ref, core), (other_ref, 1 - core)):
+        at = 0
+        for (steps, rows, by_tap), out in zip(kinds, outs):
+            there = pl.ds(pl.multiple_of(c * rows, 16), rows)
+            for k in range(steps):
+                value = ref[at : at + rows, :].astype(F32)
+                if by_tap:
+                    out[k, there, :] = value
+                else:
+                    out[there, k * 512 : (k + 1) * 512] = value
+                at += rows
+
+
+def unpack(place, own, other, kinds):
+    in_vmem = pl.BlockSpec(memory_space=pltpu.VMEM)
+    shapes = [(n, 2 * r, 512) if by_tap else (2 * r, n * 512) for n, r, by_tap in kinds]
+    return pl.pallas_call(
+        functools.partial(unpack_kernel, kinds),
+        name="unpack",
+        in_specs=[IN_SMEM, in_vmem, in_vmem],
+        out_specs=[in_vmem] * len(kinds),
+        out_shape=[jax.ShapeDtypeStruct(s, F32) for s in shapes],
+        compiler_params=pltpu.CompilerParams(vmem_limit_bytes=VMEM_LIMIT),
+        cost_estimate=cost(2),
+    )(place, own, other)
+
+
 def local_kernel(function, number, *refs):
     ins, outs = refs[:number], refs[number:]
     for out, value in zip(outs, function(*[r[...] for r in ins])):
@@ -992,22 +1036,24 @@
     )(v, *after)
 
 
-def weight_kernel(by_tap, rows, parts, place_ref, left_ref, right_ref, keep_ref, send_ref, acc):
+def weight_kernel(by_tap, rows, halves, place_ref, left_ref, right_ref, keep_ref, send_ref, acc):
     acc[...] = dot(left_ref[...], right_ref[...], TN)
-    for m in range(parts):
-        if parts == 32:
+    for m in range(32):
+        if halves:
+            if m >= 16:
+                break
+            img, c = m >> 1, m & 1
+            at, place = img * 2 + ((place_ref[1] % 2) ^ c), (img,)
+        else:
             at, c, place = place_ref[2] ^ m, m & 1, ((m >> 1) & 3, m >> 3)
             place = place + (0,) if by_tap else place
-        else:
-            at, c, place = (m & ~1) + ((place_ref[1] % 2) ^ (m & 1)), m & 1, (m >> 1,)
         block = acc[pl.ds(pl.multiple_of(at * rows, 16), rows), :].astype(BF16)
         (send_ref if c else keep_ref)[place] = block
 
 
-def weight_grad(place, left, right, taps=1, halves=False, tile=512):
+def weight_grad(place, left, right, taps=1, halves=False, us=None, tile=512):
     k, n = left.shape[1] // taps, right.shape[1]
-    parts = 16 if halves else 32
-    rows = k // parts
+    rows = k // (16 if halves else 32)
     if taps == 1:
         steps = n // tile
         left_in = (right.shape[0], k), lambda i: (0, 0)
@@ -1024,7 +1070,7 @@
         shape, block = (8, steps * rows, tile), (8, rows, tile)
         out_map = lambda i: (0, i, 0)
     return pl.pallas_call(
-        functools.partial(weight_kernel, taps > 1, rows, parts),
+        functools.partial(weight_kernel, taps > 1, rows, halves),
         name="weight_grad",
         grid=(steps,),
         in_specs=[IN_SMEM, pl.BlockSpec(*left_in), pl.BlockSpec(*right_in)],
@@ -1032,7 +1078,7 @@
         out_shape=[jax.ShapeDtypeStruct(shape, BF16)] * 2,
         scratch_shapes=[pltpu.VMEM((k, tile), F32)],
         compiler_params=pltpu.CompilerParams(vmem_limit_bytes=VMEM_LIMIT),
-        cost_estimate=cost(10 if taps > 1 else 5),
+        cost_estimate=cost(us or (10 if taps > 1 else 5)),
     )(place, left, right)
 
 
@@ -1070,7 +1116,16 @@
         return [self.swap(v, a), self.swap(v, b), self.swap(v, a | b)]
 
     def total(self, v):
-        for stage in self.stages():
+        return self.end_total(self.begin_total(v))
+
+    def begin_total(self, v):
+        return self.add_stages(v, self.stages()[:1])
+
+    def end_total(self, v):
+        return self.add_stages(v, self.stages()[1:])
+
+    def add_stages(self, v, stages):
+        for stage in stages:
             got = self.partners(v, stage)
             if len(got) == 1:
                 v = v + got[0]
@@ -1136,54 +1191,54 @@
 class Weights:
     def __init__(self, links, place, staged, shards):
         self.links, self.place, self.staged, self.shards = links, place, staged, shards
-        self.now, self.halves = {}, {}
-
-    def cut(self, names, after=()):
+        self.now = {}
+
+    def whole(self, name):
+        shard = self.shards[name]
+        return lax.all_gather(shard, "img", axis=shard.ndim - 2, tiled=True)
+
+    def first(self, name, during):
+        if not self.staged:
+            return self.whole(name), during(())
+        (block,) = cut(self.place, [self.shards[name]])
+        z = self.links.from_each(block, (8, 16, 24))
+        x = during((block,))
+        (z,) = local(lambda *v: [jnp.stack(v)], z, (x,), "stack")
+        plane = self.links.from_each(z, (2, 4, 6))
+        (own,) = local(lambda *v: [jnp.stack(v)], plane, (), "stack")
+        return assemble(self.place, own, self.links.across(own)), x
+
+    def fetch(self, bases, height, after=()):
+        names = list(bases)
         if self.staged:
-            self.now.update(zip(names, cut(self.place, [self.shards[n] for n in names], after)))
-
-    def along_z(self, name):
-        if self.staged:
-            self.now[name] = self.links.from_each(self.now[name], (8, 16, 24))
-
-    def in_plane(self, name, after=()):
-        if self.staged:
-            (z,) = local(lambda *v: [jnp.stack(v)], self.now[name], after, "stack")
-            self.now[name] = self.links.from_each(z, (2, 4, 6))
-
-    def swap(self, name, after=()):
-        if self.staged:
-            (own,) = local(lambda *v: [jnp.stack(v)], self.now[name], after, "stack")
-            self.now[name] = own, self.links.across(own)
-
-    def fetch(self, *names, after=()):
+            shards = [self.shards[n] for n in names]
+            own = pack(self.place, shards, list(bases.values()), (height, 512), after)
+            buffer = lax.all_gather(own, AXES)
+        else:
+            own, at, blocks = None, 0, []
+            for n in names:
+                w = self.whole(n)
+                if w.ndim == 2:
+                    w = w.reshape(w.shape[0], -1, 512).transpose(1, 0, 2)
+                w = w.reshape(w.shape[0], 32, -1, 512).transpose(1, 0, 2, 3).reshape(32, -1, 512)
+                blocks += [jnp.zeros((32, bases[n] - at, 512), BF16), w]
+                at = bases[n] + w.shape[1]
+            blocks.append(jnp.zeros((32, height - at, 512), BF16))
+            buffer = jnp.concatenate(blocks, 1)
+        for n in names:
+            shard = self.shards[n]
+            rows = shard.shape[-2] * self.links.img // 32
+            steps = shard.shape[0] if shard.ndim == 3 else shard.shape[1] // 512
+            self.now[n] = Packed(buffer, bases[n], rows, steps)
+        return () if own is None else (own,)
+
+    def fetch_rows(self, name, after=()):
         if not self.staged:
+            self.now[name] = self.whole(name)
             return ()
-        at, widest = 0, max(self.shards[n].shape[-1] for n in names)
-        for n in names:
-            half, folds = self.shards[n].shape[-2] // 2, widest // self.shards[n].shape[-1]
-            self.halves[n] = names, at, half, folds
-            at += half // folds
-        own = half_of(self.place, [self.shards[n] for n in names], after)
-        self.now[names] = lax.all_gather(own, "img")
+        (own,) = cut(self.place, [self.shards[name]], after)
+        self.now[name] = lax.all_gather(own, AXES, axis=0, tiled=True)
         return (own,)
-
-    def hand_on(self, *names, after=()):
-        if self.staged:
-            own = pin(self.now[names], after)
-            self.now[names] = own, self.links.across(own)
-
-    def get(self, name):
-        if not self.staged:
-            shard = self.shards[name]
-            return lax.all_gather(shard, "img", axis=shard.ndim - 2, tiled=True)
-        if name in self.halves:
-            names, *where = self.halves[name]
-            return join_halves(self.place, *self.now[names], *where)
-        return assemble(self.place, *self.now[name])
-
-    def state(self, *names):
-        return tuple(jax.tree.leaves([self.now[n] for n in names])) if self.staged else ()
 
 
 class Sums:
@@ -1191,9 +1246,9 @@
         self.links, self.place, self.staged = links, place, staged
         self.now = {}
 
-    def start(self, name, left, right, taps=1, halves=False):
+    def start(self, name, left, right, taps=1, halves=False, us=None):
         if self.staged:
-            self.now[name] = weight_grad(self.place, left, right, taps, halves)
+            self.now[name] = weight_grad(self.place, left, right, taps, halves, us)
         else:
             self.now[name] = self.links.scatter_plain(left, right, taps)
 
@@ -1225,28 +1280,23 @@
             join = lambda *v: [jnp.concatenate([add2(a, b) for a, b in zip(v[::2], v[1::2])], 1)]
             (part,) = local(join, parts, after, "fold", 4)
             self.now[names] = lax.psum_scatter(part, "img", scatter_dimension=0, tiled=False)
+            return (part,)
+        return ()
 
     def across_y(self, *names):
         if self.staged:
             own = self.now[names]
-            (own,) = local(lambda a, b: [add2(a, b)], [own, self.links.swap(own, 2)], (), "fold")
+            self.now[names] = own, self.links.swap(own, 2)
+
+    def across_cores(self, *names, after=()):
+        if self.staged:
+            (own,) = local(lambda a, b: [add2(a, b)], self.now[names], after, "fold")
             self.now[names] = own, self.links.across(own)
 
-    def split(self, names, rows):
+    def split(self, names, kinds):
         if not self.staged:
             return [self.now[n] for n in names]
-        own, other = self.now[names]
-        core = self.links.me & 1
-        both = jnp.where(core == 0, own, other), jnp.where(core == 0, other, own)
-        found, at = [], 0
-        for steps, half, by_tap in rows:
-            pieces = [b[at : at + steps * half].reshape(steps, half, -1) for b in both]
-            piece = jnp.concatenate(pieces, 1).astype(F32)
-            if not by_tap:
-                piece = jnp.concatenate([piece[k] for k in range(steps)], 1)
-            found.append(piece)
-            at += steps * half
-        return found
+        return unpack(self.place, *self.now[names], kinds)
 
     def state(self, *names):
         return tuple(jax.tree.leaves([self.now[n] for n in names])) if self.staged else ()
@@ -1342,49 +1392,40 @@
     n_in, n_out = 4 * f.valid, f.valid
     all_in, all_out = n_in * links.size, n_out * links.size
 
-    weights.cut(["reduce"])
-    reduce_cut = weights.state("reduce")
-    weights.along_z("reduce")
-    weights.fetch("spatial")
-    x = split_cells(f, x_large, x_small, after=reduce_cut)
-    weights.in_plane("reduce", after=(x,))
-    first = ("expand", "short", "reduce2", "expand2")
-    first_half = weights.fetch(*first, after=(x,))
-    weights.swap("reduce")
-    w_reduce = weights.get("reduce")
-    reduced, part0 = linear(f, x, w_reduce, mask, 4, 256, after=first_half)
+    first = {"expand": 0, "reduce2": 64, "spatial": 144, "short": 288}
+    second = {"spatial2": 0, "expand2": 144}
+    weights.fetch(first, 416)
+    w = weights.now
+    w_reduce, x = weights.first(
+        "reduce", lambda after: split_cells(f, x_large, x_small, after=after)
+    )
+    second_own = weights.fetch(second, 208, after=(x,))
+    reduce_in = (w_reduce, (w_reduce.shape[0], 256), lambda i: (0, i))
+    reduced, part0 = linear(f, x, reduce_in, mid, mask, 4, 256, after=second_own)
     st0 = links.moments(part0, n_in)
-    weights.hand_on("spatial", after=(st0,))
-    spatial2_half = weights.fetch("spatial2", after=(st0,))
-    w_spatial = weights.get("spatial")
+    head_own = weights.fetch_rows("head", after=(part0,))
     patch1, turned, part1 = conv(
-        f, 2, all_in, reduced, st0, affine[0], w_spatial.reshape(9 * mid, mid), mask, after=spatial2_half
+        f, 2, all_in, reduced, st0, affine[0], w["spatial"], mask, after=head_own
     )
     st1 = links.moments(part1, n_out)
-    weights.hand_on(*first, after=(st1,))
-    w_expand, w_short, w_reduce2, w_expand2 = [weights.get(n) for n in first]
-    head_half = weights.fetch("head", after=(st1,))
-    turned_low, expanded, part2 = expand(f, all_out, turned, st1, affine[1], w_expand, mask)
-    skipped, part3 = linear(f, x, w_short, mask, 1, 512, after=(part2,) + head_half)
+    turned_low, expanded, part2 = expand(f, all_out, turned, st1, affine[1], w["expand"], mask)
+    skipped, part3 = linear(
+        f, x, w["short"].column_tile(), wide, mask, 1, 512, after=(part2,)
+    )
     joint = links.moments(jnp.concatenate([part2, part3], 1), n_out)
     st2, st3 = joint[:, :wide], joint[:, wide:]
     block_low, block_pre, mixing, part4 = mix(
-        f, all_out, expanded, skipped, st2, affine[2], st3, affine[3], w_reduce2, mask
-    )
-    weights.hand_on("spatial2", after=(part4,))
+        f, all_out, expanded, skipped, st2, affine[2], st3, affine[3], w["reduce2"], mask
+    )
     st4 = links.moments(part4, n_out)
-    w_spatial2 = weights.get("spatial2")
-    patch2, rotated, part5 = conv(
-        f, 1, all_out, mixing, st4, affine[4], w_spatial2.reshape(9 * mid, mid), mask, after=(w_expand2,)
-    )
+    patch2, rotated, part5 = conv(f, 1, all_out, mixing, st4, affine[4], w["spatial2"], mask)
     st5 = links.moments(part5, n_out)
-    rotated_low, widened, part6 = expand(f, all_out, rotated, st5, affine[5], w_expand2, mask)
+    rotated_low, widened, part6 = expand(f, all_out, rotated, st5, affine[5], w["expand2"], mask)
     st6 = links.moments(part6, n_out)
-    weights.hand_on("head", after=(st6,))
     pooled, slopes, view_sums = pool(f, all_out, widened, block_pre, st6, affine[6], mask)
     pooled = pooled.astype(BF16)
     labels = jnp.concatenate([large_image, small_image], 0)
-    w_head = weights.get("head")
+    w_head = w["head"]
 
     shard = head_hidden.shape[0]
     if staged:
@@ -1411,68 +1452,72 @@
     sums6 = links.total(sums6)
 
     widened_back, d5, part5 = widen_back(
-        f, all_out, widened, slopes, back, st6, affine[6], sums6, w_expand2, rotated, st5, affine[5], mask
+        f, all_out, widened, slopes, back, st6, affine[6], sums6, w["expand2"], rotated, st5, affine[5], mask
     )
     sums.start("expand2", rotated_low, widened_back, halves=True)
+    started = sums.state("expand2")
     sums.swap("expand2")
     sums5 = links.total(part5)
     rotated_back, d4, part4 = conv_back(
-        f, 1, all_out, all_out, d5, rotated, st5, affine[5], sums5, w_spatial2, mixing, st4, affine[4],
-        mask, after=sums.state("expand2"),
+        f, 1, all_out, all_out, d5, rotated, st5, affine[5], sums5, w["spatial2"], mixing, st4, affine[4],
+        mask, after=started,
     )
     sums.start("spatial2", patch2, rotated_back, 9, halves=True)
     sums.swap("spatial2")
     sums4 = links.total(part4)
     first = ("expand2", "spatial2")
-    sums.scatter(*first, after=(sums4,))
+    first_own = sums.scatter(*first)
     mixing_back, block_grad, part23 = mix_back(
-        f, all_out, d4, mixing, st4, affine[4], sums4, w_reduce2, back, slopes, block_pre,
-        expanded, st2, affine[2], skipped, st3, affine[3], mask, after=sums.state("spatial2"),
+        f, all_out, d4, mixing, st4, affine[4], sums4, w["reduce2"], back, slopes, block_pre,
+        expanded, st2, affine[2], skipped, st3, affine[3], mask, after=first_own,
     )
     sums.start("reduce2", block_low, mixing_back, halves=True)
+    started = sums.state("reduce2")
     sums.swap("reduce2")
     sums23 = links.total(part23)
     expanded_back, skipped_back, d1, part1 = block_back(
-        f, all_out, block_grad, expanded, st2, affine[2], skipped, st3, affine[3], sums23, w_expand,
-        turned, st1, affine[1], mask, after=sums.state("reduce2"),
+        f, all_out, block_grad, expanded, st2, affine[2], skipped, st3, affine[3], sums23, w["expand"],
+        turned, st1, affine[1], mask, after=started,
     )
     sums.start("expand", turned_low, expanded_back, halves=True)
     sums.swap("expand")
     sums.start("short", x, skipped_back, halves=True)
     sums.swap("short")
-    sub = dot(skipped_back, w_short, NT)
     sums1 = links.total(part1)
     second = ("reduce2", "expand", "short")
-    sums.scatter(*second, after=(sums1,))
+    second_own = sums.scatter(*second)
     turned_back, d0, part0 = conv_back(
-        f, 2, all_out, all_in, d1, turned, st1, affine[1], sums1, w_spatial, reduced, st0, affine[0], mask,
-        after=sums.state("expand", "short"),
+        f, 2, all_out, all_in, d1, turned, st1, affine[1], sums1, w["spatial"], reduced, st0, affine[0], mask,
+        after=second_own,
     )
     sums.start("spatial", patch1, turned_back, 9)
     sums.swap("spatial")
-    sums0 = links.total(pin(part0, sums.state(first)))
+    sums0 = links.total(part0)
+    sums.in_plane("spatial")
+    reduced_back = input_low(
+        f, all_in, d0, reduced, st0, affine[0], sums0, mask, after=sums.state("spatial")[:1]
+    )
+    sums.start("reduce", x, reduced_back, us=0.1)
+    sums.swap("reduce")
+    sub = sub_back(skipped_back, w["short"], x.shape[1], after=(reduced_back,))
+    grad_large, grad_small = input_back(f, reduced_back, w_reduce, sub)
+    sums.in_plane("reduce", after=sums.state("spatial") + (grad_small,))
+    sums.along_z("spatial")
     sums.across_y(*first)
-    sums.in_plane("spatial", after=(sums0,))
-    reduced_back, grad_large, grad_small = input_back(
-        f, all_in, d0, reduced, st0, affine[0], sums0, w_reduce, sub, mask, after=sums.state("spatial")[:1]
-    )
-    sums.start("reduce", x, reduced_back)
-    sums.swap("reduce")
-    sums.in_plane("reduce", after=sums.state("spatial"))
-    sums.along_z("spatial")
+    sums.across_y(*second)
     sums.along_z("reduce")
-    sums.join("spatial")
+    sums.across_cores(*first)
+    sums.join("spatial", after=sums.state(first) + sums.state(second))
+    sums.across_cores(*second)
     sums.join("reduce")
-    sums.across_y(*second)
-    eighth = lambda n: n // (2 * links.img)
+    part = lambda n: n // 16
     expand2_grad, spatial2_grad = sums.split(
-        first, [(wide // 512, eighth(mid), False), (9, eighth(mid), True)]
+        first, [(wide // 512, part(mid), False), (9, part(mid), True)]
     )
     reduce2_grad, expand_grad, short_grad = sums.split(
-        second,
-        [(1, eighth(wide), False), (wide // 512, eighth(mid), False), (wide // 512, eighth(2 * mid), False)],
-    )
-    spatial_grad, reduce_grad = sums.get("spatial"), sums.get("reduce")
+        second, [(1, part(wide), False), (wide // 512, part(mid), False), (wide // 512, part(2 * mid), False)]
+    )
+    reduce_grad, spatial_grad = sums.get("reduce"), sums.get("spatial")
 
     gain_grads = jnp.concatenate(
         [sums0[1], sums1[1], sums23[1], sums23[2], sums4[1], sums5[1], sums6[1], gain7]

time: 705 us -> 630 us (0.89)
  waiting for transfers between devices: 234 us -> 201 us
  local copies, waits for them, and re-layouts: 43.9 us -> 23.6 us
  Pallas kernels: 240 us -> 230 us
    ppermute x131 -> x127, waiting for transfers between devices: 186 us -> 160 us  [swap(): return lax.ppermute(v, AXES, [(i, i ^ bits) for i in range(self.size)])]
    unnamed x173 -> x149, local copies, waits for them, and re-layouts: 41.5 us -> 21.5 us
    pallas_call x23 -> x11, Pallas kernels: 73 us -> 53.6 us  [the longest x7 44.5 us: weight_grad(): pl.pallas_call(functools.partial(weight_kernel, taps > 1, rows, halves),...]
    pallas_call x15 -> x17, Pallas kernels: 104 us -> 113 us  [call(): pl.pallas_call(skipping(kernel, len(inputs), len(after)), name=kernel.fun...]
    all_gather x4 -> x3, waiting for transfers between devices: 47.1 us -> 39.5 us  [the longest x2 39.5 us: fetch(): buffer = lax.all_gather(own, AXES)]
    ppermute x131 -> x127, starting transfers between devices: 132 us -> 135 us  [swap(): return lax.ppermute(v, AXES, [(i, i ^ bits) for i in range(self.size)])]
  transfers between devices with their start and end apart: 137 -> 132, of which waited for: 79 -> 76; matrix products, arithmetic and copies ran while one was open for 5% -> 4% of each run, Pallas kernels for 26% -> 28%
where the time goes in v3:
time: 630 us; the launch traced here: 623 us
  Pallas kernels  230 us (37%)
  waiting for transfers between devices  201 us (32%)
  starting transfers between devices  135 us (21%)
  local copies, waits for them, and re-layouts  23.6 us (4%)
  other arithmetic  18.9 us (3%)
  between operations  15 us (2%)
    ppermute x127, waiting for transfers between devices, swap(): return lax.ppermute(v, AXES, [(i, i ^ bits) for i in range(self.size)])  160 us
    ppermute x127, starting transfers between devices, swap(): return lax.ppermute(v, AXES, [(i, i ^ bits) for i in range(self.size)])  135 us
    pallas_call x17, Pallas kernels, call(): pl.pallas_call(skipping(kernel, len(inputs), len(after)), name=kernel.fun...  113 us
    pallas_call x7, Pallas kernels, weight_grad(): pl.pallas_call(functools.partial(weight_kernel, taps > 1, rows, halves),...  44.5 us
    all_gather x2, waiting for transfers between devices, fetch(): buffer = lax.all_gather(own, AXES)  39.5 us
    pallas_call x12, Pallas kernels, local(): pl.pallas_call(skipping(kernel, len(arrays), len(after)), name=name, in_s...  33.4 us
    pallas_call x1, Pallas kernels, head(): pl.pallas_call(functools.partial(head_kernel, f, devices, shard), name='h...  21.9 us
    unnamed x149, local copies, waits for them, and re-layouts  21.5 us
  transfers between devices with their start and end apart: 132, of which 76 were waited for; matrix products, arithmetic and copies ran while one was open for 4% of the time, Pallas kernels for 28%

profile of v3, /device:TPU:0, one launch (start us, length us, event | category | flops | bytes accessed | tf_op | source)
XLA Modules:
  0.0 623.3 jit_solution(11353995941196011171)
XLA Ops:
  14.3 4.9 split_kernel.1.refs_4_.refs_3_.refs_0_.left_ref
  21.2 3.1 collective-permute-start
  26.9 4.8 collective-permute-done.1.refs_2_
  38.8 3.1 collective-permute-done.3.refs_1_
  52.5 5.7 linear_kernel.2
  78.5 39.5 %all-gather.8.cloned.1.call-done = bf16[13312,512]{1,0:T(8,128)(2,1)} async-done(((bf16[416,512]{1,0:T(8,128)(2,1)}), bf16[13312,512]{1,0:T(8,128)(2,1)}) %all-gather.8.cloned.1.call-update) | async-done | bytes 13631504 | tf_op jit(solution)/shard_map/all_gather | solution.py:1216
  118.0 8.1 %conv_kernel.2 = (bf16[384,4608]{1,0:T(8,128)(2,1)}, f32[384,512]{1,0:T(8,128)}, f32[2,512]{1,0:T(2,128)}) custom-call(f32[1536,512]{1,0:T(8,128)} %get-tuple-element.96.refs_0_.refs_6_.refs_1_, f32[2,512]{1,0:T(2,128)} %pad_maximum_fusion.14.refs_1_.refs_7_.refs_2_, f32[2,512]{1,0:T(2,128)} %get-tuple-element.261.refs_2_.refs_8_.refs_3_, ...), custom_call_target="tpu_custom_call" | custom-call | bytes 28000000 | tf_op jit(solution)/shard_map/conv_kernel/pallas_call | solution.py:33
  132.5 3.0 collective-permute-done.17
  143.7 5.5 expand_kernel.2
  149.1 6.0 linear_kernel.3
  161.3 3.1 collective-permute-done.24
  174.6 7.7 %mix_kernel.1 = (bf16[384,2048]{1,0:T(8,128)(2,1)}, f32[384,2048]{1,0:T(8,128)}, f32[384,512]{1,0:T(8,128)}, f32[2,512]{1,0:T(2,128)}) custom-call(f32[384,2048]{1,0:T(8,128)} %get-tuple-element.100.exp_ref.refs_9_.refs_1_, f32[384,2048]{1,0:T(8,128)} %get-tuple-element.102.skip_ref.refs_12_.refs_4_, f32[2,2048]{1,0:T(2,128)} %get-tuple-element.268.stats_a.refs_10_.refs_2_, ...), custom_call_target="tpu_custom_call" | custom-call | bytes 28000000 | tf_op jit(solution)/shard_map/mix_kernel/pallas_call | solution.py:33
  200.2 6.3 %conv_kernel.3 = (bf16[384,4608]{1,0:T(8,128)(2,1)}, f32[384,512]{1,0:T(8,128)}, f32[2,512]{1,0:T(2,128)}) custom-call(f32[384,512]{1,0:T(8,128)} %get-tuple-element.104.pre_ref.refs_6_.refs_1_, f32[2,512]{1,0:T(2,128)} %pad_maximum_fusion.20.stats_ref.refs_7_.refs_2_, f32[2,512]{1,0:T(2,128)} %get-tuple-element.259.affine_ref.refs_8_.refs_3_, ...), custom_call_target="tpu_custom_call" | custom-call | bytes 28000000 | tf_op jit(solution)/shard_map/conv_kernel/pallas_call | solution.py:33
  211.5 3.4 collective-permute-done.38
  219.6 3.2 collective-permute-done.41
  223.4 5.4 expand_kernel.3
  238.2 3.0 collective-permute-start.47
  243.0 3.9 collective-permute-done.48
  247.5 7.1 %pool_kernel.1 = (f32[16,2048]{1,0:T(8,128)}, f32[384,2048]{1,0:T(8,128)}, f32[32,2048]{1,0:T(8,128)}) custom-call(f32[384,2048]{1,0:T(8,128)} %get-tuple-element.108.wide_ref, f32[384,2048]{1,0:T(8,128)} %get-tuple-element.109.pre_ref.refs_8_, f32[2,2048]{1,0:T(2,128)} %pad_maximum_fusion.9.stats_ref, f32[2,2048]{1,0:T(2,128)} %get-tuple-element.257.affine_ref, ...), custom_call_target="tpu_custom_call" | custom-call | bytes 23450000 | tf_op jit(solution)/shard_map/pool_kernel/pallas_call | solution.py:33
  260.1 3.1 collective-permute-done.49
  263.2 4.4 collective-permute-done.50
  271.2 5.5 collective-permute-done.52
  282.7 3.9 assemble.3.p_ref.digit_ref
  288.0 21.9 %head.1 = (f32[8,128]{1,0:T(8,128)}, f32[256,2048]{1,0:T(8,128)}, f32[256,128]{1,0:T(8,128)}, f32[2,2048]{1,0:T(2,128)}, f32[16,2048]{1,0:T(8,128)}, /*index=5*/f32[2,2048]{1,0:T(2,128)}) custom-call(s32[3]{0:T(128)} %pad_add_fusion.place_ref.refs_0_, bf16[512,2176]{1,0:T(8,128)(2,1)} %copy-done, bf16[512,2176]{1,0:T(8,128)(2,1)} %copy-done, ...), custom_call_target="tpu_custom_call" | custom-call | bytes 77000000 | tf_op jit(solution)/shard_map/head/pallas_call | solution.py:584
  318.7 4.9 collective-permute-start.60
  331.4 7.2 %widen_back_kernel.1 = (bf16[384,2048]{1,0:T(8,128)(2,1)}, f32[384,512]{1,0:T(8,128)}, f32[2,512]{1,0:T(2,128)}) custom-call(f32[384,2048]{1,0:T(8,128)} %get-tuple-element.108.wide_ref, f32[384,2048]{1,0:T(8,128)} %get-tuple-element.114.slope_ref.refs_7_, f32[16,2048]{1,0:T(8,128)} %get-tuple-element.115.back_ref.refs_6_, ...), custom_call_target="tpu_custom_call" | custom-call | bytes 25900000 | tf_op jit(solution)/shard_map/widen_back_kernel/pallas_call | solution.py:33
  351.6 4.8 weight_grad.7
  357.0 6.7 %conv_back_kernel.2 = (bf16[384,512]{1,0:T(8,128)(2,1)}, f32[384,512]{1,0:T(8,128)}, f32[2,512]{1,0:T(2,128)}) custom-call(f32[384,512]{1,0:T(8,128)} %get-tuple-element.117.refs_0_, f32[384,512]{1,0:T(8,128)} %get-tuple-element.106.pre_ref.turn_ref.refs_1_, f32[2,512]{1,0:T(2,128)} %pad_maximum_fusion.23.stats_ref.turn_stats.refs_2_, ...), custom_call_target="tpu_custom_call" | custom-call | bytes 25200000 | tf_op jit(solution)/shard_map/conv_back_kernel/pallas_call | solution.py:33
  363.7 9.5 %weight_grad.8 = (bf16[8,288,512]{2,1,0:T(8,128)(2,1)}, bf16[8,288,512]{2,1,0:T(8,128)(2,1)}) custom-call(s32[3]{0:T(128)} %pad_add_fusion.place_ref.refs_0_, bf16[384,4608]{1,0:T(8,128)(2,1)} %get-tuple-element.125.left_ref, bf16[384,512]{1,0:T(8,128)(2,1)} %get-tuple-element.126.right_ref), custom_call_target="tpu_custom_call" | custom-call | bytes 35000000 | tf_op jit(solution)/shard_map/weight_grad/pallas_call | solution.py:1072
  373.7 5.2 collective-permute-done.77.refs_1_
  380.8 5.6 fold.10.refs_16_
  403.2 9.8 %mix_back_kernel.1 = (bf16[384,512]{1,0:T(8,128)(2,1)}, f32[384,2048]{1,0:T(8,128)}, f32[3,2048]{1,0:T(4,128)}) custom-call(f32[384,512]{1,0:T(8,128)} %get-tuple-element.123.refs_0_, f32[384,512]{1,0:T(8,128)} %get-tuple-element.104.pre_ref.refs_6_.refs_1_, f32[2,512]{1,0:T(2,128)} %pad_maximum_fusion.20.stats_ref.refs_7_.refs_2_, ...), custom_call_target="tpu_custom_call" | custom-call | bytes 34300000 | tf_op jit(solution)/shard_map/mix_back_kernel/pallas_call | solution.py:33
  427.1 4.3 weight_grad.9
  432.0 8.5 %block_back_kernel.1 = (bf16[384,2048]{1,0:T(8,128)(2,1)}, bf16[384,2048]{1,0:T(8,128)(2,1)}, f32[384,512]{1,0:T(8,128)}, f32[2,512]{1,0:T(2,128)}) custom-call(f32[384,2048]{1,0:T(8,128)} %get-tuple-element.129.refs_0_, f32[384,2048]{1,0:T(8,128)} %get-tuple-element.100.exp_ref.refs_9_.refs_1_, f32[2,2048]{1,0:T(2,128)} %get-tuple-element.268.stats_a.refs_10_.refs_2_, ...), custom_call_target="tpu_custom_call" | custom-call | bytes 30800000 | tf_op jit(solution)/shard_map/block_back_kernel/pallas_call | solution.py:33
  440.6 6.3 %weight_grad.11 = (bf16[8,256,512]{2,1,0:T(8,128)(2,1)}, bf16[8,256,512]{2,1,0:T(8,128)(2,1)}) custom-call(s32[3]{0:T(128)} %pad_add_fusion.place_ref.refs_0_, bf16[1536,1024]{1,0:T(8,128)(2,1)} %split_kernel.1.refs_4_.refs_3_.refs_0_.left_ref, bf16[384,2048]{1,0:T(8,128)(2,1)} %get-tuple-element.141.right_ref.refs_0_), custom_call_target="tpu_custom_call" | custom-call | bytes 17500000 | tf_op jit(solution)/shard_map/weight_grad/pallas_call | solution.py:1072
  447.5 4.8 weight_grad.10
  456.8 6.5 %fold.11.refs_10_ = bf16[8,512,512]{2,1,0:T(8,128)(2,1)} custom-call(bf16[8,128,512]{2,1,0:T(8,128)(2,1)} %get-tuple-element.133.refs_13_.refs_0_, bf16[8,128,512]{2,1,0:T(8,128)(2,1)} %copy-done.21, bf16[8,128,512]{2,1,0:T(8,128)(2,1)} %get-tuple-element.139.refs_2_, bf16[8,128,512]{2,1,0:T(8,128)(2,1)} %copy-done.22, ...), custom_call_target="tpu_custom_call" | custom-call | bytes 14000000 | tf_op jit(solution)/shard_map/fold/pallas_call | solution.py:1009
  480.9 7.6 %conv_back_kernel.3 = (bf16[384,512]{1,0:T(8,128)(2,1)}, f32[1536,512]{1,0:T(8,128)}, f32[2,512]{1,0:T(2,128)}) custom-call(f32[384,512]{1,0:T(8,128)} %get-tuple-element.135.refs_0_, f32[384,512]{1,0:T(8,128)} %get-tuple-element.98.pre_ref.refs_9_.refs_1_, f32[2,512]{1,0:T(2,128)} %pad_maximum_fusion.17.stats_ref.refs_10_.refs_2_, ...), custom_call_target="tpu_custom_call" | custom-call | bytes 25200000 | tf_op jit(solution)/shard_map/conv_back_kernel/pallas_call | solution.py:33
  488.6 9.5 %weight_grad.12 = (bf16[4,4,9,16,512]{4,3,2,1,0:T(8,128)(2,1)}, bf16[4,4,9,16,512]{4,3,2,1,0:T(8,128)(2,1)}) custom-call(s32[3]{0:T(128)} %pad_add_fusion.place_ref.refs_0_, bf16[384,4608]{1,0:T(8,128)(2,1)} %get-tuple-element.146.left_ref, bf16[384,512]{1,0:T(8,128)(2,1)} %get-tuple-element.147.right_ref), custom_call_target="tpu_custom_call" | custom-call | bytes 35000000 | tf_op jit(solution)/shard_map/weight_grad/pallas_call | solution.py:1072
  510.9 3.0 collective-permute-done.102
  515.5 4.0 fold.12
  523.0 4.4 input_low_kernel.1.refs_2_.low_ref.right_ref
  527.4 5.3 weight_grad.13
  534.0 6.2 %sub_kernel.1.sub_ref = f32[384,1024]{1,0:T(8,128)} custom-call(bf16[384,2048]{1,0:T(8,128)(2,1)} %get-tuple-element.141.right_ref.refs_0_, bf16[32,416,512]{2,1,0:T(8,128)(2,1)} %bitcast.54, bf16[1536,512]{1,0:T(8,128)(2,1)} %input_low_kernel.1.refs_2_.low_ref.right_ref), custom_call_target="tpu_custom_call" | custom-call | bytes 350000 | tf_op jit(solution)/shard_map/sub_kernel/pallas_call | solution.py:33
  540.3 6.1 input_back_kernel.1
  546.4 9.2 %collective-permute-done.107.refs_5_.refs_3_ = bf16[4,9,16,512]{3,2,1,0:T(8,128)(2,1)S(1)} collective-permute-done((bf16[4,9,16,512]{3,2,1,0:T(8,128)(2,1)}, bf16[4,9,16,512]{3,2,1,0:T(8,128)(2,1)S(1)}, u32[]{:S(2)}, u32[]{:S(2)}) %collective-permute-start.107) | collective-permute-done | bytes 589856 | tf_op jit(solution)/shard_map/ppermute | solution.py:1094
  585.3 3.4 collective-permute-done.117.refs_1_
  588.7 5.0 collective-permute-done.118.refs_2_
  (498 shorter events, 295.2 us)
Async XLA Ops:
  7.2 110.8 %all-gather.8.cloned.1.call-start = ((), (), s32[]{:S(2)}) async-start(), calls=%async_computation.5 | async-start | bytes 14057472 | tf_op jit(solution)/shard_map/all_gather | solution.py:1216
  10.0 190.2 %all-gather.10.cloned.1.call-start = ((), (), s32[]{:S(2)}) async-start(), calls=%async_computation.6 | async-start | bytes 7028736 | tf_op jit(solution)/shard_map/all_gather | solution.py:1216
  21.1 266.9 %all-gather.6.cloned.1.call-start = ((), (), s32[]{:S(2)}) async-start(), calls=%async_computation.2 | async-start | bytes 9191424 | tf_op jit(solution)/shard_map/all_gather | solution.py:1240
  24.2 7.5 %collective-permute-start.1 = (bf16[32,512]{1,0:T(8,128)(2,1)S(1)}, bf16[32,512]{1,0:T(8,128)(2,1)S(1)}, u32[]{:S(2)}, u32[]{:S(2)}) collective-permute-start(bf16[32,512]{1,0:T(8,128)(2,1)S(1)} %copy-done.4), channel_id=1, source_target_pairs={{0,16},{1,17},{2,18},{3,19},{4,20},{5,21},{6,22},{7,23},{8,24},{9,... | collective-permute-start | bytes 98312 | tf_op jit(solution)/shard_map/ppermute | solution.py:1094
  26.8 6.4 %collective-permute-start.2 = (bf16[32,512]{1,0:T(8,128)(2,1)S(1)}, bf16[32,512]{1,0:T(8,128)(2,1)S(1)}, u32[]{:S(2)}, u32[]{:S(2)}) collective-permute-start(bf16[32,512]{1,0:T(8,128)(2,1)S(1)} %copy-done.4), channel_id=1, source_target_pairs={{0,24},{1,25},{2,26},{3,27},{4,28},{5,29},{6,30},{7,31},{8,16},{9,... | collective-permute-start | bytes 98312 | tf_op jit(solution)/shard_map/ppermute | solution.py:1094
  35.3 6.6 %collective-permute-start.3 = (bf16[4,32,512]{2,1,0:T(8,128)(2,1)}, bf16[4,32,512]{2,1,0:T(8,128)(2,1)S(1)}, u32[]{:S(2)}, u32[]{:S(2)}) collective-permute-start(bf16[4,32,512]{2,1,0:T(8,128)(2,1)} %stack.185.refs_0_), channel_id=1, source_target_pairs={{0,2},{1,3},{2,0},{3,1},{4,6},{5,7},{6,4},{7,5},{8,10},{9,11},{10,... | collective-permute-start | bytes 393224 | tf_op jit(solution)/shard_map/ppermute | solution.py:1094
  60.1 472.6 %reduce-scatter.3.cloned.1.call-start = ((), (), s32[]{:S(2)}) async-start(), calls=%async_computation.3 | async-start | bytes 3833856 | tf_op jit(solution)/shard_map/reduce_scatter | solution.py:1282
  164.5 7.9 %collective-permute-start.26 = (f32[2,4096]{1,0:T(2,128)S(1)}, f32[2,4096]{1,0:T(2,128)S(1)}, u32[]{:S(2)}, u32[]{:S(2)}) collective-permute-start(f32[2,4096]{1,0:T(2,128)S(1)} %pad_maximum_fusion.4), channel_id=1, source_target_pairs={{0,16},{1,17},{2,18},{3,19},{4,20},{5,21},{6,22},{7,23},{8,24},{9,... | collective-permute-start | bytes 98312 | tf_op jit(solution)/shard_map/ppermute | solution.py:1094
  167.4 6.4 %collective-permute-start.27 = (f32[2,4096]{1,0:T(2,128)S(1)}, f32[2,4096]{1,0:T(2,128)S(1)}, u32[]{:S(2)}, u32[]{:S(2)}) collective-permute-start(f32[2,4096]{1,0:T(2,128)S(1)} %pad_maximum_fusion.4), channel_id=1, source_target_pairs={{0,24},{1,25},{2,26},{3,27},{4,28},{5,29},{6,30},{7,31},{8,16},{9,... | collective-permute-start | bytes 98312 | tf_op jit(solution)/shard_map/ppermute | solution.py:1094
  255.6 7.6 %collective-permute-start.49 = (bf16[16,2176]{1,0:T(8,128)(2,1)S(1)}, bf16[16,2176]{1,0:T(8,128)(2,1)S(1)}, u32[]{:S(2)}, u32[]{:S(2)}) collective-permute-start(bf16[16,2176]{1,0:T(8,128)(2,1)S(1)} %get-tuple-element.263), channel_id=1, source_target_pairs={{0,8},{1,9},{2,10},{3,11},{4,12},{5,13},{6,14},{7,15},{8,0},{9,1},... | collective-permute-start | bytes 208904 | tf_op jit(solution)/shard_map/ppermute | solution.py:1094
  255.7 11.9 %collective-permute-start.50 = (bf16[16,2176]{1,0:T(8,128)(2,1)S(1)}, bf16[16,2176]{1,0:T(8,128)(2,1)S(1)}, u32[]{:S(2)}, u32[]{:S(2)}) collective-permute-start(bf16[16,2176]{1,0:T(8,128)(2,1)S(1)} %get-tuple-element.263), channel_id=1, source_target_pairs={{0,16},{1,17},{2,18},{3,19},{4,20},{5,21},{6,22},{7,23},{8,24},{9,... | collective-permute-start | bytes 208904 | tf_op jit(solution)/shard_map/ppermute | solution.py:1094
  257.8 9.8 %collective-permute-start.51 = (bf16[16,2176]{1,0:T(8,128)(2,1)S(1)}, bf16[16,2176]{1,0:T(8,128)(2,1)S(1)}, u32[]{:S(2)}, u32[]{:S(2)}) collective-permute-start(bf16[16,2176]{1,0:T(8,128)(2,1)S(1)} %get-tuple-element.263), channel_id=1, source_target_pairs={{0,24},{1,25},{2,26},{3,27},{4,28},{5,29},{6,30},{7,31},{8,16},{9,... | collective-permute-start | bytes 208904 | tf_op jit(solution)/shard_map/ppermute | solution.py:1094
  267.7 9.0 %collective-permute-start.52 = (bf16[4,16,2176]{2,1,0:T(8,128)(2,1)S(1)}, bf16[4,16,2176]{2,1,0:T(8,128)(2,1)S(1)}, u32[]{:S(2)}, u32[]{:S(2)}) collective-permute-start(bf16[4,16,2176]{2,1,0:T(8,128)(2,1)S(1)} %get-tuple-element.249), channel_id=1, source_target_pairs={{0,2},{1,3},{2,0},{3,1},{4,6},{5,7},{6,4},{7,5},{8,10},{9,11},{10,... | collective-permute-start | bytes 835592 | tf_op jit(solution)/shard_map/ppermute | solution.py:1094
  269.3 7.4 %collective-permute-start.53 = (bf16[4,16,2176]{2,1,0:T(8,128)(2,1)S(1)}, bf16[4,16,2176]{2,1,0:T(8,128)(2,1)S(1)}, u32[]{:S(2)}, u32[]{:S(2)}) collective-permute-start(bf16[4,16,2176]{2,1,0:T(8,128)(2,1)S(1)} %get-tuple-element.249), channel_id=1, source_target_pairs={{0,4},{1,5},{2,6},{3,7},{4,0},{5,1},{6,2},{7,3},{8,12},{9,13},{10,... | collective-permute-start | bytes 835592 | tf_op jit(solution)/shard_map/ppermute | solution.py:1094
  269.4 10.3 %collective-permute-start.54 = (bf16[4,16,2176]{2,1,0:T(8,128)(2,1)S(1)}, bf16[4,16,2176]{2,1,0:T(8,128)(2,1)S(1)}, u32[]{:S(2)}, u32[]{:S(2)}) collective-permute-start(bf16[4,16,2176]{2,1,0:T(8,128)(2,1)S(1)} %get-tuple-element.249), channel_id=1, source_target_pairs={{0,6},{1,7},{2,4},{3,5},{4,2},{5,3},{6,0},{7,1},{8,14},{9,15},{10,... | collective-permute-start | bytes 835592 | tf_op jit(solution)/shard_map/ppermute | solution.py:1094
  318.7 8.0 %collective-permute-start.60 = (f32[2,2048]{1,0:T(2,128)S(1)}, f32[2,2048]{1,0:T(2,128)S(1)}, u32[]{:S(2)}, u32[]{:S(2)}) collective-permute-start(f32[2,2048]{1,0:T(2,128)S(1)} %add.1109), channel_id=1, source_target_pairs={{0,8},{1,9},{2,10},{3,11},{4,12},{5,13},{6,14},{7,15},{8,0},{9,1},... | collective-permute-start | bytes 49160 | tf_op jit(solution)/shard_map/ppermute | solution.py:1094
  347.2 9.2 %collective-permute-start.67 = (f32[2,512]{1,0:T(2,128)S(1)}, f32[2,512]{1,0:T(2,128)S(1)}, u32[]{:S(2)}, u32[]{:S(2)}) collective-permute-start(f32[2,512]{1,0:T(2,128)S(1)} %add.1116), channel_id=1, source_target_pairs={{0,8},{1,9},{2,10},{3,11},{4,12},{5,13},{6,14},{7,15},{8,0},{9,1},... | collective-permute-start | bytes 12296 | tf_op jit(solution)/shard_map/ppermute | solution.py:1094
  347.4 9.0 %collective-permute-start.68 = (f32[2,512]{1,0:T(2,128)S(1)}, f32[2,512]{1,0:T(2,128)S(1)}, u32[]{:S(2)}, u32[]{:S(2)}) collective-permute-start(f32[2,512]{1,0:T(2,128)S(1)} %add.1116), channel_id=1, source_target_pairs={{0,16},{1,17},{2,18},{3,19},{4,20},{5,21},{6,22},{7,23},{8,24},{9,... | collective-permute-start | bytes 12296 | tf_op jit(solution)/shard_map/ppermute | solution.py:1094
  349.2 7.2 %collective-permute-start.69 = (f32[2,512]{1,0:T(2,128)S(1)}, f32[2,512]{1,0:T(2,128)S(1)}, u32[]{:S(2)}, u32[]{:S(2)}) collective-permute-start(f32[2,512]{1,0:T(2,128)S(1)} %add.1116), channel_id=1, source_target_pairs={{0,24},{1,25},{2,26},{3,27},{4,28},{5,29},{6,30},{7,31},{8,16},{9,... | collective-permute-start | bytes 12296 | tf_op jit(solution)/shard_map/ppermute | solution.py:1094
  373.2 6.2 %collective-permute-start.78 = (bf16[8,288,512]{2,1,0:T(8,128)(2,1)}, bf16[8,288,512]{2,1,0:T(8,128)(2,1)S(1)}, u32[]{:S(2)}, u32[]{:S(2)}) collective-permute-start(bf16[8,288,512]{2,1,0:T(8,128)(2,1)} %get-tuple-element.128), channel_id=1, source_target_pairs={{0,1},{1,0},{2,3},{3,2},{4,5},{5,4},{6,7},{7,6},{8,9},{9,8},{10,11... | collective-permute-start | bytes 7077896 | tf_op jit(solution)/shard_map/ppermute | solution.py:1094
  386.4 177.5 %reduce-scatter.5.cloned.1.call-start = ((), (), s32[]{:S(2)}) async-start(), calls=%async_computation.4 | async-start | bytes 4718592 | tf_op jit(solution)/shard_map/reduce_scatter | solution.py:1282
  422.6 8.8 %collective-permute-start.83 = (f32[3,2048]{1,0:T(4,128)S(1)}, f32[3,2048]{1,0:T(4,128)S(1)}, u32[]{:S(2)}, u32[]{:S(2)}) collective-permute-start(f32[3,2048]{1,0:T(4,128)S(1)} %add.1130), channel_id=1, source_target_pairs={{0,8},{1,9},{2,10},{3,11},{4,12},{5,13},{6,14},{7,15},{8,0},{9,1},... | collective-permute-start | bytes 73736 | tf_op jit(solution)/shard_map/ppermute | solution.py:1094
  422.7 8.7 %collective-permute-start.84 = (f32[3,2048]{1,0:T(4,128)S(1)}, f32[3,2048]{1,0:T(4,128)S(1)}, u32[]{:S(2)}, u32[]{:S(2)}) collective-permute-start(f32[3,2048]{1,0:T(4,128)S(1)} %add.1130), channel_id=1, source_target_pairs={{0,16},{1,17},{2,18},{3,19},{4,20},{5,21},{6,22},{7,23},{8,24},{9,... | collective-permute-start | bytes 73736 | tf_op jit(solution)/shard_map/ppermute | solution.py:1094
  446.9 8.2 %collective-permute-start.95 = (bf16[8,256,512]{2,1,0:T(8,128)(2,1)}, bf16[8,256,512]{2,1,0:T(8,128)(2,1)S(1)}, u32[]{:S(2)}, u32[]{:S(2)}) collective-permute-start(bf16[8,256,512]{2,1,0:T(8,128)(2,1)} %get-tuple-element.143), channel_id=1, source_target_pairs={{0,1},{1,0},{2,3},{3,2},{4,5},{5,4},{6,7},{7,6},{8,9},{9,8},{10,11... | collective-permute-start | bytes 6291464 | tf_op jit(solution)/shard_map/ppermute | solution.py:1094
  498.1 15.9 %collective-permute-start.103 = (bf16[4,4,9,16,512]{4,3,2,1,0:T(8,128)(2,1)}, bf16[4,4,9,16,512]{4,3,2,1,0:T(8,128)(2,1)S(1)}, u32[]{:S(2)}, u32[]{:S(2)}) collective-permute-start(bf16[4,4,9,16,512]{4,3,2,1,0:T(8,128)(2,1)} %get-tuple-element.149), channel_id=1, source_target_pairs={{0,1},{1,0},{2,3},{3,2},{4,5},{5,4},{6,7},{7,6},{8,9},{9,8},{10,11... | collective-permute-start | bytes 7077896 | tf_op jit(solution)/shard_map/ppermute | solution.py:1094
  519.5 26.9 %collective-permute-start.105 = (bf16[4,9,16,512]{3,2,1,0:T(8,128)(2,1)}, bf16[4,9,16,512]{3,2,1,0:T(8,128)(2,1)S(1)}, u32[]{:S(2)}, u32[]{:S(2)}) collective-permute-start(bf16[4,9,16,512]{3,2,1,0:T(8,128)(2,1)} %get-tuple-element.155), channel_id=1, source_target_pairs={{0,2},{1,3},{2,0},{3,1},{4,6},{5,7},{6,4},{7,5},{8,10},{9,11},{10,... | collective-permute-start | bytes 1769480 | tf_op jit(solution)/shard_map/ppermute | solution.py:1094
  520.7 25.7 %collective-permute-start.106 = (bf16[4,9,16,512]{3,2,1,0:T(8,128)(2,1)}, bf16[4,9,16,512]{3,2,1,0:T(8,128)(2,1)S(1)}, u32[]{:S(2)}, u32[]{:S(2)}) collective-permute-start(bf16[4,9,16,512]{3,2,1,0:T(8,128)(2,1)} %get-tuple-element.156), channel_id=1, source_target_pairs={{0,4},{1,5},{2,6},{3,7},{4,0},{5,1},{6,2},{7,3},{8,12},{9,13},{10,... | collective-permute-start | bytes 1769480 | tf_op jit(solution)/shard_map/ppermute | solution.py:1094
  522.2 33.4 %collective-permute-start.107 = (bf16[4,9,16,512]{3,2,1,0:T(8,128)(2,1)}, bf16[4,9,16,512]{3,2,1,0:T(8,128)(2,1)S(1)}, u32[]{:S(2)}, u32[]{:S(2)}) collective-permute-start(bf16[4,9,16,512]{3,2,1,0:T(8,128)(2,1)} %get-tuple-element.157), channel_id=1, source_target_pairs={{0,6},{1,7},{2,4},{3,5},{4,2},{5,3},{6,0},{7,1},{8,14},{9,15},{10,... | collective-permute-start | bytes 1769480 | tf_op jit(solution)/shard_map/ppermute | solution.py:1094
  532.7 13.7 %collective-permute-start.104 = (bf16[4,4,32,512]{3,2,1,0:T(8,128)(2,1)}, bf16[4,4,32,512]{3,2,1,0:T(8,128)(2,1)S(1)}, u32[]{:S(2)}, u32[]{:S(2)}) collective-permute-start(bf16[4,4,32,512]{3,2,1,0:T(8,128)(2,1)} %get-tuple-element.154), channel_id=1, source_target_pairs={{0,1},{1,0},{2,3},{3,2},{4,5},{5,4},{6,7},{7,6},{8,9},{9,8},{10,11... | collective-permute-start | bytes 1572872 | tf_op jit(solution)/shard_map/ppermute | solution.py:1094
  532.7 41.2 %collective-permute-start.120 = (bf16[416,512]{1,0:T(8,128)(2,1)}, bf16[416,512]{1,0:T(8,128)(2,1)S(1)}, u32[]{:S(2)}, u32[]{:S(2)}) collective-permute-start(bf16[416,512]{1,0:T(8,128)(2,1)} %bitcast.68), channel_id=1, source_target_pairs={{0,2},{1,3},{2,0},{3,1},{4,6},{5,7},{6,4},{7,5},{8,10},{9,11},{10,... | collective-permute-start | bytes 1277960 | tf_op jit(solution)/shard_map/ppermute | solution.py:1094
  558.4 6.9 %collective-permute-start.108 = (bf16[4,32,512]{2,1,0:T(8,128)(2,1)}, bf16[4,32,512]{2,1,0:T(8,128)(2,1)S(1)}, u32[]{:S(2)}, u32[]{:S(2)}) collective-permute-start(bf16[4,32,512]{2,1,0:T(8,128)(2,1)} %get-tuple-element.159), channel_id=1, source_target_pairs={{0,2},{1,3},{2,0},{3,1},{4,6},{5,7},{6,4},{7,5},{8,10},{9,11},{10,... | collective-permute-start | bytes 393224 | tf_op jit(solution)/shard_map/ppermute | solution.py:1094
  559.1 6.3 %collective-permute-start.109 = (bf16[4,32,512]{2,1,0:T(8,128)(2,1)}, bf16[4,32,512]{2,1,0:T(8,128)(2,1)S(1)}, u32[]{:S(2)}, u32[]{:S(2)}) collective-permute-start(bf16[4,32,512]{2,1,0:T(8,128)(2,1)} %get-tuple-element.160), channel_id=1, source_target_pairs={{0,4},{1,5},{2,6},{3,7},{4,0},{5,1},{6,2},{7,3},{8,12},{9,13},{10,... | collective-permute-start | bytes 393224 | tf_op jit(solution)/shard_map/ppermute | solution.py:1094
  560.7 6.5 %collective-permute-start.110 = (bf16[4,32,512]{2,1,0:T(8,128)(2,1)}, bf16[4,32,512]{2,1,0:T(8,128)(2,1)S(1)}, u32[]{:S(2)}, u32[]{:S(2)}) collective-permute-start(bf16[4,32,512]{2,1,0:T(8,128)(2,1)} %get-tuple-element.161), channel_id=1, source_target_pairs={{0,6},{1,7},{2,4},{3,5},{4,2},{5,3},{6,0},{7,1},{8,14},{9,15},{10,... | collective-permute-start | bytes 393224 | tf_op jit(solution)/shard_map/ppermute | solution.py:1094
  563.8 34.8 %collective-permute-start.122 = (bf16[512,512]{1,0:T(8,128)(2,1)}, bf16[512,512]{1,0:T(8,128)(2,1)S(1)}, u32[]{:S(2)}, u32[]{:S(2)}) collective-permute-start(bf16[512,512]{1,0:T(8,128)(2,1)} %bitcast.59), channel_id=1, source_target_pairs={{0,2},{1,3},{2,0},{3,1},{4,6},{5,7},{6,4},{7,5},{8,10},{9,11},{10,... | collective-permute-start | bytes 1572872 | tf_op jit(solution)/shard_map/ppermute | solution.py:1094
  569.5 9.8 %collective-permute-start.111 = (bf16[32,512]{1,0:T(8,128)(2,1)}, bf16[32,512]{1,0:T(8,128)(2,1)S(1)}, u32[]{:S(2)}, u32[]{:S(2)}) collective-permute-start(bf16[32,512]{1,0:T(8,128)(2,1)} %get-tuple-element.163), channel_id=1, source_target_pairs={{0,8},{1,9},{2,10},{3,11},{4,12},{5,13},{6,14},{7,15},{8,0},{9,1},... | collective-permute-start | bytes 98312 | tf_op jit(solution)/shard_map/ppermute | solution.py:1094
  570.4 9.0 %collective-permute-start.112 = (bf16[32,512]{1,0:T(8,128)(2,1)}, bf16[32,512]{1,0:T(8,128)(2,1)S(1)}, u32[]{:S(2)}, u32[]{:S(2)}) collective-permute-start(bf16[32,512]{1,0:T(8,128)(2,1)} %get-tuple-element.164), channel_id=1, source_target_pairs={{0,16},{1,17},{2,18},{3,19},{4,20},{5,21},{6,22},{7,23},{8,24},{9,... | collective-permute-start | bytes 98312 | tf_op jit(solution)/shard_map/ppermute | solution.py:1094
  572.4 9.9 %collective-permute-start.113 = (bf16[32,512]{1,0:T(8,128)(2,1)}, bf16[32,512]{1,0:T(8,128)(2,1)S(1)}, u32[]{:S(2)}, u32[]{:S(2)}) collective-permute-start(bf16[32,512]{1,0:T(8,128)(2,1)} %get-tuple-element.165), channel_id=1, source_target_pairs={{0,24},{1,25},{2,26},{3,27},{4,28},{5,29},{6,30},{7,31},{8,16},{9,... | collective-permute-start | bytes 98312 | tf_op jit(solution)/shard_map/ppermute | solution.py:1094
  576.7 21.9 %collective-permute-start.121 = (bf16[416,512]{1,0:T(8,128)(2,1)}, bf16[416,512]{1,0:T(8,128)(2,1)S(1)}, u32[]{:S(2)}, u32[]{:S(2)}) collective-permute-start(bf16[416,512]{1,0:T(8,128)(2,1)} %fold.17.refs_4_.own_ref), channel_id=1, source_target_pairs={{0,1},{1,0},{2,3},{3,2},{4,5},{5,4},{6,7},{7,6},{8,9},{9,8},{10,11... | collective-permute-start | bytes 1277960 | tf_op jit(solution)/shard_map/ppermute | solution.py:1094
  579.4 9.3 %collective-permute-start.117 = (bf16[9,16,512]{2,1,0:T(8,128)(2,1)}, bf16[9,16,512]{2,1,0:T(8,128)(2,1)S(1)}, u32[]{:S(2)}, u32[]{:S(2)}) collective-permute-start(bf16[9,16,512]{2,1,0:T(8,128)(2,1)} %get-tuple-element.167), channel_id=1, source_target_pairs={{0,8},{1,9},{2,10},{3,11},{4,12},{5,13},{6,14},{7,15},{8,0},{9,1},... | collective-permute-start | bytes 442376 | tf_op jit(solution)/shard_map/ppermute | solution.py:1094
  579.5 14.2 %collective-permute-start.118 = (bf16[9,16,512]{2,1,0:T(8,128)(2,1)}, bf16[9,16,512]{2,1,0:T(8,128)(2,1)S(1)}, u32[]{:S(2)}, u32[]{:S(2)}) collective-permute-start(bf16[9,16,512]{2,1,0:T(8,128)(2,1)} %get-tuple-element.168), channel_id=1, source_target_pairs={{0,16},{1,17},{2,18},{3,19},{4,20},{5,21},{6,22},{7,23},{8,24},{9,... | collective-permute-start | bytes 442376 | tf_op jit(solution)/shard_map/ppermute | solution.py:1094
  582.4 12.6 %collective-permute-start.119 = (bf16[9,16,512]{2,1,0:T(8,128)(2,1)}, bf16[9,16,512]{2,1,0:T(8,128)(2,1)S(1)}, u32[]{:S(2)}, u32[]{:S(2)}) collective-permute-start(bf16[9,16,512]{2,1,0:T(8,128)(2,1)} %get-tuple-element.169), channel_id=1, source_target_pairs={{0,24},{1,25},{2,26},{3,27},{4,28},{5,29},{6,30},{7,31},{8,16},{9,... | collective-permute-start | bytes 442376 | tf_op jit(solution)/shard_map/ppermute | solution.py:1094
  588.7 16.9 %collective-permute-start.114 = (bf16[32,512]{1,0:T(8,128)(2,1)}, bf16[32,512]{1,0:T(8,128)(2,1)S(1)}, u32[]{:S(2)}, u32[]{:S(2)}) collective-permute-start(bf16[32,512]{1,0:T(8,128)(2,1)} %fold.15), channel_id=1, source_target_pairs={{0,1},{1,0},{2,3},{3,2},{4,5},{5,4},{6,7},{7,6},{8,9},{9,8},{10,11... | collective-permute-start | bytes 98312 | tf_op jit(solution)/shard_map/ppermute | solution.py:1094
  593.7 12.1 %collective-permute-start.115 = (bf16[32,512]{1,0:T(8,128)(2,1)}, bf16[32,512]{1,0:T(8,128)(2,1)S(1)}, u32[]{:S(2)}, u32[]{:S(2)}) collective-permute-start(bf16[32,512]{1,0:T(8,128)(2,1)} %fold.15), channel_id=1, source_target_pairs={{0,2},{1,3},{2,0},{3,1},{4,6},{5,7},{6,4},{7,5},{8,10},{9,11},{10,... | collective-permute-start | bytes 98312 | tf_op jit(solution)/shard_map/ppermute | solution.py:1094
  594.9 11.6 %collective-permute-start.116 = (bf16[32,512]{1,0:T(8,128)(2,1)}, bf16[32,512]{1,0:T(8,128)(2,1)S(1)}, u32[]{:S(2)}, u32[]{:S(2)}) collective-permute-start(bf16[32,512]{1,0:T(8,128)(2,1)} %fold.15), channel_id=1, source_target_pairs={{0,3},{1,2},{2,1},{3,0},{4,7},{5,6},{6,5},{7,4},{8,11},{9,10},{10,... | collective-permute-start | bytes 98312 | tf_op jit(solution)/shard_map/ppermute | solution.py:1094
  601.4 8.3 %collective-permute-start.123 = (bf16[9,16,512]{2,1,0:T(8,128)(2,1)}, bf16[9,16,512]{2,1,0:T(8,128)(2,1)S(1)}, u32[]{:S(2)}, u32[]{:S(2)}) collective-permute-start(bf16[9,16,512]{2,1,0:T(8,128)(2,1)} %fold.18), channel_id=1, source_target_pairs={{0,1},{1,0},{2,3},{3,2},{4,5},{5,4},{6,7},{7,6},{8,9},{9,8},{10,11... | collective-permute-start | bytes 442376 | tf_op jit(solution)/shard_map/ppermute | solution.py:1094
  602.3 7.5 %collective-permute-start.124 = (bf16[9,16,512]{2,1,0:T(8,128)(2,1)}, bf16[9,16,512]{2,1,0:T(8,128)(2,1)S(1)}, u32[]{:S(2)}, u32[]{:S(2)}) collective-permute-start(bf16[9,16,512]{2,1,0:T(8,128)(2,1)} %fold.18), channel_id=1, source_target_pairs={{0,2},{1,3},{2,0},{3,1},{4,6},{5,7},{6,4},{7,5},{8,10},{9,11},{10,... | collective-permute-start | bytes 442376 | tf_op jit(solution)/shard_map/ppermute | solution.py:1094
  605.6 6.3 %collective-permute-start.125 = (bf16[9,16,512]{2,1,0:T(8,128)(2,1)}, bf16[9,16,512]{2,1,0:T(8,128)(2,1)S(1)}, u32[]{:S(2)}, u32[]{:S(2)}) collective-permute-start(bf16[9,16,512]{2,1,0:T(8,128)(2,1)} %fold.18), channel_id=1, source_target_pairs={{0,3},{1,2},{2,1},{3,0},{4,7},{5,6},{6,5},{7,4},{8,11},{9,10},{10,... | collective-permute-start | bytes 442376 | tf_op jit(solution)/shard_map/ppermute | solution.py:1094
  605.8 7.4 %collective-permute-start.126 = (bf16[512,512]{1,0:T(8,128)(2,1)}, bf16[512,512]{1,0:T(8,128)(2,1)S(1)}, u32[]{:S(2)}, u32[]{:S(2)}) collective-permute-start(bf16[512,512]{1,0:T(8,128)(2,1)} %fold.19.own_ref), channel_id=1, source_target_pairs={{0,1},{1,0},{2,3},{3,2},{4,5},{5,4},{6,7},{7,6},{8,9},{9,8},{10,11... | collective-permute-start | bytes 1572872 | tf_op jit(solution)/shard_map/ppermute | solution.py:1094
  (149 other events, 750.9 us)
Sparse Core Ops, SparseCore 0:
  11.5 106.4 all-gather.7
  121.4 69.7 all-gather.9
  194.7 82.1 all-gather.5
  386.5 76.0 reduce-scatter.2
  466.4 97.3 reduce-scatter.4

commit v4 on v3

--- a/solution.py
+++ b/solution.py
@@ -112,7 +112,7 @@
 
 
 def sigmoid(v):
-    return 1.0 / (1.0 + jnp.exp(-v))
+    return 0.5 * jnp.tanh(0.5 * v) + 0.5
 
 
 def spread(mask, width):
@@ -443,13 +443,29 @@
 
 
 def head_kernel(
-    f, devices, shard, place_ref, p_ref, digit_ref, h_ref, e_ref, affine_ref, view_ref, cells_ref,
+    f, devices, shard, place_ref, mine_ref, other_ref, h_ref, e_ref, affine_ref, view_ref, cells_ref,
     loss_ref, hidden_ref, embed_ref, gain_ref, back_ref, sums_ref,
-    hat, low, emb, grad, own, factors, pooled_grad,
+    hat, low, emb, grad, own, factors, pooled_grad, rows_ref, sems,
 ):
     step = pl.program_id(0)
     tiles = pl.num_programs(0) // 2
-    v = p_ref.shape[0]
+    p_ref = rows_ref.at[:, 0 : view_ref.shape[1]]
+    digit_ref = rows_ref.at[:, view_ref.shape[1] :]
+
+    @pl.when(step == 0)
+    def _():
+        copies = []
+        for m in range(32):
+            c, j, k = m & 1, (m >> 1) & 3, m >> 3
+            at = pl.ds(pl.multiple_of((place_ref[2] ^ m) * SLOT, SLOT), SLOT)
+            src = (other_ref if c else mine_ref).at[j, k]
+            copies.append(pltpu.make_async_copy(src, rows_ref.at[at, :], sems.at[m]))
+        for copy in copies:
+            copy.start()
+        for copy in copies:
+            copy.wait()
+
+    v = rows_ref.shape[0]
     tile = h_ref.shape[1]
     number = devices * f.views
     row_id = lax.broadcasted_iota(jnp.int32, (v, 128), 0)
@@ -559,14 +575,12 @@
 
 
 def head(f, devices, shard, place, pooled, weight, affine, view_sums, tile=512):
-    v, c = pooled.shape[0], weight.shape[0]
+    v, c = devices * SLOT, weight.shape[0]
     n, w = affine.shape[1], weight.shape[1] - affine.shape[1]
     tiles = n // tile
     cells = jnp.asarray(np.repeat(f.cells(), c, 1))
     late = lambda i: (0, jnp.maximum(i - tiles, 0))
     inputs = [
-        (pooled, (v, c), lambda i: (0, 0)),
-        (pooled, (v, 128), lambda i: (0, c // 128)),
         (weight, (c, tile), lambda i: (0, i % tiles)),
         (weight, (tile, w), lambda i: (i % tiles, n // w)),
         (affine, (2, tile), lambda i: (0, i % tiles)),
@@ -585,7 +599,7 @@
         functools.partial(head_kernel, f, devices, shard),
         name="head",
         grid=(2 * tiles,),
-        in_specs=[pl.BlockSpec(memory_space=pltpu.SMEM)] + [pl.BlockSpec(b, m) for _, b, m in inputs],
+        in_specs=[IN_SMEM, IN_PLACE, IN_PLACE] + [pl.BlockSpec(b, m) for _, b, m in inputs],
         out_specs=[pl.BlockSpec(b, m) for _, _, b, m in outputs],
         out_shape=[jax.ShapeDtypeStruct(s, d) for s, d, _, _ in outputs],
         scratch_shapes=[
@@ -596,10 +610,12 @@
             pltpu.VMEM((v, tile), BF16),
             pltpu.VMEM((tiles, 8, tile), F32),
             pltpu.VMEM((SLOT, c), F32),
+            pltpu.VMEM((v, pooled[0].shape[-1]), BF16),
+            pltpu.SemaphoreType.DMA((32,)),
         ],
         compiler_params=pltpu.CompilerParams(vmem_limit_bytes=VMEM_LIMIT),
         cost_estimate=cost(22),
-    )(place, *[a for a, _, _ in inputs])
+    )(place, *pooled, *[a for a, _, _ in inputs])
 
 
 def widen_back_kernel(
@@ -992,7 +1008,7 @@
         out_specs=[in_vmem] * len(kinds),
         out_shape=[jax.ShapeDtypeStruct(s, F32) for s in shapes],
         compiler_params=pltpu.CompilerParams(vmem_limit_bytes=VMEM_LIMIT),
-        cost_estimate=cost(2),
+        cost_estimate=cost(0.1),
     )(place, own, other)
 
 
@@ -1002,7 +1018,7 @@
         out[...] = value
 
 
-def local(function, arrays, after=(), name="local", us=2):
+def local(function, arrays, after=(), name="local", us=0.1):
     shapes = jax.eval_shape(function, *arrays)
     in_vmem = pl.BlockSpec(memory_space=pltpu.VMEM)
     kernel = functools.partial(local_kernel, function, len(arrays))
@@ -1434,7 +1450,7 @@
         pooled = jnp.concatenate([pooled, jnp.pad(digits, ((0, 0), (0, 126)))], 1)
         every = jnp.stack(links.from_each(pooled, (8, 16, 24)))
         every = jnp.stack(links.from_each(every, (2, 4, 6)))
-        every = assemble(place, every, links.across(every))
+        every = every, links.across(every)
         loss, hidden_grad, embed_grad, gains7, back, sums6 = head(
             f, links.size, shard, place, every, w_head, affine[7], view_sums
         )
@@ -1464,9 +1480,9 @@
     )
     sums.start("spatial2", patch2, rotated_back, 9, halves=True)
     sums.swap("spatial2")
-    sums4 = links.total(part4)
     first = ("expand2", "spatial2")
     first_own = sums.scatter(*first)
+    sums4 = links.total(pin(part4, first_own))
     mixing_back, block_grad, part23 = mix_back(
         f, all_out, d4, mixing, st4, affine[4], sums4, w["reduce2"], back, slopes, block_pre,
         expanded, st2, affine[2], skipped, st3, affine[3], mask, after=first_own,
@@ -1488,7 +1504,7 @@
     second_own = sums.scatter(*second)
     turned_back, d0, part0 = conv_back(
         f, 2, all_out, all_in, d1, turned, st1, affine[1], sums1, w["spatial"], reduced, st0, affine[0], mask,
-        after=second_own,
+        after=second_own + sums.state(first),
     )
     sums.start("spatial", patch1, turned_back, 9)
     sums.swap("spatial")
@@ -1501,14 +1517,14 @@
     sums.swap("reduce")
     sub = sub_back(skipped_back, w["short"], x.shape[1], after=(reduced_back,))
     grad_large, grad_small = input_back(f, reduced_back, w_reduce, sub)
-    sums.in_plane("reduce", after=sums.state("spatial") + (grad_small,))
-    sums.along_z("spatial")
+    sums.along_z("spatial", after=(grad_small,))
+    sums.in_plane("reduce", after=sums.state("spatial")[:1])
     sums.across_y(*first)
     sums.across_y(*second)
     sums.along_z("reduce")
+    sums.across_cores(*second)
+    sums.join("spatial", after=sums.state(second)[:1])
     sums.across_cores(*first)
-    sums.join("spatial", after=sums.state(first) + sums.state(second))
-    sums.across_cores(*second)
     sums.join("reduce")
     part = lambda n: n // 16
     expand2_grad, spatial2_grad = sums.split(

time: 630 us -> 625 us (level)
    unnamed x149 -> x159, local copies, waits for them, and re-layouts: 21.5 us -> 23.3 us
  transfers between devices with their start and end apart: 132 -> 132, of which waited for: 76 -> 77; matrix products, arithmetic and copies ran while one was open for 4% -> 4% of each run, Pallas kernels for 28% -> 28%
where the time goes in v4:
time: 625 us; the launch traced here: 619 us
  Pallas kernels  227 us (36%)
  waiting for transfers between devices  203 us (32%)
  starting transfers between devices  129 us (21%)
  local copies, waits for them, and re-layouts  25.4 us (4%)
  other arithmetic  19.8 us (3%)
  between operations  15 us (2%)
    ppermute x127, waiting for transfers between devices, swap(): return lax.ppermute(v, AXES, [(i, i ^ bits) for i in range(self.size)])  164 us
    ppermute x127, starting transfers between devices, swap(): return lax.ppermute(v, AXES, [(i, i ^ bits) for i in range(self.size)])  129 us
    pallas_call x17, Pallas kernels, call(): pl.pallas_call(skipping(kernel, len(inputs), len(after)), name=kernel.fun...  113 us
    pallas_call x7, Pallas kernels, weight_grad(): pl.pallas_call(functools.partial(weight_kernel, taps > 1, rows, halves),...  44.7 us
    all_gather x2, waiting for transfers between devices, fetch(): buffer = lax.all_gather(own, AXES)  39.1 us
    pallas_call x12, Pallas kernels, local(): pl.pallas_call(skipping(kernel, len(arrays), len(after)), name=name, in_s...  33.4 us
    unnamed x159, local copies, waits for them, and re-layouts  23.3 us
    pallas_call x1, Pallas kernels, head(): pl.pallas_call(functools.partial(head_kernel, f, devices, shard), name='h...  22.7 us
  transfers between devices with their start and end apart: 132, of which 77 were waited for; matrix products, arithmetic and copies ran while one was open for 4% of the time, Pallas kernels for 28%

profile of v4, /device:TPU:0, one launch (start us, length us, event | category | flops | bytes accessed | tf_op | source)
XLA Modules:
  0.0 619.3 jit_solution(1668796041643782861)
XLA Ops:
  14.3 4.9 split_kernel.1.refs_4_.refs_3_.refs_0_.left_ref
  21.2 3.1 collective-permute-start
  27.8 4.0 collective-permute-done.1.refs_2_
  38.9 3.1 collective-permute-done.3.refs_1_
  52.4 5.7 linear_kernel.2
  78.6 39.1 %all-gather.8.cloned.1.call-done = bf16[13312,512]{1,0:T(8,128)(2,1)} async-done(((bf16[416,512]{1,0:T(8,128)(2,1)}), bf16[13312,512]{1,0:T(8,128)(2,1)}) %all-gather.8.cloned.1.call-update) | async-done | bytes 13631504 | tf_op jit(solution)/shard_map/all_gather | solution.py:1232
  117.7 8.2 %conv_kernel.2 = (bf16[384,4608]{1,0:T(8,128)(2,1)}, f32[384,512]{1,0:T(8,128)}, f32[2,512]{1,0:T(2,128)}) custom-call(f32[1536,512]{1,0:T(8,128)} %get-tuple-element.96.refs_0_.refs_6_.refs_1_, f32[2,512]{1,0:T(2,128)} %pad_maximum_fusion.14.refs_1_.refs_7_.refs_2_, f32[2,512]{1,0:T(2,128)} %get-tuple-element.261.refs_2_.refs_8_.refs_3_, ...), custom_call_target="tpu_custom_call" | custom-call | bytes 28000000 | tf_op jit(solution)/shard_map/conv_kernel/pallas_call | solution.py:33
  132.3 3.1 collective-permute-done.17
  143.5 5.5 expand_kernel.2
  149.0 6.0 linear_kernel.3
  161.1 3.0 collective-permute-done.24
  174.4 7.6 %mix_kernel.1 = (bf16[384,2048]{1,0:T(8,128)(2,1)}, f32[384,2048]{1,0:T(8,128)}, f32[384,512]{1,0:T(8,128)}, f32[2,512]{1,0:T(2,128)}) custom-call(f32[384,2048]{1,0:T(8,128)} %get-tuple-element.100.exp_ref.refs_9_.refs_1_, f32[384,2048]{1,0:T(8,128)} %get-tuple-element.102.skip_ref.refs_12_.refs_4_, f32[2,2048]{1,0:T(2,128)} %get-tuple-element.268.stats_a.refs_10_.refs_2_, ...), custom_call_target="tpu_custom_call" | custom-call | bytes 28000000 | tf_op jit(solution)/shard_map/mix_kernel/pallas_call | solution.py:33
  200.1 6.4 %conv_kernel.3 = (bf16[384,4608]{1,0:T(8,128)(2,1)}, f32[384,512]{1,0:T(8,128)}, f32[2,512]{1,0:T(2,128)}) custom-call(f32[384,512]{1,0:T(8,128)} %get-tuple-element.104.pre_ref.refs_6_.refs_1_, f32[2,512]{1,0:T(2,128)} %pad_maximum_fusion.20.stats_ref.refs_7_.refs_2_, f32[2,512]{1,0:T(2,128)} %get-tuple-element.259.affine_ref.refs_8_.refs_3_, ...), custom_call_target="tpu_custom_call" | custom-call | bytes 28000000 | tf_op jit(solution)/shard_map/conv_kernel/pallas_call | solution.py:33
  211.4 3.4 collective-permute-done.38
  219.5 3.2 collective-permute-done.41
  223.3 5.8 expand_kernel.3
  243.3 4.1 collective-permute-done.48
  248.1 6.6 %pool_kernel.1 = (f32[16,2048]{1,0:T(8,128)}, f32[384,2048]{1,0:T(8,128)}, f32[32,2048]{1,0:T(8,128)}) custom-call(f32[384,2048]{1,0:T(8,128)} %get-tuple-element.108.wide_ref, f32[384,2048]{1,0:T(8,128)} %get-tuple-element.109.pre_ref.refs_8_, f32[2,2048]{1,0:T(2,128)} %pad_maximum_fusion.9.stats_ref, f32[2,2048]{1,0:T(2,128)} %get-tuple-element.257.affine_ref, ...), custom_call_target="tpu_custom_call" | custom-call | bytes 23450000 | tf_op jit(solution)/shard_map/pool_kernel/pallas_call | solution.py:33
  260.0 3.5 collective-permute-done.49
  263.5 4.3 collective-permute-done.50
  271.4 5.0 collective-permute-done.52
  283.4 22.7 %head.1 = (f32[8,128]{1,0:T(8,128)}, f32[256,2048]{1,0:T(8,128)}, f32[256,128]{1,0:T(8,128)}, f32[2,2048]{1,0:T(2,128)}, f32[16,2048]{1,0:T(8,128)}, /*index=5*/f32[2,2048]{1,0:T(2,128)}) custom-call(s32[3]{0:T(128)} %pad_add_fusion.place_ref.refs_0_, bf16[4,4,16,2176]{3,2,1,0:T(8,128)(2,1)} %copy-done.10, bf16[4,4,16,2176]{3,2,1,0:T(8,128)(2,1)} %copy-done.18, ...), custom_call_target="tpu_custom_call" | custom-call | bytes 77000000 | tf_op jit(solution)/shard_map/head/pallas_call | solution.py:598
  312.5 3.4 collective-permute-done.59
  315.9 5.8 collective-permute-start.60
  328.7 7.0 %widen_back_kernel.1 = (bf16[384,2048]{1,0:T(8,128)(2,1)}, f32[384,512]{1,0:T(8,128)}, f32[2,512]{1,0:T(2,128)}) custom-call(f32[384,2048]{1,0:T(8,128)} %get-tuple-element.108.wide_ref, f32[384,2048]{1,0:T(8,128)} %get-tuple-element.114.slope_ref.refs_7_, f32[16,2048]{1,0:T(8,128)} %get-tuple-element.115.back_ref.refs_6_, ...), custom_call_target="tpu_custom_call" | custom-call | bytes 25900000 | tf_op jit(solution)/shard_map/widen_back_kernel/pallas_call | solution.py:33
  348.4 4.8 weight_grad.7
  353.8 6.6 %conv_back_kernel.2 = (bf16[384,512]{1,0:T(8,128)(2,1)}, f32[384,512]{1,0:T(8,128)}, f32[2,512]{1,0:T(2,128)}) custom-call(f32[384,512]{1,0:T(8,128)} %get-tuple-element.117.refs_0_, f32[384,512]{1,0:T(8,128)} %get-tuple-element.106.pre_ref.turn_ref.refs_1_, f32[2,512]{1,0:T(2,128)} %pad_maximum_fusion.23.stats_ref.turn_stats.refs_2_, ...), custom_call_target="tpu_custom_call" | custom-call | bytes 25200000 | tf_op jit(solution)/shard_map/conv_back_kernel/pallas_call | solution.py:33
  360.4 9.5 %weight_grad.8 = (bf16[8,288,512]{2,1,0:T(8,128)(2,1)}, bf16[8,288,512]{2,1,0:T(8,128)(2,1)}) custom-call(s32[3]{0:T(128)} %pad_add_fusion.place_ref.refs_0_, bf16[384,4608]{1,0:T(8,128)(2,1)} %get-tuple-element.125.left_ref, bf16[384,512]{1,0:T(8,128)(2,1)} %get-tuple-element.126.right_ref), custom_call_target="tpu_custom_call" | custom-call | bytes 35000000 | tf_op jit(solution)/shard_map/weight_grad/pallas_call | solution.py:1088
  370.5 5.2 collective-permute-done.70.refs_1_
  377.6 5.6 fold.10.refs_1_.refs_16_
  398.1 3.2 collective-permute-done.78
  401.9 9.6 %mix_back_kernel.1 = (bf16[384,512]{1,0:T(8,128)(2,1)}, f32[384,2048]{1,0:T(8,128)}, f32[3,2048]{1,0:T(4,128)}) custom-call(f32[384,512]{1,0:T(8,128)} %get-tuple-element.123.refs_0_, f32[384,512]{1,0:T(8,128)} %get-tuple-element.104.pre_ref.refs_6_.refs_1_, f32[2,512]{1,0:T(2,128)} %pad_maximum_fusion.20.stats_ref.refs_7_.refs_2_, ...), custom_call_target="tpu_custom_call" | custom-call | bytes 34300000 | tf_op jit(solution)/shard_map/mix_back_kernel/pallas_call | solution.py:33
  417.8 4.3 collective-permute-done.82
  426.5 4.4 weight_grad.9
  431.5 8.5 %block_back_kernel.1 = (bf16[384,2048]{1,0:T(8,128)(2,1)}, bf16[384,2048]{1,0:T(8,128)(2,1)}, f32[384,512]{1,0:T(8,128)}, f32[2,512]{1,0:T(2,128)}) custom-call(f32[384,2048]{1,0:T(8,128)} %get-tuple-element.129.refs_0_, f32[384,2048]{1,0:T(8,128)} %get-tuple-element.100.exp_ref.refs_9_.refs_1_, f32[2,2048]{1,0:T(2,128)} %get-tuple-element.268.stats_a.refs_10_.refs_2_, ...), custom_call_target="tpu_custom_call" | custom-call | bytes 30800000 | tf_op jit(solution)/shard_map/block_back_kernel/pallas_call | solution.py:33
  440.0 6.4 %weight_grad.11 = (bf16[8,256,512]{2,1,0:T(8,128)(2,1)}, bf16[8,256,512]{2,1,0:T(8,128)(2,1)}) custom-call(s32[3]{0:T(128)} %pad_add_fusion.place_ref.refs_0_, bf16[1536,1024]{1,0:T(8,128)(2,1)} %split_kernel.1.refs_4_.refs_3_.refs_0_.left_ref, bf16[384,2048]{1,0:T(8,128)(2,1)} %get-tuple-element.141.right_ref.refs_0_), custom_call_target="tpu_custom_call" | custom-call | bytes 17500000 | tf_op jit(solution)/shard_map/weight_grad/pallas_call | solution.py:1088
  446.9 4.9 weight_grad.10
  456.4 6.5 %fold.11.refs_10_ = bf16[8,512,512]{2,1,0:T(8,128)(2,1)} custom-call(bf16[8,128,512]{2,1,0:T(8,128)(2,1)} %get-tuple-element.133.refs_13_.refs_0_, bf16[8,128,512]{2,1,0:T(8,128)(2,1)} %copy-done.20, bf16[8,128,512]{2,1,0:T(8,128)(2,1)} %get-tuple-element.139.refs_2_, bf16[8,128,512]{2,1,0:T(8,128)(2,1)} %copy-done.21, ...), custom_call_target="tpu_custom_call" | custom-call | bytes 14000000 | tf_op jit(solution)/shard_map/fold/pallas_call | solution.py:1025
  468.0 3.3 collective-permute-done.89
  479.5 7.6 %conv_back_kernel.3 = (bf16[384,512]{1,0:T(8,128)(2,1)}, f32[1536,512]{1,0:T(8,128)}, f32[2,512]{1,0:T(2,128)}) custom-call(f32[384,512]{1,0:T(8,128)} %get-tuple-element.135.refs_0_, f32[384,512]{1,0:T(8,128)} %get-tuple-element.98.pre_ref.refs_9_.refs_1_, f32[2,512]{1,0:T(2,128)} %pad_maximum_fusion.17.stats_ref.refs_10_.refs_2_, ...), custom_call_target="tpu_custom_call" | custom-call | bytes 25200000 | tf_op jit(solution)/shard_map/conv_back_kernel/pallas_call | solution.py:33
  487.2 9.6 %weight_grad.12 = (bf16[4,4,9,16,512]{4,3,2,1,0:T(8,128)(2,1)}, bf16[4,4,9,16,512]{4,3,2,1,0:T(8,128)(2,1)}) custom-call(s32[3]{0:T(128)} %pad_add_fusion.place_ref.refs_0_, bf16[384,4608]{1,0:T(8,128)(2,1)} %get-tuple-element.146.left_ref, bf16[384,512]{1,0:T(8,128)(2,1)} %get-tuple-element.147.right_ref), custom_call_target="tpu_custom_call" | custom-call | bytes 35000000 | tf_op jit(solution)/shard_map/weight_grad/pallas_call | solution.py:1088
  515.0 4.1 fold.12
  522.6 4.5 input_low_kernel.1.refs_2_.low_ref.right_ref
  527.1 5.2 weight_grad.13
  532.4 6.4 %sub_kernel.1.sub_ref = f32[384,1024]{1,0:T(8,128)} custom-call(bf16[384,2048]{1,0:T(8,128)(2,1)} %get-tuple-element.141.right_ref.refs_0_, bf16[32,416,512]{2,1,0:T(8,128)(2,1)} %bitcast.54, bf16[1536,512]{1,0:T(8,128)(2,1)} %input_low_kernel.1.refs_2_.low_ref.right_ref), custom_call_target="tpu_custom_call" | custom-call | bytes 350000 | tf_op jit(solution)/shard_map/sub_kernel/pallas_call | solution.py:33
  538.8 6.1 input_back_kernel.1
  544.9 8.3 %collective-permute-done.107.refs_3_ = bf16[4,9,16,512]{3,2,1,0:T(8,128)(2,1)S(1)} collective-permute-done((bf16[4,9,16,512]{3,2,1,0:T(8,128)(2,1)}, bf16[4,9,16,512]{3,2,1,0:T(8,128)(2,1)S(1)}, u32[]{:S(2)}, u32[]{:S(2)}) %collective-permute-start.107) | collective-permute-done | bytes 589856 | tf_op jit(solution)/shard_map/ppermute | solution.py:1110
  600.7 4.6 collective-permute-done.122
  (508 shorter events, 290.8 us)
Async XLA Ops:
  7.2 110.5 %all-gather.8.cloned.1.call-start = ((), (), s32[]{:S(2)}) async-start(), calls=%async_computation.5 | async-start | bytes 14057472 | tf_op jit(solution)/shard_map/all_gather | solution.py:1232
  10.0 190.0 %all-gather.10.cloned.1.call-start = ((), (), s32[]{:S(2)}) async-start(), calls=%async_computation.6 | async-start | bytes 7028736 | tf_op jit(solution)/shard_map/all_gather | solution.py:1232
  21.1 258.5 %all-gather.6.cloned.1.call-start = ((), (), s32[]{:S(2)}) async-start(), calls=%async_computation.2 | async-start | bytes 9191424 | tf_op jit(solution)/shard_map/all_gather | solution.py:1256
  21.2 6.6 %collective-permute-start = (bf16[32,512]{1,0:T(8,128)(2,1)S(1)}, bf16[32,512]{1,0:T(8,128)(2,1)S(1)}, u32[]{:S(2)}, u32[]{:S(2)}) collective-permute-start(bf16[32,512]{1,0:T(8,128)(2,1)S(1)} %copy-done.4), channel_id=1, source_target_pairs={{0,8},{1,9},{2,10},{3,11},{4,12},{5,13},{6,14},{7,15},{8,0},{9,1},... | collective-permute-start | bytes 98312 | tf_op jit(solution)/shard_map/ppermute | solution.py:1110
  24.3 7.5 %collective-permute-start.1 = (bf16[32,512]{1,0:T(8,128)(2,1)S(1)}, bf16[32,512]{1,0:T(8,128)(2,1)S(1)}, u32[]{:S(2)}, u32[]{:S(2)}) collective-permute-start(bf16[32,512]{1,0:T(8,128)(2,1)S(1)} %copy-done.4), channel_id=1, source_target_pairs={{0,16},{1,17},{2,18},{3,19},{4,20},{5,21},{6,22},{7,23},{8,24},{9,... | collective-permute-start | bytes 98312 | tf_op jit(solution)/shard_map/ppermute | solution.py:1110
  26.9 6.4 %collective-permute-start.2 = (bf16[32,512]{1,0:T(8,128)(2,1)S(1)}, bf16[32,512]{1,0:T(8,128)(2,1)S(1)}, u32[]{:S(2)}, u32[]{:S(2)}) collective-permute-start(bf16[32,512]{1,0:T(8,128)(2,1)S(1)} %copy-done.4), channel_id=1, source_target_pairs={{0,24},{1,25},{2,26},{3,27},{4,28},{5,29},{6,30},{7,31},{8,16},{9,... | collective-permute-start | bytes 98312 | tf_op jit(solution)/shard_map/ppermute | solution.py:1110
  35.4 6.6 %collective-permute-start.3 = (bf16[4,32,512]{2,1,0:T(8,128)(2,1)}, bf16[4,32,512]{2,1,0:T(8,128)(2,1)S(1)}, u32[]{:S(2)}, u32[]{:S(2)}) collective-permute-start(bf16[4,32,512]{2,1,0:T(8,128)(2,1)} %stack.185.refs_0_), channel_id=1, source_target_pairs={{0,2},{1,3},{2,0},{3,1},{4,6},{5,7},{6,4},{7,5},{8,10},{9,11},{10,... | collective-permute-start | bytes 393224 | tf_op jit(solution)/shard_map/ppermute | solution.py:1110
  38.2 6.1 collective-permute-start.5
  60.0 419.5 %reduce-scatter.3.cloned.1.call-start = ((), (), s32[]{:S(2)}) async-start(), calls=%async_computation.3 | async-start | bytes 3833856 | tf_op jit(solution)/shard_map/reduce_scatter | solution.py:1298
  164.4 7.8 %collective-permute-start.26 = (f32[2,4096]{1,0:T(2,128)S(1)}, f32[2,4096]{1,0:T(2,128)S(1)}, u32[]{:S(2)}, u32[]{:S(2)}) collective-permute-start(f32[2,4096]{1,0:T(2,128)S(1)} %pad_maximum_fusion.4), channel_id=1, source_target_pairs={{0,16},{1,17},{2,18},{3,19},{4,20},{5,21},{6,22},{7,23},{8,24},{9,... | collective-permute-start | bytes 98312 | tf_op jit(solution)/shard_map/ppermute | solution.py:1110
  167.3 6.4 %collective-permute-start.27 = (f32[2,4096]{1,0:T(2,128)S(1)}, f32[2,4096]{1,0:T(2,128)S(1)}, u32[]{:S(2)}, u32[]{:S(2)}) collective-permute-start(f32[2,4096]{1,0:T(2,128)S(1)} %pad_maximum_fusion.4), channel_id=1, source_target_pairs={{0,24},{1,25},{2,26},{3,27},{4,28},{5,29},{6,30},{7,31},{8,16},{9,... | collective-permute-start | bytes 98312 | tf_op jit(solution)/shard_map/ppermute | solution.py:1110
  255.6 7.9 %collective-permute-start.49 = (bf16[16,2176]{1,0:T(8,128)(2,1)S(1)}, bf16[16,2176]{1,0:T(8,128)(2,1)S(1)}, u32[]{:S(2)}, u32[]{:S(2)}) collective-permute-start(bf16[16,2176]{1,0:T(8,128)(2,1)S(1)} %get-tuple-element.263), channel_id=1, source_target_pairs={{0,8},{1,9},{2,10},{3,11},{4,12},{5,13},{6,14},{7,15},{8,0},{9,1},... | collective-permute-start | bytes 208904 | tf_op jit(solution)/shard_map/ppermute | solution.py:1110
  255.7 12.1 %collective-permute-start.50 = (bf16[16,2176]{1,0:T(8,128)(2,1)S(1)}, bf16[16,2176]{1,0:T(8,128)(2,1)S(1)}, u32[]{:S(2)}, u32[]{:S(2)}) collective-permute-start(bf16[16,2176]{1,0:T(8,128)(2,1)S(1)} %get-tuple-element.263), channel_id=1, source_target_pairs={{0,16},{1,17},{2,18},{3,19},{4,20},{5,21},{6,22},{7,23},{8,24},{9,... | collective-permute-start | bytes 208904 | tf_op jit(solution)/shard_map/ppermute | solution.py:1110
  257.8 10.0 %collective-permute-start.51 = (bf16[16,2176]{1,0:T(8,128)(2,1)S(1)}, bf16[16,2176]{1,0:T(8,128)(2,1)S(1)}, u32[]{:S(2)}, u32[]{:S(2)}) collective-permute-start(bf16[16,2176]{1,0:T(8,128)(2,1)S(1)} %get-tuple-element.263), channel_id=1, source_target_pairs={{0,24},{1,25},{2,26},{3,27},{4,28},{5,29},{6,30},{7,31},{8,16},{9,... | collective-permute-start | bytes 208904 | tf_op jit(solution)/shard_map/ppermute | solution.py:1110
  267.8 8.6 %collective-permute-start.52 = (bf16[4,16,2176]{2,1,0:T(8,128)(2,1)S(1)}, bf16[4,16,2176]{2,1,0:T(8,128)(2,1)S(1)}, u32[]{:S(2)}, u32[]{:S(2)}) collective-permute-start(bf16[4,16,2176]{2,1,0:T(8,128)(2,1)S(1)} %get-tuple-element.249), channel_id=1, source_target_pairs={{0,2},{1,3},{2,0},{3,1},{4,6},{5,7},{6,4},{7,5},{8,10},{9,11},{10,... | collective-permute-start | bytes 835592 | tf_op jit(solution)/shard_map/ppermute | solution.py:1110
  269.2 7.4 %collective-permute-start.53 = (bf16[4,16,2176]{2,1,0:T(8,128)(2,1)S(1)}, bf16[4,16,2176]{2,1,0:T(8,128)(2,1)S(1)}, u32[]{:S(2)}, u32[]{:S(2)}) collective-permute-start(bf16[4,16,2176]{2,1,0:T(8,128)(2,1)S(1)} %get-tuple-element.249), channel_id=1, source_target_pairs={{0,4},{1,5},{2,6},{3,7},{4,0},{5,1},{6,2},{7,3},{8,12},{9,13},{10,... | collective-permute-start | bytes 835592 | tf_op jit(solution)/shard_map/ppermute | solution.py:1110
  269.3 10.1 %collective-permute-start.54 = (bf16[4,16,2176]{2,1,0:T(8,128)(2,1)S(1)}, bf16[4,16,2176]{2,1,0:T(8,128)(2,1)S(1)}, u32[]{:S(2)}, u32[]{:S(2)}) collective-permute-start(bf16[4,16,2176]{2,1,0:T(8,128)(2,1)S(1)} %get-tuple-element.249), channel_id=1, source_target_pairs={{0,6},{1,7},{2,4},{3,5},{4,2},{5,3},{6,0},{7,1},{8,14},{9,15},{10,... | collective-permute-start | bytes 835592 | tf_op jit(solution)/shard_map/ppermute | solution.py:1110
  315.9 8.2 %collective-permute-start.60 = (f32[2,2048]{1,0:T(2,128)S(1)}, f32[2,2048]{1,0:T(2,128)S(1)}, u32[]{:S(2)}, u32[]{:S(2)}) collective-permute-start(f32[2,2048]{1,0:T(2,128)S(1)} %add.1109), channel_id=1, source_target_pairs={{0,8},{1,9},{2,10},{3,11},{4,12},{5,13},{6,14},{7,15},{8,0},{9,1},... | collective-permute-start | bytes 49160 | tf_op jit(solution)/shard_map/ppermute | solution.py:1110
  344.0 9.2 %collective-permute-start.67 = (f32[2,512]{1,0:T(2,128)S(1)}, f32[2,512]{1,0:T(2,128)S(1)}, u32[]{:S(2)}, u32[]{:S(2)}) collective-permute-start(f32[2,512]{1,0:T(2,128)S(1)} %add.1116), channel_id=1, source_target_pairs={{0,8},{1,9},{2,10},{3,11},{4,12},{5,13},{6,14},{7,15},{8,0},{9,1},... | collective-permute-start | bytes 12296 | tf_op jit(solution)/shard_map/ppermute | solution.py:1110
  344.2 9.0 %collective-permute-start.68 = (f32[2,512]{1,0:T(2,128)S(1)}, f32[2,512]{1,0:T(2,128)S(1)}, u32[]{:S(2)}, u32[]{:S(2)}) collective-permute-start(f32[2,512]{1,0:T(2,128)S(1)} %add.1116), channel_id=1, source_target_pairs={{0,16},{1,17},{2,18},{3,19},{4,20},{5,21},{6,22},{7,23},{8,24},{9,... | collective-permute-start | bytes 12296 | tf_op jit(solution)/shard_map/ppermute | solution.py:1110
  347.0 6.2 collective-permute-start.69
  369.9 6.2 %collective-permute-start.71 = (bf16[8,288,512]{2,1,0:T(8,128)(2,1)}, bf16[8,288,512]{2,1,0:T(8,128)(2,1)S(1)}, u32[]{:S(2)}, u32[]{:S(2)}) collective-permute-start(bf16[8,288,512]{2,1,0:T(8,128)(2,1)} %get-tuple-element.128), channel_id=1, source_target_pairs={{0,1},{1,0},{2,3},{3,2},{4,5},{5,4},{6,7},{7,6},{8,9},{9,8},{10,11... | collective-permute-start | bytes 7077896 | tf_op jit(solution)/shard_map/ppermute | solution.py:1110
  383.2 179.8 %reduce-scatter.5.cloned.1.call-start = ((), (), s32[]{:S(2)}) async-start(), calls=%async_computation.4 | async-start | bytes 4718592 | tf_op jit(solution)/shard_map/reduce_scatter | solution.py:1298
  422.1 8.8 %collective-permute-start.83 = (f32[3,2048]{1,0:T(4,128)S(1)}, f32[3,2048]{1,0:T(4,128)S(1)}, u32[]{:S(2)}, u32[]{:S(2)}) collective-permute-start(f32[3,2048]{1,0:T(4,128)S(1)} %add.1130), channel_id=1, source_target_pairs={{0,8},{1,9},{2,10},{3,11},{4,12},{5,13},{6,14},{7,15},{8,0},{9,1},... | collective-permute-start | bytes 73736 | tf_op jit(solution)/shard_map/ppermute | solution.py:1110
  422.1 8.7 %collective-permute-start.84 = (f32[3,2048]{1,0:T(4,128)S(1)}, f32[3,2048]{1,0:T(4,128)S(1)}, u32[]{:S(2)}, u32[]{:S(2)}) collective-permute-start(f32[3,2048]{1,0:T(4,128)S(1)} %add.1130), channel_id=1, source_target_pairs={{0,16},{1,17},{2,18},{3,19},{4,20},{5,21},{6,22},{7,23},{8,24},{9,... | collective-permute-start | bytes 73736 | tf_op jit(solution)/shard_map/ppermute | solution.py:1110
  424.1 6.8 %collective-permute-start.85 = (f32[3,2048]{1,0:T(4,128)S(1)}, f32[3,2048]{1,0:T(4,128)S(1)}, u32[]{:S(2)}, u32[]{:S(2)}) collective-permute-start(f32[3,2048]{1,0:T(4,128)S(1)} %add.1130), channel_id=1, source_target_pairs={{0,24},{1,25},{2,26},{3,27},{4,28},{5,29},{6,30},{7,31},{8,16},{9,... | collective-permute-start | bytes 73736 | tf_op jit(solution)/shard_map/ppermute | solution.py:1110
  446.4 8.3 %collective-permute-start.95 = (bf16[8,256,512]{2,1,0:T(8,128)(2,1)}, bf16[8,256,512]{2,1,0:T(8,128)(2,1)S(1)}, u32[]{:S(2)}, u32[]{:S(2)}) collective-permute-start(bf16[8,256,512]{2,1,0:T(8,128)(2,1)} %get-tuple-element.143), channel_id=1, source_target_pairs={{0,1},{1,0},{2,3},{3,2},{4,5},{5,4},{6,7},{7,6},{8,9},{9,8},{10,11... | collective-permute-start | bytes 6291464 | tf_op jit(solution)/shard_map/ppermute | solution.py:1110
  496.8 16.8 %collective-permute-start.103 = (bf16[4,4,9,16,512]{4,3,2,1,0:T(8,128)(2,1)}, bf16[4,4,9,16,512]{4,3,2,1,0:T(8,128)(2,1)S(1)}, u32[]{:S(2)}, u32[]{:S(2)}) collective-permute-start(bf16[4,4,9,16,512]{4,3,2,1,0:T(8,128)(2,1)} %get-tuple-element.149), channel_id=1, source_target_pairs={{0,1},{1,0},{2,3},{3,2},{4,5},{5,4},{6,7},{7,6},{8,9},{9,8},{10,11... | collective-permute-start | bytes 7077896 | tf_op jit(solution)/shard_map/ppermute | solution.py:1110
  509.5 54.0 %collective-permute-start.125 = (bf16[416,512]{1,0:T(8,128)(2,1)S(1)}, bf16[416,512]{1,0:T(8,128)(2,1)S(1)}, u32[]{:S(2)}, u32[]{:S(2)}) collective-permute-start(bf16[416,512]{1,0:T(8,128)(2,1)S(1)} %bitcast.61), channel_id=1, source_target_pairs={{0,2},{1,3},{2,0},{3,1},{4,6},{5,7},{6,4},{7,5},{8,10},{9,11},{10,... | collective-permute-start | bytes 1277960 | tf_op jit(solution)/shard_map/ppermute | solution.py:1110
  519.1 25.8 %collective-permute-start.105 = (bf16[4,9,16,512]{3,2,1,0:T(8,128)(2,1)}, bf16[4,9,16,512]{3,2,1,0:T(8,128)(2,1)S(1)}, u32[]{:S(2)}, u32[]{:S(2)}) collective-permute-start(bf16[4,9,16,512]{3,2,1,0:T(8,128)(2,1)} %get-tuple-element.155), channel_id=1, source_target_pairs={{0,2},{1,3},{2,0},{3,1},{4,6},{5,7},{6,4},{7,5},{8,10},{9,11},{10,... | collective-permute-start | bytes 1769480 | tf_op jit(solution)/shard_map/ppermute | solution.py:1110
  520.3 24.6 %collective-permute-start.106 = (bf16[4,9,16,512]{3,2,1,0:T(8,128)(2,1)}, bf16[4,9,16,512]{3,2,1,0:T(8,128)(2,1)S(1)}, u32[]{:S(2)}, u32[]{:S(2)}) collective-permute-start(bf16[4,9,16,512]{3,2,1,0:T(8,128)(2,1)} %get-tuple-element.156), channel_id=1, source_target_pairs={{0,4},{1,5},{2,6},{3,7},{4,0},{5,1},{6,2},{7,3},{8,12},{9,13},{10,... | collective-permute-start | bytes 1769480 | tf_op jit(solution)/shard_map/ppermute | solution.py:1110
  520.3 32.9 %collective-permute-start.107 = (bf16[4,9,16,512]{3,2,1,0:T(8,128)(2,1)}, bf16[4,9,16,512]{3,2,1,0:T(8,128)(2,1)S(1)}, u32[]{:S(2)}, u32[]{:S(2)}) collective-permute-start(bf16[4,9,16,512]{3,2,1,0:T(8,128)(2,1)} %get-tuple-element.157), channel_id=1, source_target_pairs={{0,6},{1,7},{2,4},{3,5},{4,2},{5,3},{6,0},{7,1},{8,14},{9,15},{10,... | collective-permute-start | bytes 1769480 | tf_op jit(solution)/shard_map/ppermute | solution.py:1110
  532.3 24.3 %collective-permute-start.104 = (bf16[4,4,32,512]{3,2,1,0:T(8,128)(2,1)}, bf16[4,4,32,512]{3,2,1,0:T(8,128)(2,1)S(1)}, u32[]{:S(2)}, u32[]{:S(2)}) collective-permute-start(bf16[4,4,32,512]{3,2,1,0:T(8,128)(2,1)} %get-tuple-element.154), channel_id=1, source_target_pairs={{0,1},{1,0},{2,3},{3,2},{4,5},{5,4},{6,7},{7,6},{8,9},{9,8},{10,11... | collective-permute-start | bytes 1572872 | tf_op jit(solution)/shard_map/ppermute | solution.py:1110
  559.5 9.3 %collective-permute-start.108 = (bf16[4,32,512]{2,1,0:T(8,128)(2,1)}, bf16[4,32,512]{2,1,0:T(8,128)(2,1)S(1)}, u32[]{:S(2)}, u32[]{:S(2)}) collective-permute-start(bf16[4,32,512]{2,1,0:T(8,128)(2,1)} %get-tuple-element.160), channel_id=1, source_target_pairs={{0,2},{1,3},{2,0},{3,1},{4,6},{5,7},{6,4},{7,5},{8,10},{9,11},{10,... | collective-permute-start | bytes 393224 | tf_op jit(solution)/shard_map/ppermute | solution.py:1110
  560.0 8.8 %collective-permute-start.109 = (bf16[4,32,512]{2,1,0:T(8,128)(2,1)}, bf16[4,32,512]{2,1,0:T(8,128)(2,1)S(1)}, u32[]{:S(2)}, u32[]{:S(2)}) collective-permute-start(bf16[4,32,512]{2,1,0:T(8,128)(2,1)} %get-tuple-element.161), channel_id=1, source_target_pairs={{0,4},{1,5},{2,6},{3,7},{4,0},{5,1},{6,2},{7,3},{8,12},{9,13},{10,... | collective-permute-start | bytes 393224 | tf_op jit(solution)/shard_map/ppermute | solution.py:1110
  561.5 7.3 %collective-permute-start.110 = (bf16[4,32,512]{2,1,0:T(8,128)(2,1)}, bf16[4,32,512]{2,1,0:T(8,128)(2,1)S(1)}, u32[]{:S(2)}, u32[]{:S(2)}) collective-permute-start(bf16[4,32,512]{2,1,0:T(8,128)(2,1)} %get-tuple-element.162), channel_id=1, source_target_pairs={{0,6},{1,7},{2,4},{3,5},{4,2},{5,3},{6,0},{7,1},{8,14},{9,15},{10,... | collective-permute-start | bytes 393224 | tf_op jit(solution)/shard_map/ppermute | solution.py:1110
  563.0 23.2 %collective-permute-start.120 = (bf16[512,512]{1,0:T(8,128)(2,1)}, bf16[512,512]{1,0:T(8,128)(2,1)S(1)}, u32[]{:S(2)}, u32[]{:S(2)}) collective-permute-start(bf16[512,512]{1,0:T(8,128)(2,1)} %bitcast.68), channel_id=1, source_target_pairs={{0,2},{1,3},{2,0},{3,1},{4,6},{5,7},{6,4},{7,5},{8,10},{9,11},{10,... | collective-permute-start | bytes 1572872 | tf_op jit(solution)/shard_map/ppermute | solution.py:1110
  566.2 18.5 %collective-permute-start.126 = (bf16[416,512]{1,0:T(8,128)(2,1)}, bf16[416,512]{1,0:T(8,128)(2,1)S(1)}, u32[]{:S(2)}, u32[]{:S(2)}) collective-permute-start(bf16[416,512]{1,0:T(8,128)(2,1)} %fold.19.own_ref), channel_id=1, source_target_pairs={{0,1},{1,0},{2,3},{3,2},{4,5},{5,4},{6,7},{7,6},{8,9},{9,8},{10,11... | collective-permute-start | bytes 1277960 | tf_op jit(solution)/shard_map/ppermute | solution.py:1110
  571.6 13.2 %collective-permute-start.117 = (bf16[9,16,512]{2,1,0:T(8,128)(2,1)S(1)}, bf16[9,16,512]{2,1,0:T(8,128)(2,1)S(1)}, u32[]{:S(2)}, u32[]{:S(2)}) collective-permute-start(bf16[9,16,512]{2,1,0:T(8,128)(2,1)S(1)} %copy-done.67), channel_id=1, source_target_pairs={{0,8},{1,9},{2,10},{3,11},{4,12},{5,13},{6,14},{7,15},{8,0},{9,1},... | collective-permute-start | bytes 442376 | tf_op jit(solution)/shard_map/ppermute | solution.py:1110
  575.4 5.9 collective-permute-start.113
  578.5 16.4 %collective-permute-start.118 = (bf16[9,16,512]{2,1,0:T(8,128)(2,1)S(1)}, bf16[9,16,512]{2,1,0:T(8,128)(2,1)S(1)}, u32[]{:S(2)}, u32[]{:S(2)}) collective-permute-start(bf16[9,16,512]{2,1,0:T(8,128)(2,1)S(1)} %copy-done.66), channel_id=1, source_target_pairs={{0,16},{1,17},{2,18},{3,19},{4,20},{5,21},{6,22},{7,23},{8,24},{9,... | collective-permute-start | bytes 442376 | tf_op jit(solution)/shard_map/ppermute | solution.py:1110
  581.3 14.0 %collective-permute-start.119 = (bf16[9,16,512]{2,1,0:T(8,128)(2,1)S(1)}, bf16[9,16,512]{2,1,0:T(8,128)(2,1)S(1)}, u32[]{:S(2)}, u32[]{:S(2)}) collective-permute-start(bf16[9,16,512]{2,1,0:T(8,128)(2,1)S(1)} %copy-done.65), channel_id=1, source_target_pairs={{0,24},{1,25},{2,26},{3,27},{4,28},{5,29},{6,30},{7,31},{8,16},{9,... | collective-permute-start | bytes 442376 | tf_op jit(solution)/shard_map/ppermute | solution.py:1110
  584.8 13.7 %collective-permute-start.114 = (bf16[32,512]{1,0:T(8,128)(2,1)}, bf16[32,512]{1,0:T(8,128)(2,1)S(1)}, u32[]{:S(2)}, u32[]{:S(2)}) collective-permute-start(bf16[32,512]{1,0:T(8,128)(2,1)} %fold.16), channel_id=1, source_target_pairs={{0,1},{1,0},{2,3},{3,2},{4,5},{5,4},{6,7},{7,6},{8,9},{9,8},{10,11... | collective-permute-start | bytes 98312 | tf_op jit(solution)/shard_map/ppermute | solution.py:1110
  584.8 14.9 %collective-permute-start.115 = (bf16[32,512]{1,0:T(8,128)(2,1)}, bf16[32,512]{1,0:T(8,128)(2,1)S(1)}, u32[]{:S(2)}, u32[]{:S(2)}) collective-permute-start(bf16[32,512]{1,0:T(8,128)(2,1)} %fold.16), channel_id=1, source_target_pairs={{0,2},{1,3},{2,0},{3,1},{4,6},{5,7},{6,4},{7,5},{8,10},{9,11},{10,... | collective-permute-start | bytes 98312 | tf_op jit(solution)/shard_map/ppermute | solution.py:1110
  586.1 13.9 %collective-permute-start.116 = (bf16[32,512]{1,0:T(8,128)(2,1)}, bf16[32,512]{1,0:T(8,128)(2,1)S(1)}, u32[]{:S(2)}, u32[]{:S(2)}) collective-permute-start(bf16[32,512]{1,0:T(8,128)(2,1)} %fold.16), channel_id=1, source_target_pairs={{0,3},{1,2},{2,1},{3,0},{4,7},{5,6},{6,5},{7,4},{8,11},{9,10},{10,... | collective-permute-start | bytes 98312 | tf_op jit(solution)/shard_map/ppermute | solution.py:1110
  594.9 14.2 %collective-permute-start.124 = (bf16[512,512]{1,0:T(8,128)(2,1)}, bf16[512,512]{1,0:T(8,128)(2,1)S(1)}, u32[]{:S(2)}, u32[]{:S(2)}) collective-permute-start(bf16[512,512]{1,0:T(8,128)(2,1)} %fold.17.refs_4_.own_ref), channel_id=1, source_target_pairs={{0,1},{1,0},{2,3},{3,2},{4,5},{5,4},{6,7},{7,6},{8,9},{9,8},{10,11... | collective-permute-start | bytes 1572872 | tf_op jit(solution)/shard_map/ppermute | solution.py:1110
  598.5 6.9 %collective-permute-start.122 = (bf16[9,16,512]{2,1,0:T(8,128)(2,1)}, bf16[9,16,512]{2,1,0:T(8,128)(2,1)S(1)}, u32[]{:S(2)}, u32[]{:S(2)}) collective-permute-start(bf16[9,16,512]{2,1,0:T(8,128)(2,1)} %fold.18), channel_id=1, source_target_pairs={{0,2},{1,3},{2,0},{3,1},{4,6},{5,7},{6,4},{7,5},{8,10},{9,11},{10,... | collective-permute-start | bytes 442376 | tf_op jit(solution)/shard_map/ppermute | solution.py:1110
  599.7 7.3 %collective-permute-start.123 = (bf16[9,16,512]{2,1,0:T(8,128)(2,1)}, bf16[9,16,512]{2,1,0:T(8,128)(2,1)S(1)}, u32[]{:S(2)}, u32[]{:S(2)}) collective-permute-start(bf16[9,16,512]{2,1,0:T(8,128)(2,1)} %fold.18), channel_id=1, source_target_pairs={{0,3},{1,2},{2,1},{3,0},{4,7},{5,6},{6,5},{7,4},{8,11},{9,10},{10,... | collective-permute-start | bytes 442376 | tf_op jit(solution)/shard_map/ppermute | solution.py:1110
  (154 other events, 835.7 us)
Sparse Core Ops, SparseCore 0:
  11.5 106.1 all-gather.7
  121.1 69.7 all-gather.9
  194.4 82.7 all-gather.5
  383.3 76.6 reduce-scatter.2
  463.9 96.7 reduce-scatter.4
